TPU v7x, 32 devices: a whole 2x2x4 slice. The times are simulated.
32 devices in a mesh: gx: 16 (over z, y, core), gy: 2 (over x).
Axes of the slice: x: 2, y: 2, z: 4, core: 2. Of those that a mesh axis runs over, the one named last changes fastest.
Arguments:
- control: bfloat16 [2048, 8, 2048], P('gx', None, 'gy'), may hold values from -6 to 6
- innovation: float32 [2048, 8, 2048], P('gx', None, 'gy'), may hold values from -6 to 6
- obs_weight: float32 [2048, 8, 2048], P('gx', None, 'gy'), may hold values from 0.5 to 4
- courant_x: float32 [2048, 8, 2048], P('gx', None, 'gy'), may hold values from -0.9 to 0.9
- courant_y: float32 [2048, 8, 2048], P('gx', None, 'gy'), may hold values from -0.9 to 0.9
- filter_x: bfloat16 [2048, 2048], P('gx'), may hold values from -3 to 3
- filter_y: bfloat16 [2048, 2048], P('gy'), may hold values from -3 to 3
Outputs:
- end_state: float32 [2048, 8, 2048], P('gx', None, 'gy')
- gradient: float32 [2048, 8, 2048], P('gx', None, 'gy')
All inputs are finite; a program needn't handle non-finite values.
Results may differ from a plain program's by a relative error of at most 0.0029.
Values may be sent and summed in bfloat16 or wider, within the bound.
No kernel may reach another device: no remote copies, remote signals or barrier semaphores. Data moves between devices by JAX's collectives and lax.ppermute only.
A program may use at most 192 MiB of HBM per device.

v0:
```python
import jax
import jax.numpy as jnp
from jax import lax
from jax.sharding import PartitionSpec as P


def extended(array, sides, width):
    for axis, dim in sides:
        size, length = (lax.axis_size(axis), array.shape[dim])
        up = [(i, (i + 1) % size) for i in range(size - 1)]
        down = [(j, i) for i, j in up]
        last = lax.slice_in_dim(array, length - width, length, axis=dim)
        initial = lax.slice_in_dim(array, 0, width, axis=dim)
        before = lax.ppermute(last, axis, up)
        after = lax.ppermute(initial, axis, down)
        array = jnp.concatenate([before, array, after], axis=dim)
    return array


def per_device(control, innovation, obs_weight, courant_x, courant_y, filter_x, filter_y):
    columns = filter_x
    smoothed = jnp.einsum(
        "ij,jlc->ilc",
        columns,
        lax.all_gather(control, "gx", axis=0, tiled=True),
        preferred_element_type=jnp.float32,
    ).astype(jnp.bfloat16)
    columns = filter_y
    start_state = jnp.einsum(
        "kc,xlc->xlk",
        columns,
        lax.all_gather(smoothed, "gy", axis=2, tiled=True),
        preferred_element_type=jnp.float32,
    )
    padded = extended(start_state, (("gx", 0), ("gy", 2)), 1)
    end_state = (
        start_state
        - courant_x * (padded[2:, :, 1:-1] - padded[:-2, :, 1:-1]) * 0.5
        - courant_y * (padded[1:-1, :, 2:] - padded[1:-1, :, :-2]) * 0.5
    )
    misfit = obs_weight * (end_state - innovation)
    fluxes = jnp.stack([courant_x * misfit, courant_y * misfit])
    rim_cells = extended(fluxes, (("gx", 1), ("gy", 3)), 1)
    adjoint = (
        misfit
        + 0.5 * (rim_cells[0, 2:, :, 1:-1] - rim_cells[0, :-2, :, 1:-1])
        + 0.5 * (rim_cells[1, 1:-1, :, 2:] - rim_cells[1, 1:-1, :, :-2])
    ).astype(jnp.bfloat16)
    partial_sums = jnp.einsum("kc,xlk->xlc", filter_y, adjoint, preferred_element_type=jnp.float32)
    pulled = lax.psum_scatter(partial_sums, "gy", scatter_dimension=2, tiled=True).astype(
        jnp.bfloat16
    )
    columns = filter_x
    carried = lax.psum_scatter(
        jnp.einsum("ij,ilc->jlc", columns, pulled, preferred_element_type=jnp.float32),
        "gx",
        scatter_dimension=0,
        tiled=True,
    )
    gradient = control.astype(jnp.float32) + carried
    return (end_state, gradient)


def solution(mesh):
    placed = (
        P("gx", None, "gy"),
        P("gx", None, "gy"),
        P("gx", None, "gy"),
        P("gx", None, "gy"),
        P("gx", None, "gy"),
        P("gx", None),
        P("gy", None),
    )
    return jax.shard_map(
        per_device,
        mesh=mesh,
        in_specs=placed,
        out_specs=(P("gx", None, "gy"), P("gx", None, "gy")),
        check_vma=False,
    )
```

profile of v0, /device:TPU:9, one launch (start us, length us, event | category | flops | bytes accessed | tf_op | source)
XLA Modules:
  0.0 1149.4 jit_solution(17449561173813376823)
XLA Ops:
  7.2 0.0 copy-start
  7.2 0.0 all-gather.3.cloned.1.call-start
  7.2 0.7 all-gather.3.cloned.1.call-update
  7.9 0.0 all-gather.5.cloned.1.call-start
  8.0 171.3 %all-gather.3.cloned.1.call-done = bf16[2048,8,1024]{2,1,0:T(8,128)(2,1)} async-done(((bf16[128,8,1024]{2,1,0:T(8,128)(2,1)}), bf16[2048,8,1024]{2,1,0:T(8,128)(2,1)}) %all-gather.3.cloned.1.call-update) | async-done | bytes 33554448 | tf_op jit(solution)/shard_map/all_gather | solution.py:25
  179.3 40.2 %fusion.25 = bf16[128,8,1024]{2,0,1:T(8,128)(2,1)} fusion(bf16[2048,8,1024]{2,1,0:T(8,128)(2,1)} %all-gather.3.cloned.1.call-done, bf16[128,2048]{1,0:T(8,128)(2,1)S(1)} %copy-done), kind=kOutput, calls=%fused_computation.50 | convolution fusion | flops 4296015872 | bytes 36175872 | tf_op jit(solution)/shard_map/ij,jlc->ilc/dot_general | solution.py:22
  219.5 0.0 all-gather.5.cloned.1.call-update
  219.5 0.0 reduce-scatter.3.cloned.1.call-start
  219.6 56.4 %all-gather.5.cloned.1.call-done = bf16[128,8,2048]{2,0,1:T(8,128)(2,1)} async-done(((bf16[128,8,1024]{2,0,1:T(8,128)(2,1)}), bf16[128,8,2048]{2,0,1:T(8,128)(2,1)}) %all-gather.5.cloned.1.call-update) | async-done | bytes 4194320 | tf_op jit(solution)/shard_map/all_gather | solution.py:32
  276.0 7.6 fusion.21
  283.6 0.0 copy-start.3
  283.6 0.1 fusion.33
  283.7 2.6 collective-permute-start
  286.3 3.0 collective-permute-start.1
  289.3 1.0 collective-permute-done.1
  290.3 0.2 pad_maximum_fusion.26
  290.5 0.3 copy.21
  290.8 2.2 collective-permute-start.3
  293.0 0.3 copy.19
  293.4 1.3 collective-permute-start.2
  294.7 0.2 copy.22
  294.9 2.8 collective-permute-done.2
  297.8 0.2 copy.20
  298.0 29.1 %multiply_bitcast_fusion.1 = (f32[1,128,8,1024]{3,1,2,0:T(8,128)}, f32[128,8,1024]{2,0,1:T(8,128)}, f32[128,8,1024]{2,0,1:T(8,128)}) fusion(f32[128,8,1024]{2,1,0:T(8,128)} %param.10, f32[128,8,1024]{2,1,0:T(8,128)} %param.8, f32[128,8,1024]{2,1,0:T(8,128)} %param.9, f32[1,8,1024]{2,0,1:T(1,128)S(1)} %collective-permute-done, f32[128,8,1024]{2,0,1:T(8,128)} %copy-done.3, ...), kind=kLoop, calls=%fused_computation.47 | loop fusion | flops 19922944 | bytes 33628288 | tf_op jit(solution)/shard_map/stack | solution.py:42
  327.2 6.3 multiply_bitcast_fusion
  333.5 0.1 pad_maximum_fusion.27
  333.6 6.4 collective-permute-start.4
  339.9 1.9 collective-permute-start.5
  341.9 1.3 collective-permute-done.5
  343.2 0.5 pad_maximum_fusion.23
  343.7 0.6 copy.31
  344.3 1.4 collective-permute-start.7
  345.6 0.6 copy.29
  346.2 1.3 collective-permute-start.6
  347.6 0.4 copy.32
  348.0 2.7 collective-permute-done.6
  350.7 0.4 copy.30
  351.2 17.1 %fusion.19 = f32[128,8,2048]{0,2,1:T(8,128)} fusion(bf16[1024,2048]{1,0:T(8,128)(2,1)} %param.13, f32[2,130,8,1]{3,1,2,0:T(8,128)S(1)} %copy.32, f32[2,1,8,1024]{3,1,2,0:T(1,128)S(1)} %collective-permute-done.4, f32[2,1,8,1024]{3,1,2,0:T(1,128)S(1)} %collective-permute-done.5, f32[1,128,8,1024]{3,1,2,0:T(8,128)} %copy-done.2, ...), kind=kOutput, calls=%fused_computation.40 | convolution fusion | flops 4314890240 | bytes 25313536 | tf_op jit(solution)/shard_map/kc,xlk->xlc/dot_general | solution.py:49
  368.3 0.0 reduce-scatter.3.cloned.1.call-update
  368.3 0.0 reduce-scatter.5.cloned.1.call-start
  368.3 102.5 %reduce-scatter.3.cloned.1.call-done = f32[128,8,1024]{0,2,1:T(8,128)} async-done(((f32[128,8,2048]{0,2,1:T(8,128)}), f32[128,8,1024]{0,2,1:T(8,128)}) %reduce-scatter.3.cloned.1.call-update) | async-done | bytes 4194320 | tf_op jit(solution)/shard_map/reduce_scatter | solution.py:50
  470.8 25.5 %convolution_bitcast_fusion = f32[2048,8,1024]{0,2,1:T(8,128)} fusion(f32[128,8,1024]{0,2,1:T(8,128)} %reduce-scatter.3.cloned.1.call-done, bf16[128,2048]{1,0:T(8,128)(2,1)S(1)} %copy-done), kind=kOutput, calls=%fused_computation.2 | convolution fusion | flops 4296015872 | bytes 71827456 | tf_op jit(solution)/shard_map/ij,ilc->jlc/dot_general | solution.py:55
  496.3 0.0 reduce-scatter.5.cloned.1.call-update
  496.3 3.3 copy.24
  499.6 7.1 copy.33
  506.7 626.1 %reduce-scatter.5.cloned.1.call-done = f32[128,8,1024]{0,2,1:T(8,128)} async-done(((f32[2048,8,1024]{0,2,1:T(8,128)}), f32[128,8,1024]{0,2,1:T(8,128)}) %reduce-scatter.5.cloned.1.call-update) | async-done | bytes 4194320 | tf_op jit(solution)/shard_map/reduce_scatter | solution.py:54
  1132.8 4.5 convert_add_fusion
  1137.2 5.4 copy.34
  (10 shorter events, 0.0 us)
Async XLA Ops:
  7.2 172.1 %copy-start = (bf16[128,2048]{1,0:T(8,128)(2,1)S(1)}, bf16[128,2048]{1,0:T(8,128)(2,1)}, u32[]{:S(2)}) copy-start(bf16[128,2048]{1,0:T(8,128)(2,1)} %param.12) | copy-start | bytes 1572868
  7.2 172.1 %all-gather.3.cloned.1.call-start = ((), (), s32[]{:S(2)}) async-start(), calls=%async_computation.2 | async-start | bytes 35651584 | tf_op jit(solution)/shard_map/all_gather | solution.py:25
  7.9 268.1 %all-gather.5.cloned.1.call-start = ((), (), s32[]{:S(2)}) async-start(), calls=%async_computation.3 | async-start | bytes 6291456 | tf_op jit(solution)/shard_map/all_gather | solution.py:32
  219.5 251.3 %reduce-scatter.3.cloned.1.call-start = ((), (), s32[]{:S(2)}) async-start(), calls=%async_computation.4 | async-start | bytes 12582912 | tf_op jit(solution)/shard_map/reduce_scatter | solution.py:50
  283.6 6.7 copy-start.3
  283.7 5.6 collective-permute-start
  286.3 4.0 collective-permute-start.1
  290.8 3.8 collective-permute-start.3
  293.4 4.4 collective-permute-start.2
  327.2 6.3 copy-start.1
  333.5 9.7 copy-start.2
  333.6 8.3 collective-permute-start.4
  339.9 3.2 collective-permute-start.5
  344.3 3.3 collective-permute-start.7
  346.2 4.5 collective-permute-start.6
  368.3 764.5 %reduce-scatter.5.cloned.1.call-start = ((), (), s32[]{:S(2)}) async-start(), calls=%async_computation.5 | async-start | bytes 71303168 | tf_op jit(solution)/shard_map/reduce_scatter | solution.py:54
Sparse Core Ops, SparseCore 0:
  9.6 169.6 all-gather.2
  219.6 56.3 all-gather.4
  368.4 102.3 reduce-scatter.2
  496.4 636.2 reduce-scatter.4
where the time goes:
time: 1160 us; the launch traced here: 1150 us
  waiting for transfers between devices  965 us (83%)
  matrix products  90.3 us (8%)
  other arithmetic  40.7 us (4%)
  starting transfers between devices  20.2 us (2%)
  local copies, waits for them, and re-layouts  19.1 us (2%)
  between operations  14.2 us (1%)
    reduce_scatter x1, waiting for transfers between devices, per_device(): lax.psum_scatter(jnp.einsum('ij,ilc->jlc', columns, pulled, preferred_ele...  626 us
    all_gather x1, waiting for transfers between devices, per_device(): lax.all_gather(control, 'gx', axis=0, tiled=True)  171 us
    reduce_scatter x1, waiting for transfers between devices, per_device(): lax.psum_scatter(partial_sums, 'gy', scatter_dimension=2, tiled=True)  102 us
    all_gather x1, waiting for transfers between devices, per_device(): lax.all_gather(smoothed, 'gy', axis=2, tiled=True)  56.4 us
    dot_general x1, matrix products, per_device(): jnp.einsum('ij,jlc->ilc', columns, lax.all_gather(control, 'gx', axis=0,...  40.2 us
    another operation x3, other arithmetic, per_device(): fluxes = jnp.stack([courant_x * misfit, courant_y * misfit])  35.5 us
    dot_general x1, matrix products, per_device(): jnp.einsum('ij,ilc->jlc', columns, pulled, preferred_element_type=jnp.flo...  25.5 us
  transfers between devices with their start and end apart: 12, of which 8 were waited for; matrix products, arithmetic and copies ran while one was open for 1% of the time, Pallas kernels for 0%

commit v1 on v0

v1 whole, which is shorter than its diff:
```python
import functools

import jax
import jax.numpy as jnp
from jax import lax
from jax.experimental import pallas as pl
from jax.experimental.pallas import tpu as pltpu
from jax.sharding import PartitionSpec as P

BF16 = jnp.bfloat16
F32 = jnp.float32
STEP = 16
CHUNKS = 2
PARAMS = pltpu.CompilerParams(vmem_limit_bytes=56 * 1024 * 1024)


def cost(flops, *arrays):
    return pl.CostEstimate(
        flops=flops,
        bytes_accessed=sum(a.size * a.dtype.itemsize for a in arrays),
        transcendentals=0,
    )


def lines_body(parts, block, out, turned):
    levels, width = block.shape[1:]
    part = width // parts
    turned[...] = block[...].astype(F32)
    for l in range(levels):
        for s in range(parts):
            out[l * parts + s] = turned[:, l, s * part : (s + 1) * part].astype(BF16)


def as_lines(block, parts):
    rows, levels, width = block.shape
    shape = (levels * parts, rows, width // parts)
    return pl.pallas_call(
        functools.partial(lines_body, parts),
        grid=(rows // STEP,),
        in_specs=[pl.BlockSpec((STEP, levels, width), lambda i: (i, 0, 0))],
        out_specs=pl.BlockSpec((shape[0], STEP, shape[2]), lambda i: (0, i, 0)),
        out_shape=jax.ShapeDtypeStruct(shape, BF16),
        scratch_shapes=[pltpu.VMEM((STEP, levels, width), F32)],
        compiler_params=PARAMS,
        cost_estimate=cost(0, block, block),
        name="as_lines",
    )(block)


def gradient_body(parts, lines, control, out, turned):
    levels, width = control.shape[1:]
    part = width // parts
    for l in range(levels):
        for s in range(parts):
            turned[:, l, s * part : (s + 1) * part] = lines[l * parts + s].astype(F32)
    out[...] = control[...].astype(F32) + turned[...]


def add_lines(control, lines, parts):
    rows, levels, width = control.shape
    whole = (STEP, levels, width)
    return pl.pallas_call(
        functools.partial(gradient_body, parts),
        grid=(rows // STEP,),
        in_specs=[
            pl.BlockSpec((levels * parts, STEP, width // parts), lambda i: (0, i, 0)),
            pl.BlockSpec(whole, lambda i: (i, 0, 0)),
        ],
        out_specs=pl.BlockSpec(whole, lambda i: (i, 0, 0)),
        out_shape=jax.ShapeDtypeStruct(control.shape, F32),
        scratch_shapes=[pltpu.VMEM(whole, F32)],
        compiler_params=PARAMS,
        cost_estimate=cost(control.size, control, control, control, control),
        name="add_lines",
    )(lines, control)


def forward_body(parts, *refs):
    lines = refs[:CHUNKS]
    rows_in, sides, innovation, weight, wind_x, wind_y = refs[CHUNKS : CHUNKS + 6]
    end, flat, row_flux, side_flux, state, flux = refs[CHUNKS + 6 :]
    step = pl.program_id(0)
    rows, levels, width = flat.shape
    part = width // parts
    cut = rows // CHUNKS

    @pl.when(step == 0)
    def _():
        state[pl.ds(0, 1)] = rows_in[pl.ds(0, 1)]
        state[pl.ds(rows + 1, 1)] = rows_in[pl.ds(1, 1)]
        for h in range(CHUNKS):
            for l in range(levels):
                for s in range(parts):
                    got = lines[h][l * parts + s].astype(F32)
                    state[pl.ds(1 + h * cut, cut), l, s * part : (s + 1) * part] = got
        flux[pl.ds(0, 2)] = jnp.zeros((2, levels, width), F32)
        flux[pl.ds(rows + 2, 1)] = jnp.zeros((1, levels, width), F32)

    first = step * STEP
    place = lax.broadcasted_iota(jnp.int32, (STEP, levels, width), 2)
    left_edge, right_edge = place == 0, place == width - 1
    here = state[pl.ds(first + 1, STEP)]
    cx, cy = wind_x[...], wind_y[...]
    left = jnp.where(left_edge, sides[:, :, 0:1], pltpu.roll(here, 1, 2))
    right = jnp.where(right_edge, sides[:, :, 1:2], pltpu.roll(here, width - 1, 2))
    after = (
        here
        - cx * (state[pl.ds(first + 2, STEP)] - state[pl.ds(first, STEP)]) * 0.5
        - cy * (right - left) * 0.5
    )
    end[...] = after
    misfit = weight[...] * (after - innovation[...])
    p = cy * misfit
    side_flux[:, :, 0:1] = p[:, :, 0:1]
    side_flux[:, :, 1:2] = p[:, :, width - 1 : width]
    left = jnp.where(left_edge, 0.0, pltpu.roll(p, 1, 2))
    right = jnp.where(right_edge, 0.0, pltpu.roll(p, width - 1, 2))
    flat[pl.ds(first, STEP)] = misfit + 0.5 * (right - left)
    flux[pl.ds(first + 2, STEP)] = cx * misfit

    @pl.when(step == 0)
    def _():
        flat[pl.ds(0, STEP - 1)] += 0.5 * (
            flux[pl.ds(3, STEP - 1)] - flux[pl.ds(1, STEP - 1)]
        )

    @pl.when(step > 0)
    def _():
        flat[pl.ds(first - 1, STEP)] += 0.5 * (
            flux[pl.ds(first + 2, STEP)] - flux[pl.ds(first, STEP)]
        )

    @pl.when(step == rows // STEP - 1)
    def _():
        flat[pl.ds(rows - 1, 1)] += -0.5 * flux[pl.ds(rows, 1)]
        row_flux[pl.ds(0, 1)] = flux[pl.ds(2, 1)]
        row_flux[pl.ds(1, 1)] = flux[pl.ds(rows + 1, 1)]


def forward(lines, rows_in, sides, innovation, weight, wind_x, wind_y, parts):
    rows, levels, width = innovation.shape
    blocked = pl.BlockSpec((STEP, levels, width), lambda i: (i, 0, 0))
    side = pl.BlockSpec((STEP, levels, 2), lambda i: (i, 0, 0))
    pair = pl.BlockSpec((2, levels, width), lambda i: (0, 0, 0))
    line = pl.BlockSpec(lines[0].shape, lambda i: (0, 0, 0))
    whole = pl.BlockSpec((rows, levels, width), lambda i: (0, 0, 0))
    return pl.pallas_call(
        functools.partial(forward_body, parts),
        grid=(rows // STEP,),
        in_specs=[line] * CHUNKS + [pair, side, blocked, blocked, blocked, blocked],
        out_specs=[blocked, whole, pair, side],
        out_shape=[
            jax.ShapeDtypeStruct((rows, levels, width), F32),
            jax.ShapeDtypeStruct((rows, levels, width), F32),
            jax.ShapeDtypeStruct((2, levels, width), F32),
            jax.ShapeDtypeStruct((rows, levels, 2), F32),
        ],
        scratch_shapes=[
            pltpu.VMEM((rows + 2, levels, width), F32),
            pltpu.VMEM((rows + 3, levels, width), F32),
        ],
        compiler_params=PARAMS,
        cost_estimate=cost(30 * innovation.size, *[innovation] * 7),
        name="forward",
    )(*lines, rows_in, sides, innovation, weight, wind_x, wind_y)


def rim_body(parts, offset, last, flat, rows_in, sides, out, turned):
    step = pl.program_id(0) + offset
    levels, width = flat.shape[1:]
    part = width // parts
    place = lax.broadcasted_iota(jnp.int32, flat.shape, 2)
    value = flat[...]
    value = value - jnp.where(place == 0, 0.5 * sides[:, :, 0:1], 0.0)
    value = value + jnp.where(place == width - 1, 0.5 * sides[:, :, 1:2], 0.0)
    turned[...] = value

    @pl.when(step == 0)
    def _():
        turned[pl.ds(0, 1)] += -0.5 * rows_in[pl.ds(0, 1)]

    @pl.when(step == last)
    def _():
        turned[pl.ds(STEP - 1, 1)] += 0.5 * rows_in[pl.ds(1, 1)]

    for l in range(levels):
        for s in range(parts):
            out[l * parts + s] = turned[:, l, s * part : (s + 1) * part].astype(BF16)


def rim_lines(flat, rows_in, sides, parts, chunk):
    rows, levels, width = flat.shape
    cut = rows // CHUNKS
    offset = chunk * cut // STEP
    shape = (levels * parts, cut, width // parts)
    return pl.pallas_call(
        functools.partial(rim_body, parts, offset, rows // STEP - 1),
        grid=(cut // STEP,),
        in_specs=[
            pl.BlockSpec((STEP, levels, width), lambda i: (i + offset, 0, 0)),
            pl.BlockSpec((2, levels, width), lambda i: (0, 0, 0)),
            pl.BlockSpec((STEP, levels, 2), lambda i: (i + offset, 0, 0)),
        ],
        out_specs=pl.BlockSpec((shape[0], STEP, shape[2]), lambda i: (0, i, 0)),
        out_shape=jax.ShapeDtypeStruct(shape, BF16),
        scratch_shapes=[pltpu.VMEM((STEP, levels, width), F32)],
        compiler_params=PARAMS,
        cost_estimate=cost(4 * flat.size, flat, flat),
        name="rim_lines",
    )(flat, rows_in, sides)


def swap_all(lines):
    return lax.all_to_all(lines, "gx", 0, 0, tiled=True)


def plane_pieces(lines, parts):
    n_x, n_y = lax.axis_size("gx"), lax.axis_size("gy")
    groups = [list(range(i, i + parts)) for i in range(0, n_x, parts)]
    if n_y == 2 and parts == 2:
        pairs = [(a, b) for g in groups for a, b in (g, g[::-1])]
        far = lax.ppermute(lines, "gy", [(0, 1), (1, 0)])
        near = lax.ppermute(lines, "gx", pairs)
        cross = lax.ppermute(far, "gx", pairs)
        return [lines, near, far, cross]
    plane = lax.all_gather(lines, "gy", axis=0, tiled=False)
    plane = lax.all_gather(plane, "gx", axis=0, tiled=False, axis_index_groups=groups)
    return [plane[s, g] for s in range(parts) for g in range(n_y)]


def piece_order(parts):
    n_y = lax.axis_size("gy")
    sub, me = lax.rem(lax.axis_index("gx"), parts), lax.axis_index("gy")
    if n_y == 2 and parts == 2:
        return [(sub, me), (1 - sub, me), (sub, 1 - me), (1 - sub, 1 - me)]
    return [(s, g) for s in range(parts) for g in range(n_y)]


def filter_pieces(filter_y, parts):
    width, n_y = filter_y.shape[0], lax.axis_size("gy")
    part = width // parts
    sub, me = lax.rem(lax.axis_index("gx"), parts), lax.axis_index("gy")
    order = piece_order(parts)
    rows = [
        lax.dynamic_slice(filter_y, (sub * part, g * width + s * part), (part, part))
        for s, g in order
    ]
    if n_y == 2 and parts == 2:
        mine = lax.dynamic_slice(filter_y, (0, me * width + sub * part), (width, part))
        sent = lax.dynamic_slice(
            filter_y, (0, (1 - me) * width + sub * part), (width, part)
        )
        got = lax.ppermute(sent, "gy", [(0, 1), (1, 0)])
        columns = [
            lax.dynamic_slice_in_dim(source, s * part, part, axis=0)
            for source, (s, _) in zip((mine, mine, got, got), order)
        ]
    else:
        split = filter_y.reshape(width, n_y, parts, part)
        split = lax.dynamic_index_in_dim(split, sub, axis=2, keepdims=False)
        split = lax.all_to_all(split, "gy", 1, 0, tiled=True)
        split = split.reshape(n_y, parts, part, part)
        columns = [split[g, s] for s, g in order]
    return rows, columns


def row_halo(first, last):
    n_x = lax.axis_size("gx")
    up = [(i, i + 1) for i in range(n_x - 1)]
    down = [(i + 1, i) for i in range(n_x - 1)]
    return jnp.stack([lax.ppermute(last, "gx", up), lax.ppermute(first, "gx", down)])


def side_halo(first, last):
    n_y, me = lax.axis_size("gy"), lax.axis_index("gy")
    if n_y == 2:
        got = lax.ppermute(jnp.where(me == 0, last, first), "gy", [(0, 1), (1, 0)])
        none = jnp.zeros_like(got)
        return jnp.where(me == 0, none, got), jnp.where(me == 0, got, none)
    up = [(i, i + 1) for i in range(n_y - 1)]
    down = [(i + 1, i) for i in range(n_y - 1)]
    return lax.ppermute(last, "gy", up), lax.ppermute(first, "gy", down)


def per_device(control, innovation, obs_weight, courant_x, courant_y, filter_x, filter_y):
    rows, levels, width = control.shape
    n_x = lax.axis_size("gx")
    parts = n_x // levels
    part = width // parts
    cut = rows // CHUNKS

    lines = swap_all(as_lines(control, parts)).reshape(n_x * rows, part)
    matrix_x = lax.all_gather(filter_x, "gx", axis=0, tiled=True)
    rows_y, columns_y = filter_pieces(filter_y, parts)
    split_x = matrix_x.reshape(n_x, CHUNKS, cut, n_x * rows)

    came = []
    for h in range(CHUNKS):
        smoothed = jnp.einsum(
            "brj,jc->brc", split_x[:, h], lines, preferred_element_type=F32
        ).astype(BF16)
        start = sum(
            jnp.einsum("brc,kc->brk", piece, matrix, preferred_element_type=F32)
            for piece, matrix in zip(plane_pieces(smoothed, parts), rows_y)
        )
        came.append(swap_all(start.astype(BF16)))

    def as_row(edge):
        edge = edge.reshape(levels, parts * part)
        return edge

    rows_in = row_halo(as_row(came[0][:, 0]), as_row(came[-1][:, -1])).astype(F32)
    by_level = [c.reshape(levels, parts, cut, part) for c in came]
    first = jnp.concatenate([c[:, 0, :, 0] for c in by_level], axis=1)
    last = jnp.concatenate([c[:, -1, :, -1] for c in by_level], axis=1)
    before, after = side_halo(first, last)
    sides = jnp.stack([before.T, after.T], axis=2).astype(F32)

    end_state, flat, row_flux, side_flux = forward(
        came, rows_in, sides, innovation, obs_weight, courant_x, courant_y, parts
    )
    rows_in = row_halo(row_flux[0], row_flux[1])
    before, after = side_halo(side_flux[:, :, 0].T, side_flux[:, :, 1].T)
    sides = jnp.stack([before.T, after.T], axis=2)

    carried = 0.0
    for h in range(CHUNKS):
        adjoint = swap_all(rim_lines(flat, rows_in, sides, parts, h))
        pulled = sum(
            jnp.einsum("brk,kc->brc", piece, matrix, preferred_element_type=F32)
            for piece, matrix in zip(plane_pieces(adjoint, parts), columns_y)
        ).astype(BF16)
        carried = carried + jnp.einsum(
            "brj,brc->jc", split_x[:, h], pulled, preferred_element_type=F32
        )
    carried = swap_all(carried.astype(BF16).reshape(n_x, rows, part))
    return (end_state, add_lines(control, carried, parts))


def solution(mesh):
    placed = (
        P("gx", None, "gy"),
        P("gx", None, "gy"),
        P("gx", None, "gy"),
        P("gx", None, "gy"),
        P("gx", None, "gy"),
        P("gx", None),
        P("gy", None),
    )
    return jax.shard_map(
        per_device,
        mesh=mesh,
        in_specs=placed,
        out_specs=(P("gx", None, "gy"), P("gx", None, "gy")),
        check_vma=False,
    )
```

time: 1160 us -> 472 us (0.41)
  waiting for transfers between devices: 965 us -> 140 us
  blocking collectives: 0 us -> 151 us
  Pallas kernels: 0 us -> 41.8 us
  other arithmetic: 40.7 us -> 2.79 us
  starting transfers between devices: 20.2 us -> 49.1 us
  matrix products: 90.3 us -> 63.3 us
  local copies, waits for them, and re-layouts: 19.1 us -> 7.32 us
    reduce_scatter x2 -> x0, waiting for transfers between devices: 729 us -> none  [the longest x1 626 us: per_device(): lax.psum_scatter(jnp.einsum('ij,ilc->jlc', columns, pulled, preferred_ele...]
    all_gather x2 -> x1, waiting for transfers between devices: 228 us -> 3.05 us  [per_device(): matrix_x = lax.all_gather(filter_x, 'gx', axis=0, tiled=True)]
    all_to_all x0 -> x2, blocking collectives: none -> 151 us  [swap_all(): return lax.all_to_all(lines, 'gx', 0, 0, tiled=True)]
    all_to_all x0 -> x4, waiting for transfers between devices: none -> 70.5 us  [swap_all(): return lax.all_to_all(lines, 'gx', 0, 0, tiled=True)]
    ppermute x8 -> x19, waiting for transfers between devices: 7.88 us -> 65.3 us  [the longest x4 50.5 us: plane_pieces(): far = lax.ppermute(lines, 'gy', [(0, 1), (1, 0)])]
    pallas_call x0 -> x5, Pallas kernels: none -> 41.8 us  [the longest x1 16.6 us: forward(): pl.pallas_call(functools.partial(forward_body, parts), grid=(rows // STEP...]
    another operation x3 -> x4, other arithmetic: 35.5 us -> 0.64 us  [the longest x1 0.63 us: row_halo(): jnp.stack([lax.ppermute(last, 'gx', up), lax.ppermute(first, 'gx', down)])]
    dot_general x4 -> x18, matrix products: 90.3 us -> 63.3 us  [the longest x6 19.8 us: per_device(): jnp.einsum('brk,kc->brc', piece, matrix, preferred_element_type=F32)]
  transfers between devices with their start and end apart: 12 -> 24, of which waited for: 8 -> 9; matrix products, arithmetic and copies ran while one was open for 1% -> 11% of each run, Pallas kernels for 0% -> 3%
where the time goes in v1:
time: 472 us; the launch traced here: 469 us
  blocking collectives  151 us (32%)
  waiting for transfers between devices  140 us (30%)
  matrix products  63.3 us (13%)
  starting transfers between devices  49.1 us (10%)
  Pallas kernels  41.8 us (9%)
  between operations  14.3 us (3%)
  local copies, waits for them, and re-layouts  7.32 us (2%)
    all_to_all x2, blocking collectives, swap_all(): return lax.all_to_all(lines, 'gx', 0, 0, tiled=True)  151 us
    all_to_all x4, waiting for transfers between devices, swap_all(): return lax.all_to_all(lines, 'gx', 0, 0, tiled=True)  70.5 us
    ppermute x4, waiting for transfers between devices, plane_pieces(): far = lax.ppermute(lines, 'gy', [(0, 1), (1, 0)])  50.5 us
    all_to_all x4, starting transfers between devices, swap_all(): return lax.all_to_all(lines, 'gx', 0, 0, tiled=True)  26.2 us
    dot_general x6, matrix products, per_device(): jnp.einsum('brk,kc->brc', piece, matrix, preferred_element_type=F32)  19.8 us
    dot_general x2, matrix products, per_device(): jnp.einsum('brj,brc->jc', split_x[:, h], pulled, preferred_element_type=F32)  18.9 us
    pallas_call x1, Pallas kernels, forward(): pl.pallas_call(functools.partial(forward_body, parts), grid=(rows // STEP...  16.6 us
    ppermute x1, waiting for transfers between devices, filter_pieces(): got = lax.ppermute(sent, 'gy', [(0, 1), (1, 0)])  14.8 us
  transfers between devices with their start and end apart: 24, of which 9 were waited for; matrix products, arithmetic and copies ran while one was open for 11% of the time, Pallas kernels for 3%

profile of v1, /device:TPU:9, one launch (start us, length us, event | category | flops | bytes accessed | tf_op | source)
XLA Modules:
  0.0 469.1 jit_solution(11622072049026504764)
XLA Ops:
  7.9 7.9 %as_lines.1 = bf16[16,128,512]{2,1,0:T(8,128)(2,1)} custom-call(bf16[128,8,1024]{2,1,0:T(8,128)(2,1)} %control.1), custom_call_target="tpu_custom_call" | custom-call | bytes 4194304 | tf_op jit(solution)/shard_map/as_lines/pallas_call | solution.py:37
  15.8 97.4 %all_to_all.30 = bf16[16,128,512]{2,1,0:T(8,128)(2,1)S(1)} all-to-all(bf16[16,128,512]{2,1,0:T(8,128)(2,1)} %as_lines.1), channel_id=1, replica_groups=mesh['gx'=16,'gy'=2] {'gx'}, dimensions={0} | all-to-all | bytes 4194304 | tf_op jit(solution)/shard_map/all_to_all | solution.py:214
  113.2 3.0 all-gather.2.cloned.1.call-done
  116.2 5.5 %fusion.7 = bf16[16,64,512]{2,1,0:T(8,128)(2,1)} fusion(bf16[2048,512,1]{1,0,2:T(8,128)(2,1)S(1)} %bitcast.131, bf16[16,2,64,2048]{3,2,1,0:T(8,128)(2,1)} %bitcast.140), kind=kOutput, calls=%fused_computation.14 | convolution fusion | flops 2148007936 | bytes 7340032 | tf_op jit(solution)/shard_map/brj,jc->brc/dot_general | solution.py:299
  121.7 1.4 collective-permute-start.1
  123.8 22.4 %collective-permute-done.1 = bf16[16,64,512]{2,1,0:T(8,128)(2,1)S(1)} collective-permute-done((bf16[16,64,512]{2,1,0:T(8,128)(2,1)}, bf16[16,64,512]{2,1,0:T(8,128)(2,1)S(1)}, u32[]{:S(2)}, u32[]{:S(2)}) %collective-permute-start.1) | collective-permute-done | bytes 1048608 | tf_op jit(solution)/shard_map/ppermute | solution.py:222
  146.2 1.3 collective-permute-start.2
  147.5 5.5 %fusion.6 = bf16[16,64,512]{2,1,0:T(8,128)(2,1)} fusion(bf16[2048,512,1]{1,0,2:T(8,128)(2,1)S(1)} %bitcast.132, bf16[16,2,64,2048]{3,2,1,0:T(8,128)(2,1)} %bitcast.141), kind=kOutput, calls=%fused_computation.13 | convolution fusion | flops 2148007936 | bytes 7340032 | tf_op jit(solution)/shard_map/brj,jc->brc/dot_general | solution.py:299
  153.0 1.4 collective-permute-start.4
  154.4 2.0 fusion.36
  157.9 1.7 add_convert_fusion.3
  159.6 9.0 %all-to-all-start.1 = ((bf16[16,64,512]{2,1,0:T(8,128)(2,1)}), bf16[16,64,512]{2,1,0:T(8,128)(2,1)S(1)}, u32[]{:S(2)}, u32[]{:S(2)}) async-start(bf16[16,64,512]{2,1,0:T(8,128)(2,1)} %add_convert_fusion.3), calls=%async_computation.1 | async-start | bytes 2097152 | tf_op jit(solution)/shard_map/all_to_all | solution.py:214
  169.0 9.0 %collective-permute-done.4 = bf16[16,64,512]{2,1,0:T(8,128)(2,1)S(1)} collective-permute-done((bf16[16,64,512]{2,1,0:T(8,128)(2,1)}, bf16[16,64,512]{2,1,0:T(8,128)(2,1)S(1)}, u32[]{:S(2)}, u32[]{:S(2)}) %collective-permute-start.4) | collective-permute-done | bytes 1048608 | tf_op jit(solution)/shard_map/ppermute | solution.py:222
  178.8 2.1 fusion.34
  180.9 1.8 fusion.26
  182.7 1.8 fusion.30
  184.5 2.8 add_convert_fusion.2
  187.2 6.2 %all-to-all-done.1.refs_0_ = bf16[16,64,512]{2,1,0:T(8,128)(2,1)S(1)} async-done(((bf16[16,64,512]{2,1,0:T(8,128)(2,1)}), bf16[16,64,512]{2,1,0:T(8,128)(2,1)S(1)}, u32[]{:S(2)}, u32[]{:S(2)}) %all-to-all-start.1) | async-done | bytes 1048608 | tf_op jit(solution)/shard_map/all_to_all | solution.py:214
  193.4 5.0 %all-to-all-start.2 = ((bf16[16,64,512]{2,1,0:T(8,128)(2,1)}), bf16[16,64,512]{2,1,0:T(8,128)(2,1)S(1)}, u32[]{:S(2)}, u32[]{:S(2)}) async-start(bf16[16,64,512]{2,1,0:T(8,128)(2,1)} %add_convert_fusion.2), calls=%async_computation.2 | async-start | bytes 2097152 | tf_op jit(solution)/shard_map/all_to_all | solution.py:214
  198.5 2.3 collective-permute-start.7
  200.8 22.5 %all-to-all-done.2.refs_1_ = bf16[16,64,512]{2,1,0:T(8,128)(2,1)S(1)} async-done(((bf16[16,64,512]{2,1,0:T(8,128)(2,1)}), bf16[16,64,512]{2,1,0:T(8,128)(2,1)S(1)}, u32[]{:S(2)}, u32[]{:S(2)}) %all-to-all-start.2) | async-done | bytes 1048608 | tf_op jit(solution)/shard_map/all_to_all | solution.py:214
  224.4 3.7 collective-permute-start.6
  229.8 16.6 %forward.1 = (f32[128,8,1024]{2,1,0:T(8,128)}, f32[128,8,1024]{2,1,0:T(8,128)}, f32[2,8,1024]{2,1,0:T(8,128)}, f32[128,8,2]{2,1,0:T(8,128)}) custom-call(bf16[16,64,512]{2,1,0:T(8,128)(2,1)} %copy-done.1, bf16[16,64,512]{2,1,0:T(8,128)(2,1)} %copy-done.2, f32[2,8,1024]{2,1,0:T(8,128)} %maximum_convert_fusion.refs_2_, f32[128,8,2]{2,1,0:T(8,128)} %copy.114.refs_3_, ...), custom_call_target="tpu_custom_call" | custom-call | flops 31457280 | bytes 29360128 | tf_op jit(solution)/shard_map/forward/pallas_call | solution.py:147
  246.4 1.4 slice_select_fusion
  248.1 1.3 collective-permute-start.11
  249.3 3.4 collective-permute-start.10
  252.7 2.6 collective-permute-start.9
  257.0 5.1 %rim_lines.2 = bf16[16,64,512]{2,1,0:T(8,128)(2,1)} custom-call(f32[128,8,1024]{2,1,0:T(8,128)} %get-tuple-element.7.flat, f32[2,8,1024]{2,1,0:T(8,128)} %pad_maximum_fusion.rows_in, f32[128,8,2]{2,1,0:T(8,128)} %copy.116.sides), custom_call_target="tpu_custom_call" | custom-call | flops 4194304 | bytes 8388608 | tf_op jit(solution)/shard_map/rim_lines/pallas_call | solution.py:196
  262.1 7.3 %all-to-all-start.3 = ((bf16[16,64,512]{2,1,0:T(8,128)(2,1)}), bf16[16,64,512]{2,1,0:T(8,128)(2,1)S(1)}, u32[]{:S(2)}, u32[]{:S(2)}) async-start(bf16[16,64,512]{2,1,0:T(8,128)(2,1)} %rim_lines.2), calls=%async_computation.3 | async-start | bytes 2097152 | tf_op jit(solution)/shard_map/all_to_all | solution.py:214
  269.4 5.0 %rim_lines.3 = bf16[16,64,512]{2,1,0:T(8,128)(2,1)} custom-call(f32[128,8,1024]{2,1,0:T(8,128)} %get-tuple-element.7.flat, f32[2,8,1024]{2,1,0:T(8,128)} %pad_maximum_fusion.rows_in, f32[128,8,2]{2,1,0:T(8,128)} %copy.116.sides), custom_call_target="tpu_custom_call" | custom-call | flops 4194304 | bytes 8388608 | tf_op jit(solution)/shard_map/rim_lines/pallas_call | solution.py:196
  274.4 19.9 %all-to-all-done.3 = bf16[16,64,512]{2,1,0:T(8,128)(2,1)S(1)} async-done(((bf16[16,64,512]{2,1,0:T(8,128)(2,1)}), bf16[16,64,512]{2,1,0:T(8,128)(2,1)S(1)}, u32[]{:S(2)}, u32[]{:S(2)}) %all-to-all-start.3) | async-done | bytes 1048608 | tf_op jit(solution)/shard_map/all_to_all | solution.py:214
  294.2 5.0 %all-to-all-start.4 = ((bf16[16,64,512]{2,1,0:T(8,128)(2,1)}), bf16[16,64,512]{2,1,0:T(8,128)(2,1)S(1)}, u32[]{:S(2)}, u32[]{:S(2)}) async-start(bf16[16,64,512]{2,1,0:T(8,128)(2,1)} %rim_lines.3), calls=%async_computation.4 | async-start | bytes 2097152 | tf_op jit(solution)/shard_map/all_to_all | solution.py:214
  299.4 1.3 constant_dynamic-slice_fusion
  300.7 1.3 collective-permute-start.14
  302.0 22.0 %all-to-all-done.4 = bf16[16,64,512]{2,1,0:T(8,128)(2,1)S(1)} async-done(((bf16[16,64,512]{2,1,0:T(8,128)(2,1)}), bf16[16,64,512]{2,1,0:T(8,128)(2,1)S(1)}, u32[]{:S(2)}, u32[]{:S(2)}) %all-to-all-start.4) | async-done | bytes 1048608 | tf_op jit(solution)/shard_map/all_to_all | solution.py:214
  324.8 3.2 fusion.22
  328.0 3.3 fusion.20
  331.4 14.8 %collective-permute-done.14 = bf16[1024,512]{1,0:T(8,128)(2,1)} collective-permute-done((bf16[1024,512]{1,0:T(8,128)(2,1)S(1)}, bf16[1024,512]{1,0:T(8,128)(2,1)}, u32[]{:S(2)}, u32[]{:S(2)}) %collective-permute-start.14) | collective-permute-done | bytes 1048608 | tf_op jit(solution)/shard_map/ppermute | solution.py:253
  346.2 3.4 fusion.14
  349.6 19.1 %collective-permute-done.17 = bf16[16,64,512]{2,1,0:T(8,128)(2,1)} collective-permute-done((bf16[16,64,512]{2,1,0:T(8,128)(2,1)S(1)}, bf16[16,64,512]{2,1,0:T(8,128)(2,1)}, u32[]{:S(2)}, u32[]{:S(2)}) %collective-permute-start.17) | collective-permute-done | bytes 1048608 | tf_op jit(solution)/shard_map/ppermute | solution.py:222
  369.8 3.4 fusion.12
  373.3 3.2 fusion.18
  376.5 3.2 fusion.16
  379.7 9.7 %fusion.1 = f32[512,2048,1]{1,0,2:T(8,128)} fusion(bf16[16,2,64,2048]{3,2,1,0:T(8,128)(2,1)} %bitcast.142, f32[16,64,512]{2,1,0:T(8,128)} %fusion.14, f32[16,64,512]{2,1,0:T(8,128)} %fusion.22, f32[16,64,512]{2,1,0:T(8,128)} %fusion.18, bf16[16,64,512]{2,1,0:T(8,128)(2,1)} %collective-permute-done.15, bf16[1024,512]{1,0:T(8,128)(2,1)} %collective-permute-done.14, ...), kind=kOutput, calls=%fused_computation.4 | convolution fusion | flops 2686451712 | bytes 16252932 | tf_op jit(solution)/shard_map/brj,brc->jc/dot_general | solution.py:333
  389.4 9.2 %fusion.5 = bf16[2048,512]{0,1:T(8,128)(2,1)} fusion(bf16[16,2,64,2048]{3,2,1,0:T(8,128)(2,1)} %bitcast.143, f32[512,2048,1]{1,0,2:T(8,128)} %fusion.1, f32[16,64,512]{2,1,0:T(8,128)} %fusion.12, f32[16,64,512]{2,1,0:T(8,128)S(1)} %copy-done.3, f32[16,64,512]{2,1,0:T(8,128)} %fusion.16, bf16[16,64,512]{2,1,0:T(8,128)(2,1)S(1)} %collective-permute-done.18, ...), kind=kOutput, calls=%fused_computation.8 | convolution fusion | flops 2688548864 | bytes 18350084 | tf_op jit(solution)/shard_map/brj,brc->jc/dot_general | solution.py:333
  398.6 2.9 copy.118
  401.5 53.5 %all_to_all.31.lines = bf16[16,128,512]{2,1,0:T(8,128)(2,1)} all-to-all(bf16[16,128,512]{2,1,0:T(8,128)(2,1)S(1)} %bitcast.128), channel_id=1, replica_groups=mesh['gx'=16,'gy'=2] {'gx'}, dimensions={0} | all-to-all | bytes 4194304 | tf_op jit(solution)/shard_map/all_to_all | solution.py:214
  455.0 7.2 %add_lines.1 = f32[128,8,1024]{2,1,0:T(8,128)} custom-call(bf16[16,128,512]{2,1,0:T(8,128)(2,1)} %all_to_all.31.lines, bf16[128,8,1024]{2,1,0:T(8,128)(2,1)} %control.1), custom_call_target="tpu_custom_call" | custom-call | flops 1048576 | bytes 8388608 | tf_op jit(solution)/shard_map/add_lines/pallas_call | solution.py:62
  (58 shorter events, 11.1 us)
Async XLA Ops:
  7.2 109.1 %all-gather.2.cloned.1.call-start = ((), (), s32[]{:S(2)}) async-start(), calls=%async_computation.6 | async-start | bytes 8912896 | tf_op jit(solution)/shard_map/all_gather | solution.py:293
  121.7 24.5 %collective-permute-start.1 = (bf16[16,64,512]{2,1,0:T(8,128)(2,1)}, bf16[16,64,512]{2,1,0:T(8,128)(2,1)S(1)}, u32[]{:S(2)}, u32[]{:S(2)}) collective-permute-start(bf16[16,64,512]{2,1,0:T(8,128)(2,1)} %fusion.7), channel_id=1, source_target_pairs={{0,1},{1,0},{2,3},{3,2},{4,5},{5,4},{6,7},{7,6},{8,9},{9,8},{10,11... | collective-permute-start | bytes 3145736 | tf_op jit(solution)/shard_map/ppermute | solution.py:222
  123.1 31.3 %copy-start = (bf16[1024,2048]{1,0:T(8,128)(2,1)S(1)}, bf16[1024,2048]{1,0:T(8,128)(2,1)}, u32[]{:S(2)}) copy-start(bf16[1024,2048]{1,0:T(8,128)(2,1)} %param.13) | copy-start | bytes 12582916
  123.1 34.0 %collective-permute-start = (bf16[16,64,512]{2,1,0:T(8,128)(2,1)}, bf16[16,64,512]{2,1,0:T(8,128)(2,1)S(1)}, u32[]{:S(2)}, u32[]{:S(2)}) collective-permute-start(bf16[16,64,512]{2,1,0:T(8,128)(2,1)} %fusion.7), channel_id=1, source_target_pairs={{0,2},{2,0},{4,6},{6,4},{8,10},{10,8},{12,14},{14,12},{16,18},{18,... | collective-permute-start | bytes 3145736 | tf_op jit(solution)/shard_map/ppermute | solution.py:223
  146.2 11.7 %collective-permute-start.2 = (bf16[16,64,512]{2,1,0:T(8,128)(2,1)S(1)}, bf16[16,64,512]{2,1,0:T(8,128)(2,1)S(1)}, u32[]{:S(2)}, u32[]{:S(2)}) collective-permute-start(bf16[16,64,512]{2,1,0:T(8,128)(2,1)S(1)} %collective-permute-done.1), channel_id=1, source_target_pairs={{0,2},{2,0},{4,6},{6,4},{8,10},{10,8},{12,14},{14,12},{16,18},{18,... | collective-permute-start | bytes 3145736 | tf_op jit(solution)/shard_map/ppermute | solution.py:224
  153.0 25.0 %collective-permute-start.4 = (bf16[16,64,512]{2,1,0:T(8,128)(2,1)}, bf16[16,64,512]{2,1,0:T(8,128)(2,1)S(1)}, u32[]{:S(2)}, u32[]{:S(2)}) collective-permute-start(bf16[16,64,512]{2,1,0:T(8,128)(2,1)} %fusion.6), channel_id=1, source_target_pairs={{0,1},{1,0},{2,3},{3,2},{4,5},{5,4},{6,7},{7,6},{8,9},{9,8},{10,11... | collective-permute-start | bytes 3145736 | tf_op jit(solution)/shard_map/ppermute | solution.py:222
  159.6 33.8 %all-to-all-start.1 = ((bf16[16,64,512]{2,1,0:T(8,128)(2,1)}), bf16[16,64,512]{2,1,0:T(8,128)(2,1)S(1)}, u32[]{:S(2)}, u32[]{:S(2)}) async-start(bf16[16,64,512]{2,1,0:T(8,128)(2,1)} %add_convert_fusion.3), calls=%async_computation.1 | async-start | bytes 2097152 | tf_op jit(solution)/shard_map/all_to_all | solution.py:214
  168.6 14.1 %collective-permute-start.3 = (bf16[16,64,512]{2,1,0:T(8,128)(2,1)}, bf16[16,64,512]{2,1,0:T(8,128)(2,1)S(1)}, u32[]{:S(2)}, u32[]{:S(2)}) collective-permute-start(bf16[16,64,512]{2,1,0:T(8,128)(2,1)} %fusion.6), channel_id=1, source_target_pairs={{0,2},{2,0},{4,6},{6,4},{8,10},{10,8},{12,14},{14,12},{16,18},{18,... | collective-permute-start | bytes 3145736 | tf_op jit(solution)/shard_map/ppermute | solution.py:223
  178.0 6.5 %collective-permute-start.5 = (bf16[16,64,512]{2,1,0:T(8,128)(2,1)S(1)}, bf16[16,64,512]{2,1,0:T(8,128)(2,1)S(1)}, u32[]{:S(2)}, u32[]{:S(2)}) collective-permute-start(bf16[16,64,512]{2,1,0:T(8,128)(2,1)S(1)} %collective-permute-done.4), channel_id=1, source_target_pairs={{0,2},{2,0},{4,6},{6,4},{8,10},{10,8},{12,14},{14,12},{16,18},{18,... | collective-permute-start | bytes 3145736 | tf_op jit(solution)/shard_map/ppermute | solution.py:224
  193.4 36.3 %copy-start.1 = (bf16[16,64,512]{2,1,0:T(8,128)(2,1)}, bf16[16,64,512]{2,1,0:T(8,128)(2,1)S(1)}, u32[]{:S(2)}) copy-start(bf16[16,64,512]{2,1,0:T(8,128)(2,1)S(1)} %all-to-all-done.1.refs_0_) | copy-start | bytes 3145732
  193.4 29.8 %all-to-all-start.2 = ((bf16[16,64,512]{2,1,0:T(8,128)(2,1)}), bf16[16,64,512]{2,1,0:T(8,128)(2,1)S(1)}, u32[]{:S(2)}, u32[]{:S(2)}) async-start(bf16[16,64,512]{2,1,0:T(8,128)(2,1)} %add_convert_fusion.2), calls=%async_computation.2 | async-start | bytes 2097152 | tf_op jit(solution)/shard_map/all_to_all | solution.py:214
  198.5 30.6 %collective-permute-start.7 = (bf16[8,1024]{1,0:T(8,128)(2,1)S(1)}, bf16[8,1024]{1,0:T(8,128)(2,1)S(1)}, u32[]{:S(2)}, u32[]{:S(2)}) collective-permute-start(bf16[8,1024]{1,0:T(8,128)(2,1)S(1)} %reshape_squeeze.7), channel_id=1, source_target_pairs={{2,0},{4,2},{6,4},{8,6},{10,8},{12,10},{14,12},{16,14},{18,16},{20... | collective-permute-start | bytes 49160 | tf_op jit(solution)/shard_map/ppermute | solution.py:271
  223.2 6.5 %copy-start.2 = (bf16[16,64,512]{2,1,0:T(8,128)(2,1)}, bf16[16,64,512]{2,1,0:T(8,128)(2,1)S(1)}, u32[]{:S(2)}) copy-start(bf16[16,64,512]{2,1,0:T(8,128)(2,1)S(1)} %all-to-all-done.2.refs_1_) | copy-start | bytes 3145732
  224.0 4.1 collective-permute-start.8
  224.4 4.8 %collective-permute-start.6 = (bf16[8,1024]{1,0:T(8,128)(2,1)S(1)}, bf16[8,1024]{1,0:T(8,128)(2,1)S(1)}, u32[]{:S(2)}, u32[]{:S(2)}) collective-permute-start(bf16[8,1024]{1,0:T(8,128)(2,1)S(1)} %reshape_squeeze.6), channel_id=1, source_target_pairs={{0,2},{2,4},{4,6},{6,8},{8,10},{10,12},{12,14},{14,16},{16,18},{18... | collective-permute-start | bytes 49160 | tf_op jit(solution)/shard_map/ppermute | solution.py:271
  246.4 2.9 copy-start.4
  248.1 7.3 %collective-permute-start.11 = (f32[8,128]{1,0:T(8,128)S(1)}, f32[8,128]{1,0:T(8,128)S(1)}, u32[]{:S(2)}, u32[]{:S(2)}) collective-permute-start(f32[8,128]{1,0:T(8,128)S(1)} %bitcast.139), channel_id=1, source_target_pairs={{0,1},{1,0},{2,3},{3,2},{4,5},{5,4},{6,7},{7,6},{8,9},{9,8},{10,11... | collective-permute-start | bytes 12296 | tf_op jit(solution)/shard_map/ppermute | solution.py:277
  249.3 7.1 %collective-permute-start.10 = (f32[8,1024]{1,0:T(8,128)S(1)}, f32[8,1024]{1,0:T(8,128)S(1)}, u32[]{:S(2)}, u32[]{:S(2)}) collective-permute-start(f32[8,1024]{1,0:T(8,128)S(1)} %get-tuple-element.15), channel_id=1, source_target_pairs={{2,0},{4,2},{6,4},{8,6},{10,8},{12,10},{14,12},{16,14},{18,16},{20... | collective-permute-start | bytes 98312 | tf_op jit(solution)/shard_map/ppermute | solution.py:271
  252.7 3.7 collective-permute-start.9
  262.1 32.1 %all-to-all-start.3 = ((bf16[16,64,512]{2,1,0:T(8,128)(2,1)}), bf16[16,64,512]{2,1,0:T(8,128)(2,1)S(1)}, u32[]{:S(2)}, u32[]{:S(2)}) async-start(bf16[16,64,512]{2,1,0:T(8,128)(2,1)} %rim_lines.2), calls=%async_computation.3 | async-start | bytes 2097152 | tf_op jit(solution)/shard_map/all_to_all | solution.py:214
  294.2 29.8 %all-to-all-start.4 = ((bf16[16,64,512]{2,1,0:T(8,128)(2,1)}), bf16[16,64,512]{2,1,0:T(8,128)(2,1)S(1)}, u32[]{:S(2)}, u32[]{:S(2)}) async-start(bf16[16,64,512]{2,1,0:T(8,128)(2,1)} %rim_lines.3), calls=%async_computation.4 | async-start | bytes 2097152 | tf_op jit(solution)/shard_map/all_to_all | solution.py:214
  299.2 32.1 %collective-permute-start.13 = (bf16[16,64,512]{2,1,0:T(8,128)(2,1)S(1)}, bf16[16,64,512]{2,1,0:T(8,128)(2,1)}, u32[]{:S(2)}, u32[]{:S(2)}) collective-permute-start(bf16[16,64,512]{2,1,0:T(8,128)(2,1)S(1)} %all-to-all-done.3), channel_id=1, source_target_pairs={{0,1},{1,0},{2,3},{3,2},{4,5},{5,4},{6,7},{7,6},{8,9},{9,8},{10,11... | collective-permute-start | bytes 3145736 | tf_op jit(solution)/shard_map/ppermute | solution.py:222
  300.7 45.4 %collective-permute-start.14 = (bf16[1024,512]{1,0:T(8,128)(2,1)S(1)}, bf16[1024,512]{1,0:T(8,128)(2,1)}, u32[]{:S(2)}, u32[]{:S(2)}) collective-permute-start(bf16[1024,512]{1,0:T(8,128)(2,1)S(1)} %constant_dynamic-slice_fusion), channel_id=1, source_target_pairs={{0,1},{1,0},{2,3},{3,2},{4,5},{5,4},{6,7},{7,6},{8,9},{9,8},{10,11... | collective-permute-start | bytes 3145736 | tf_op jit(solution)/shard_map/ppermute | solution.py:253
  324.1 44.6 %collective-permute-start.17 = (bf16[16,64,512]{2,1,0:T(8,128)(2,1)S(1)}, bf16[16,64,512]{2,1,0:T(8,128)(2,1)}, u32[]{:S(2)}, u32[]{:S(2)}) collective-permute-start(bf16[16,64,512]{2,1,0:T(8,128)(2,1)S(1)} %all-to-all-done.4), channel_id=1, source_target_pairs={{0,1},{1,0},{2,3},{3,2},{4,5},{5,4},{6,7},{7,6},{8,9},{9,8},{10,11... | collective-permute-start | bytes 3145736 | tf_op jit(solution)/shard_map/ppermute | solution.py:222
  324.3 49.0 %collective-permute-start.12 = (bf16[16,64,512]{2,1,0:T(8,128)(2,1)S(1)}, bf16[16,64,512]{2,1,0:T(8,128)(2,1)S(1)}, u32[]{:S(2)}, u32[]{:S(2)}) collective-permute-start(bf16[16,64,512]{2,1,0:T(8,128)(2,1)S(1)} %all-to-all-done.3), channel_id=1, source_target_pairs={{0,2},{2,0},{4,6},{6,4},{8,10},{10,8},{12,14},{14,12},{16,18},{18,... | collective-permute-start | bytes 3145736 | tf_op jit(solution)/shard_map/ppermute | solution.py:223
  324.3 52.2 %collective-permute-start.16 = (bf16[16,64,512]{2,1,0:T(8,128)(2,1)S(1)}, bf16[16,64,512]{2,1,0:T(8,128)(2,1)S(1)}, u32[]{:S(2)}, u32[]{:S(2)}) collective-permute-start(bf16[16,64,512]{2,1,0:T(8,128)(2,1)S(1)} %all-to-all-done.4), channel_id=1, source_target_pairs={{0,2},{2,0},{4,6},{6,4},{8,10},{10,8},{12,14},{14,12},{16,18},{18,... | collective-permute-start | bytes 3145736 | tf_op jit(solution)/shard_map/ppermute | solution.py:223
  331.3 48.4 %collective-permute-start.15 = (bf16[16,64,512]{2,1,0:T(8,128)(2,1)}, bf16[16,64,512]{2,1,0:T(8,128)(2,1)}, u32[]{:S(2)}, u32[]{:S(2)}) collective-permute-start(bf16[16,64,512]{2,1,0:T(8,128)(2,1)} %collective-permute-done.13), channel_id=1, source_target_pairs={{0,2},{2,0},{4,6},{6,4},{8,10},{10,8},{12,14},{14,12},{16,18},{18,... | collective-permute-start | bytes 3145736 | tf_op jit(solution)/shard_map/ppermute | solution.py:224
  368.6 20.8 %collective-permute-start.18 = (bf16[16,64,512]{2,1,0:T(8,128)(2,1)}, bf16[16,64,512]{2,1,0:T(8,128)(2,1)S(1)}, u32[]{:S(2)}, u32[]{:S(2)}) collective-permute-start(bf16[16,64,512]{2,1,0:T(8,128)(2,1)} %collective-permute-done.17), channel_id=1, source_target_pairs={{0,2},{2,0},{4,6},{6,4},{8,10},{10,8},{12,14},{14,12},{16,18},{18,... | collective-permute-start | bytes 3145736 | tf_op jit(solution)/shard_map/ppermute | solution.py:224
  379.7 9.7 %copy-start.3 = (f32[16,64,512]{2,1,0:T(8,128)S(1)}, f32[16,64,512]{2,1,0:T(8,128)}, u32[]{:S(2)}) copy-start(f32[16,64,512]{2,1,0:T(8,128)} %fusion.20) | copy-start | bytes 6291460
Sparse Core Ops, SparseCore 0:
  10.2 106.0 all-gather.1

commit v2 on v1

--- a/solution.py
+++ b/solution.py
@@ -47,12 +47,16 @@
     )(block)
 
 
-def gradient_body(parts, lines, control, out, turned):
+def gradient_body(parts, *refs):
+    lines, (control, out, turned) = refs[:CHUNKS], refs[CHUNKS:]
     levels, width = control.shape[1:]
-    part = width // parts
+    piece = width // parts // CHUNKS
     for l in range(levels):
         for s in range(parts):
-            turned[:, l, s * part : (s + 1) * part] = lines[l * parts + s].astype(F32)
+            for w in range(CHUNKS):
+                at = (s * CHUNKS + w) * piece
+                got = lines[w][l * parts + s].astype(F32)
+                turned[:, l, at : at + piece] = got
     out[...] = control[...].astype(F32) + turned[...]
 
 
@@ -63,16 +67,16 @@
         functools.partial(gradient_body, parts),
         grid=(rows // STEP,),
         in_specs=[
-            pl.BlockSpec((levels * parts, STEP, width // parts), lambda i: (0, i, 0)),
-            pl.BlockSpec(whole, lambda i: (i, 0, 0)),
-        ],
+            pl.BlockSpec((l.shape[0], STEP, l.shape[2]), lambda i: (0, i, 0)) for l in lines
+        ]
+        + [pl.BlockSpec(whole, lambda i: (i, 0, 0))],
         out_specs=pl.BlockSpec(whole, lambda i: (i, 0, 0)),
         out_shape=jax.ShapeDtypeStruct(control.shape, F32),
         scratch_shapes=[pltpu.VMEM(whole, F32)],
         compiler_params=PARAMS,
         cost_estimate=cost(control.size, control, control, control, control),
         name="add_lines",
-    )(lines, control)
+    )(*lines, control)
 
 
 def forward_body(parts, *refs):
@@ -97,38 +101,31 @@
         flux[pl.ds(rows + 2, 1)] = jnp.zeros((1, levels, width), F32)
 
     first = step * STEP
-    place = lax.broadcasted_iota(jnp.int32, (STEP, levels, width), 2)
+    place = lax.broadcasted_iota(jnp.int32, (levels, width), 1)
     left_edge, right_edge = place == 0, place == width - 1
-    here = state[pl.ds(first + 1, STEP)]
-    cx, cy = wind_x[...], wind_y[...]
-    left = jnp.where(left_edge, sides[:, :, 0:1], pltpu.roll(here, 1, 2))
-    right = jnp.where(right_edge, sides[:, :, 1:2], pltpu.roll(here, width - 1, 2))
-    after = (
-        here
-        - cx * (state[pl.ds(first + 2, STEP)] - state[pl.ds(first, STEP)]) * 0.5
-        - cy * (right - left) * 0.5
-    )
-    end[...] = after
-    misfit = weight[...] * (after - innovation[...])
-    p = cy * misfit
-    side_flux[:, :, 0:1] = p[:, :, 0:1]
-    side_flux[:, :, 1:2] = p[:, :, width - 1 : width]
-    left = jnp.where(left_edge, 0.0, pltpu.roll(p, 1, 2))
-    right = jnp.where(right_edge, 0.0, pltpu.roll(p, width - 1, 2))
-    flat[pl.ds(first, STEP)] = misfit + 0.5 * (right - left)
-    flux[pl.ds(first + 2, STEP)] = cx * misfit
-
-    @pl.when(step == 0)
-    def _():
-        flat[pl.ds(0, STEP - 1)] += 0.5 * (
-            flux[pl.ds(3, STEP - 1)] - flux[pl.ds(1, STEP - 1)]
-        )
-
-    @pl.when(step > 0)
-    def _():
-        flat[pl.ds(first - 1, STEP)] += 0.5 * (
-            flux[pl.ds(first + 2, STEP)] - flux[pl.ds(first, STEP)]
-        )
+    for j in range(STEP):
+        r = first + j
+        here = state[r + 1]
+        cx, cy = wind_x[j], wind_y[j]
+        left = jnp.where(left_edge, sides[j, :, 0:1], pltpu.roll(here, 1, 1))
+        right = jnp.where(right_edge, sides[j, :, 1:2], pltpu.roll(here, width - 1, 1))
+        after = here - cx * (state[r + 2] - state[r]) * 0.5 - cy * (right - left) * 0.5
+        end[j] = after
+        misfit = weight[j] * (after - innovation[j])
+        p, q = cy * misfit, cx * misfit
+        side_flux[j, :, 0:1] = p[:, 0:1]
+        side_flux[j, :, 1:2] = p[:, width - 1 : width]
+        left = jnp.where(left_edge, 0.0, pltpu.roll(p, 1, 1))
+        right = jnp.where(right_edge, 0.0, pltpu.roll(p, width - 1, 1))
+        flat[r] = misfit + 0.5 * (right - left)
+        flux[r + 2] = q
+        if j > 0:
+            flat[r - 1] += 0.5 * (q - flux[r])
+        else:
+
+            @pl.when(step > 0)
+            def _():
+                flat[r - 1] += 0.5 * (flux[r + 2] - flux[r])
 
     @pl.when(step == rows // STEP - 1)
     def _():
@@ -289,16 +286,20 @@
     part = width // parts
     cut = rows // CHUNKS
 
-    lines = swap_all(as_lines(control, parts)).reshape(n_x * rows, part)
-    matrix_x = lax.all_gather(filter_x, "gx", axis=0, tiled=True)
+    turned = as_lines(control, parts)
     rows_y, columns_y = filter_pieces(filter_y, parts)
-    split_x = matrix_x.reshape(n_x, CHUNKS, cut, n_x * rows)
+    matrix_x = [lax.all_gather(filter_x[:cut], "gx", axis=0, tiled=True)]
+    lines = swap_all(turned).reshape(n_x * rows, part)
+    lines, filter_x = lax.optimization_barrier((lines, filter_x))
+    for h in range(1, CHUNKS):
+        share = filter_x[h * cut : (h + 1) * cut]
+        matrix_x.append(lax.all_gather(share, "gx", axis=0, tiled=True))
+    lines, columns_y = lax.optimization_barrier((lines, columns_y))
 
     came = []
     for h in range(CHUNKS):
-        smoothed = jnp.einsum(
-            "brj,jc->brc", split_x[:, h], lines, preferred_element_type=F32
-        ).astype(BF16)
+        smoothed = jnp.dot(matrix_x[h], lines, preferred_element_type=F32)
+        smoothed = smoothed.astype(BF16).reshape(n_x, cut, part)
         start = sum(
             jnp.einsum("brc,kc->brk", piece, matrix, preferred_element_type=F32)
             for piece, matrix in zip(plane_pieces(smoothed, parts), rows_y)
@@ -323,17 +324,31 @@
     before, after = side_halo(side_flux[:, :, 0].T, side_flux[:, :, 1].T)
     sides = jnp.stack([before.T, after.T], axis=2)
 
-    carried = 0.0
-    for h in range(CHUNKS):
-        adjoint = swap_all(rim_lines(flat, rows_in, sides, parts, h))
-        pulled = sum(
-            jnp.einsum("brk,kc->brc", piece, matrix, preferred_element_type=F32)
-            for piece, matrix in zip(plane_pieces(adjoint, parts), columns_y)
-        ).astype(BF16)
-        carried = carried + jnp.einsum(
-            "brj,brc->jc", split_x[:, h], pulled, preferred_element_type=F32
-        )
-    carried = swap_all(carried.astype(BF16).reshape(n_x, rows, part))
+    planes = [
+        plane_pieces(swap_all(rim_lines(flat, rows_in, sides, parts, h)), parts)
+        for h in range(CHUNKS)
+    ]
+    piece = part // CHUNKS
+    carried = []
+    for w in range(CHUNKS):
+        total = 0.0
+        for h in range(CHUNKS):
+            pulled = sum(
+                jnp.einsum(
+                    "brk,kc->brc",
+                    plane,
+                    matrix[:, w * piece : (w + 1) * piece],
+                    preferred_element_type=F32,
+                )
+                for plane, matrix in zip(planes[h], columns_y)
+            ).astype(BF16)
+            total = total + jnp.einsum(
+                "ij,ic->jc",
+                matrix_x[h],
+                pulled.reshape(n_x * cut, piece),
+                preferred_element_type=F32,
+            )
+        carried.append(swap_all(total.astype(BF16).reshape(n_x, rows, piece)))
     return (end_state, add_lines(control, carried, parts))
 
 

time: 472 us -> 458 us (0.970)
  blocking collectives: 151 us -> 107 us
  waiting for transfers between devices: 140 us -> 159 us
  local copies, waits for them, and re-layouts: 7.32 us -> 23.6 us
  matrix products: 63.3 us -> 52.6 us
    all_to_all x2, blocking collectives: 151 us -> 107 us  [swap_all(): return lax.all_to_all(lines, 'gx', 0, 0, tiled=True)]
    dot_general x10 -> x22, matrix products: 49.7 us -> 33.1 us  [the longest x16 15.2 us: per_device(): jnp.einsum('brk,kc->brc', plane, matrix[:, w * piece:(w + 1) * piece], pr...]
    all_to_all x4 -> x5, waiting for transfers between devices: 70.5 us -> 82.1 us  [swap_all(): return lax.all_to_all(lines, 'gx', 0, 0, tiled=True)]
    ppermute x1, waiting for transfers between devices: 14.8 us -> 20.9 us  [filter_pieces(): got = lax.ppermute(sent, 'gy', [(0, 1), (1, 0)])]
    dot_general x8, matrix products: 13.6 us -> 19.6 us  [per_device(): jnp.einsum('brc,kc->brk', piece, matrix, preferred_element_type=F32)]
    unnamed x12 -> x46, local copies, waits for them, and re-layouts: 0.28 us -> 6.1 us
    dynamic_slice x0 -> x2, local copies, waits for them, and re-layouts: none -> 4.72 us  [filter_pieces(): lax.dynamic_slice_in_dim(source, s * part, part, axis=0)]
    all_to_all x4 -> x5, starting transfers between devices: 26.2 us -> 26 us  [swap_all(): return lax.all_to_all(lines, 'gx', 0, 0, tiled=True)]
  transfers between devices with their start and end apart: 24 -> 26, of which waited for: 9 -> 10; matrix products, arithmetic and copies ran while one was open for 11% -> 14% of each run, Pallas kernels for 3% -> 3%
where the time goes in v2:
time: 458 us; the launch traced here: 456 us
  waiting for transfers between devices  159 us (35%)
  blocking collectives  107 us (23%)
  matrix products  52.6 us (11%)
  starting transfers between devices  50.5 us (11%)
  Pallas kernels  45.9 us (10%)
  local copies, waits for them, and re-layouts  23.6 us (5%)
  between operations  14.5 us (3%)
    all_to_all x2, blocking collectives, swap_all(): return lax.all_to_all(lines, 'gx', 0, 0, tiled=True)  107 us
    all_to_all x5, waiting for transfers between devices, swap_all(): return lax.all_to_all(lines, 'gx', 0, 0, tiled=True)  82.1 us
    ppermute x4, waiting for transfers between devices, plane_pieces(): far = lax.ppermute(lines, 'gy', [(0, 1), (1, 0)])  53.9 us
    all_to_all x5, starting transfers between devices, swap_all(): return lax.all_to_all(lines, 'gx', 0, 0, tiled=True)  26 us
    ppermute x1, waiting for transfers between devices, filter_pieces(): got = lax.ppermute(sent, 'gy', [(0, 1), (1, 0)])  20.9 us
    pallas_call x1, Pallas kernels, forward(): pl.pallas_call(functools.partial(forward_body, parts), grid=(rows // STEP...  20.3 us
    dot_general x8, matrix products, per_device(): jnp.einsum('brc,kc->brk', piece, matrix, preferred_element_type=F32)  19.6 us
    dot_general x16, matrix products, per_device(): jnp.einsum('brk,kc->brc', plane, matrix[:, w * piece:(w + 1) * piece], pr...  15.2 us
  transfers between devices with their start and end apart: 26, of which 10 were waited for; matrix products, arithmetic and copies ran while one was open for 14% of the time, Pallas kernels for 3%

profile of v2, /device:TPU:9, one launch (start us, length us, event | category | flops | bytes accessed | tf_op | source)
XLA Modules:
  0.0 455.9 jit_solution(14468727602003956104)
XLA Ops:
  7.2 1.7 slice.68
  8.9 7.9 %as_lines.1 = bf16[16,128,512]{2,1,0:T(8,128)(2,1)} custom-call(bf16[128,8,1024]{2,1,0:T(8,128)(2,1)} %refs_2_.1), custom_call_target="tpu_custom_call" | custom-call | bytes 4194304 | tf_op jit(solution)/shard_map/as_lines/pallas_call | solution.py:37
  16.9 76.6 %all_to_all.35 = bf16[16,128,512]{2,1,0:T(8,128)(2,1)S(1)} all-to-all(bf16[16,128,512]{2,1,0:T(8,128)(2,1)} %as_lines.1), channel_id=1, replica_groups=mesh['gx'=16,'gy'=2] {'gx'}, dimensions={0} | all-to-all | bytes 4194304 | tf_op jit(solution)/shard_map/all_to_all | solution.py:211
  94.2 2.3 constant_dynamic-slice_fusion.2
  97.7 2.7 fusion.67
  100.4 20.9 %collective-permute-done = bf16[1024,512]{1,0:T(8,128)(2,1)} collective-permute-done((bf16[1024,512]{1,0:T(8,128)(2,1)}, bf16[1024,512]{1,0:T(8,128)(2,1)}, u32[]{:S(2)}, u32[]{:S(2)}) %collective-permute-start) | collective-permute-done | bytes 1048608 | tf_op jit(solution)/shard_map/ppermute | solution.py:250
  121.2 2.1 constant_dynamic-slice_fusion
  123.3 5.6 %fusion.4 = bf16[1024,512]{0,1:T(8,128)(2,1)} fusion(bf16[2048,512]{1,0:T(8,128)(2,1)S(1)} %bitcast.154, bf16[1024,2048]{1,0:T(8,128)(2,1)} %all-gather.3.cloned.1.call-done), kind=kOutput, calls=%fused_computation.10 | convolution fusion | flops 2148007936 | bytes 7340032 | tf_op jit(solution)/shard_map/dot_general | solution.py:301
  128.9 2.3 copy.132
  133.8 2.1 fusion.21
  136.0 19.0 %collective-permute-done.2 = bf16[16,64,512]{2,1,0:T(8,128)(2,1)} collective-permute-done((bf16[16,64,512]{2,1,0:T(8,128)(2,1)}, bf16[16,64,512]{2,1,0:T(8,128)(2,1)}, u32[]{:S(2)}, u32[]{:S(2)}) %collective-permute-start.2) | collective-permute-done | bytes 1048608 | tf_op jit(solution)/shard_map/ppermute | solution.py:219
  155.0 2.1 collective-permute-start.3
  157.1 3.4 fusion.13
  160.5 6.2 %convolution_convert_fusion = bf16[1024,512]{1,0:T(8,128)(2,1)} fusion(bf16[1024,2048]{1,0:T(8,128)(2,1)} %all-gather.5.cloned.1.call-done, bf16[2048,512]{1,0:T(8,128)(2,1)} %bitcast.155), kind=kOutput, calls=%fused_computation.8 | convolution fusion | flops 2148007936 | bytes 7340032 | tf_op jit(solution)/shard_map/dot_general | solution.py:301
  167.8 2.1 fusion.17
  169.9 3.2 add_convert_fusion.1
  173.1 4.7 %all-to-all-start.1 = ((bf16[16,64,512]{2,1,0:T(8,128)(2,1)}), bf16[16,64,512]{2,1,0:T(8,128)(2,1)S(1)}, u32[]{:S(2)}, u32[]{:S(2)}) async-start(bf16[16,64,512]{2,1,0:T(8,128)(2,1)} %add_convert_fusion.1), calls=%async_computation.1 | async-start | bytes 2097152 | tf_op jit(solution)/shard_map/all_to_all | solution.py:211
  178.2 13.5 %collective-permute-done.5 = bf16[16,64,512]{2,1,0:T(8,128)(2,1)} collective-permute-done((bf16[16,64,512]{2,1,0:T(8,128)(2,1)}, bf16[16,64,512]{2,1,0:T(8,128)(2,1)}, u32[]{:S(2)}, u32[]{:S(2)}) %collective-permute-start.5) | collective-permute-done | bytes 1048608 | tf_op jit(solution)/shard_map/ppermute | solution.py:219
  192.5 2.1 fusion.19
  194.6 2.1 fusion.11
  196.7 1.8 fusion.15
  198.5 2.8 add_convert_fusion
  202.7 5.0 %all-to-all-start.2 = ((bf16[16,64,512]{2,1,0:T(8,128)(2,1)}), bf16[16,64,512]{2,1,0:T(8,128)(2,1)S(1)}, u32[]{:S(2)}, u32[]{:S(2)}) async-start(bf16[16,64,512]{2,1,0:T(8,128)(2,1)} %add_convert_fusion), calls=%async_computation.2 | async-start | bytes 2097152 | tf_op jit(solution)/shard_map/all_to_all | solution.py:211
  207.8 2.5 collective-permute-start.8
  210.5 22.0 %all-to-all-done.2.refs_1_ = bf16[16,64,512]{2,1,0:T(8,128)(2,1)S(1)} async-done(((bf16[16,64,512]{2,1,0:T(8,128)(2,1)}), bf16[16,64,512]{2,1,0:T(8,128)(2,1)S(1)}, u32[]{:S(2)}, u32[]{:S(2)}) %all-to-all-start.2) | async-done | bytes 1048608 | tf_op jit(solution)/shard_map/all_to_all | solution.py:211
  233.4 3.5 collective-permute-start.7
  238.6 20.3 %forward.1 = (f32[128,8,1024]{2,1,0:T(8,128)}, f32[128,8,1024]{2,1,0:T(8,128)}, f32[2,8,1024]{2,1,0:T(8,128)}, f32[128,8,2]{2,1,0:T(8,128)}) custom-call(bf16[16,64,512]{2,1,0:T(8,128)(2,1)} %copy-done.1, bf16[16,64,512]{2,1,0:T(8,128)(2,1)} %copy-done.2, f32[2,8,1024]{2,1,0:T(8,128)} %maximum_convert_fusion.refs_2_, f32[128,8,2]{2,1,0:T(8,128)} %copy.135.refs_3_, ...), custom_call_target="tpu_custom_call" | custom-call | flops 31457280 | bytes 29360128 | tf_op jit(solution)/shard_map/forward/pallas_call | solution.py:144
  261.8 4.3 collective-permute-start.10
  266.1 1.9 collective-permute-start.11
  269.1 2.2 collective-permute-done.11
  271.9 4.9 %rim_lines.3 = bf16[16,64,512]{2,1,0:T(8,128)(2,1)} custom-call(f32[128,8,1024]{2,1,0:T(8,128)} %get-tuple-element.17.flat, f32[2,8,1024]{2,1,0:T(8,128)} %pad_maximum_fusion.rows_in, f32[128,8,2]{2,1,0:T(8,128)} %copy.137.sides), custom_call_target="tpu_custom_call" | custom-call | flops 4194304 | bytes 8388608 | tf_op jit(solution)/shard_map/rim_lines/pallas_call | solution.py:193
  276.9 6.2 %all-to-all-start.4 = ((bf16[16,64,512]{2,1,0:T(8,128)(2,1)}), bf16[16,64,512]{2,1,0:T(8,128)(2,1)S(1)}, u32[]{:S(2)}, u32[]{:S(2)}) async-start(bf16[16,64,512]{2,1,0:T(8,128)(2,1)} %rim_lines.3), calls=%async_computation.4 | async-start | bytes 2097152 | tf_op jit(solution)/shard_map/all_to_all | solution.py:211
  283.1 5.1 %rim_lines.2 = bf16[16,64,512]{2,1,0:T(8,128)(2,1)} custom-call(f32[128,8,1024]{2,1,0:T(8,128)} %get-tuple-element.17.flat, f32[2,8,1024]{2,1,0:T(8,128)} %pad_maximum_fusion.rows_in, f32[128,8,2]{2,1,0:T(8,128)} %copy.137.sides), custom_call_target="tpu_custom_call" | custom-call | flops 4194304 | bytes 8388608 | tf_op jit(solution)/shard_map/rim_lines/pallas_call | solution.py:193
  288.2 19.7 %all-to-all-done.4 = bf16[16,64,512]{2,1,0:T(8,128)(2,1)S(1)} async-done(((bf16[16,64,512]{2,1,0:T(8,128)(2,1)}), bf16[16,64,512]{2,1,0:T(8,128)(2,1)S(1)}, u32[]{:S(2)}, u32[]{:S(2)}) %all-to-all-start.4) | async-done | bytes 1048608 | tf_op jit(solution)/shard_map/all_to_all | solution.py:211
  307.9 5.0 %all-to-all-start.3 = ((bf16[16,64,512]{2,1,0:T(8,128)(2,1)}), bf16[16,64,512]{2,1,0:T(8,128)(2,1)S(1)}, u32[]{:S(2)}, u32[]{:S(2)}) async-start(bf16[16,64,512]{2,1,0:T(8,128)(2,1)} %rim_lines.2), calls=%async_computation.3 | async-start | bytes 2097152 | tf_op jit(solution)/shard_map/all_to_all | solution.py:211
  313.9 23.9 %all-to-all-done.3 = bf16[16,64,512]{2,1,0:T(8,128)(2,1)S(1)} async-done(((bf16[16,64,512]{2,1,0:T(8,128)(2,1)}), bf16[16,64,512]{2,1,0:T(8,128)(2,1)S(1)}, u32[]{:S(2)}, u32[]{:S(2)}) %all-to-all-start.3) | async-done | bytes 1048608 | tf_op jit(solution)/shard_map/all_to_all | solution.py:211
  341.4 21.3 %collective-permute-done.14 = bf16[16,64,512]{2,1,0:T(8,128)(2,1)S(1)} collective-permute-done((bf16[16,64,512]{2,1,0:T(8,128)(2,1)S(1)}, bf16[16,64,512]{2,1,0:T(8,128)(2,1)S(1)}, u32[]{:S(2)}, u32[]{:S(2)}) %collective-permute-start.14) | collective-permute-done | bytes 1048608 | tf_op jit(solution)/shard_map/ppermute | solution.py:219
  363.3 1.7 convolution_add_fusion.2
  365.0 1.7 convolution_add_fusion.8
  366.7 1.7 convolution_add_fusion.7
  368.4 2.6 convolution_add_fusion.1
  376.4 2.3 fusion.3
  378.6 2.4 copy.140
  381.1 5.2 %all-to-all-start.5 = ((bf16[16,128,256]{2,1,0:T(8,128)(2,1)}), bf16[16,128,256]{2,1,0:T(8,128)(2,1)}, u32[]{:S(2)}, u32[]{:S(2)}) async-start(bf16[16,128,256]{2,1,0:T(8,128)(2,1)} %bitcast.152), calls=%async_computation.5 | async-start | bytes 2097152 | tf_op jit(solution)/shard_map/all_to_all | solution.py:211
  386.3 1.7 convolution_add_fusion.5
  396.1 15.1 %all-to-all-done.5.refs_0_ = bf16[16,128,256]{2,1,0:T(8,128)(2,1)} async-done(((bf16[16,128,256]{2,1,0:T(8,128)(2,1)}), bf16[16,128,256]{2,1,0:T(8,128)(2,1)}, u32[]{:S(2)}, u32[]{:S(2)}) %all-to-all-start.5) | async-done | bytes 1048608 | tf_op jit(solution)/shard_map/all_to_all | solution.py:211
  411.2 30.2 %all_to_all.36.refs_1_ = bf16[16,128,256]{2,1,0:T(8,128)(2,1)} all-to-all(bf16[16,128,256]{2,1,0:T(8,128)(2,1)S(1)} %bitcast.153), channel_id=1, replica_groups=mesh['gx'=16,'gy'=2] {'gx'}, dimensions={0} | all-to-all | bytes 2097152 | tf_op jit(solution)/shard_map/all_to_all | solution.py:211
  441.4 7.6 %add_lines.1 = f32[128,8,1024]{2,1,0:T(8,128)} custom-call(bf16[16,128,256]{2,1,0:T(8,128)(2,1)} %all-to-all-done.5.refs_0_, bf16[16,128,256]{2,1,0:T(8,128)(2,1)} %all_to_all.36.refs_1_, bf16[128,8,1024]{2,1,0:T(8,128)(2,1)} %refs_2_.1), custom_call_target="tpu_custom_call" | custom-call | flops 1048576 | bytes 8388608 | tf_op jit(solution)/shard_map/add_lines/pallas_call | solution.py:66
  (115 shorter events, 34.4 us)
Async XLA Ops:
  7.2 116.1 %all-gather.3.cloned.1.call-start = ((), (), s32[]{:S(2)}) async-start(), calls=%async_computation.7 | async-start | bytes 4456448 | tf_op jit(solution)/shard_map/all_gather | solution.py:291
  8.9 151.6 %all-gather.5.cloned.1.call-start = ((), (), s32[]{:S(2)}) async-start(), calls=%async_computation.8 | async-start | bytes 4456448 | tf_op jit(solution)/shard_map/all_gather | solution.py:296
  16.9 76.6 %copy-start.16 = (bf16[128,2048]{1,0:T(8,128)(2,1)S(1)}, bf16[128,2048]{1,0:T(8,128)(2,1)}, u32[]{:S(2)}) copy-start(bf16[128,2048]{1,0:T(8,128)(2,1)} %param.12) | copy-start | bytes 1572868
  93.4 29.9 %copy-start.15 = (bf16[16,128,512]{2,1,0:T(8,128)(2,1)}, bf16[16,128,512]{2,1,0:T(8,128)(2,1)S(1)}, u32[]{:S(2)}) copy-start(bf16[16,128,512]{2,1,0:T(8,128)(2,1)S(1)} %all_to_all.35) | copy-start | bytes 6291460
  96.5 24.7 %collective-permute-start = (bf16[1024,512]{1,0:T(8,128)(2,1)}, bf16[1024,512]{1,0:T(8,128)(2,1)}, u32[]{:S(2)}, u32[]{:S(2)}) collective-permute-start(bf16[1024,512]{1,0:T(8,128)(2,1)} %constant_dynamic-slice_fusion.2), channel_id=1, source_target_pairs={{0,1},{1,0},{2,3},{3,2},{4,5},{5,4},{6,7},{7,6},{8,9},{9,8},{10,11... | collective-permute-start | bytes 3145736 | tf_op jit(solution)/shard_map/ppermute | solution.py:250
  131.2 23.8 %collective-permute-start.2 = (bf16[16,64,512]{2,1,0:T(8,128)(2,1)}, bf16[16,64,512]{2,1,0:T(8,128)(2,1)}, u32[]{:S(2)}, u32[]{:S(2)}) collective-permute-start(bf16[16,64,512]{2,1,0:T(8,128)(2,1)} %bitcast.2), channel_id=1, source_target_pairs={{0,1},{1,0},{2,3},{3,2},{4,5},{5,4},{6,7},{7,6},{8,9},{9,8},{10,11... | collective-permute-start | bytes 3145736 | tf_op jit(solution)/shard_map/ppermute | solution.py:219
  132.3 35.5 %collective-permute-start.1 = (bf16[16,64,512]{2,1,0:T(8,128)(2,1)}, bf16[16,64,512]{2,1,0:T(8,128)(2,1)}, u32[]{:S(2)}, u32[]{:S(2)}) collective-permute-start(bf16[16,64,512]{2,1,0:T(8,128)(2,1)} %bitcast.2), channel_id=1, source_target_pairs={{0,2},{2,0},{4,6},{6,4},{8,10},{10,8},{12,14},{14,12},{16,18},{18,... | collective-permute-start | bytes 3145736 | tf_op jit(solution)/shard_map/ppermute | solution.py:220
  155.0 15.0 %collective-permute-start.3 = (bf16[16,64,512]{2,1,0:T(8,128)(2,1)}, bf16[16,64,512]{2,1,0:T(8,128)(2,1)}, u32[]{:S(2)}, u32[]{:S(2)}) collective-permute-start(bf16[16,64,512]{2,1,0:T(8,128)(2,1)} %collective-permute-done.2), channel_id=1, source_target_pairs={{0,2},{2,0},{4,6},{6,4},{8,10},{10,8},{12,14},{14,12},{16,18},{18,... | collective-permute-start | bytes 3145736 | tf_op jit(solution)/shard_map/ppermute | solution.py:221
  166.6 3.3 copy-start
  166.6 25.1 %collective-permute-start.5 = (bf16[16,64,512]{2,1,0:T(8,128)(2,1)}, bf16[16,64,512]{2,1,0:T(8,128)(2,1)}, u32[]{:S(2)}, u32[]{:S(2)}) collective-permute-start(bf16[16,64,512]{2,1,0:T(8,128)(2,1)} %bitcast.7), channel_id=1, source_target_pairs={{0,1},{1,0},{2,3},{3,2},{4,5},{5,4},{6,7},{7,6},{8,9},{9,8},{10,11... | collective-permute-start | bytes 3145736 | tf_op jit(solution)/shard_map/ppermute | solution.py:219
  173.1 29.6 %all-to-all-start.1 = ((bf16[16,64,512]{2,1,0:T(8,128)(2,1)}), bf16[16,64,512]{2,1,0:T(8,128)(2,1)S(1)}, u32[]{:S(2)}, u32[]{:S(2)}) async-start(bf16[16,64,512]{2,1,0:T(8,128)(2,1)} %add_convert_fusion.1), calls=%async_computation.1 | async-start | bytes 2097152 | tf_op jit(solution)/shard_map/all_to_all | solution.py:211
  177.8 18.9 %collective-permute-start.4 = (bf16[16,64,512]{2,1,0:T(8,128)(2,1)}, bf16[16,64,512]{2,1,0:T(8,128)(2,1)S(1)}, u32[]{:S(2)}, u32[]{:S(2)}) collective-permute-start(bf16[16,64,512]{2,1,0:T(8,128)(2,1)} %bitcast.7), channel_id=1, source_target_pairs={{0,2},{2,0},{4,6},{6,4},{8,10},{10,8},{12,14},{14,12},{16,18},{18,... | collective-permute-start | bytes 3145736 | tf_op jit(solution)/shard_map/ppermute | solution.py:220
  191.7 6.8 %collective-permute-start.6 = (bf16[16,64,512]{2,1,0:T(8,128)(2,1)}, bf16[16,64,512]{2,1,0:T(8,128)(2,1)S(1)}, u32[]{:S(2)}, u32[]{:S(2)}) collective-permute-start(bf16[16,64,512]{2,1,0:T(8,128)(2,1)} %collective-permute-done.5), channel_id=1, source_target_pairs={{0,2},{2,0},{4,6},{6,4},{8,10},{10,8},{12,14},{14,12},{16,18},{18,... | collective-permute-start | bytes 3145736 | tf_op jit(solution)/shard_map/ppermute | solution.py:221
  202.7 36.0 %copy-start.1 = (bf16[16,64,512]{2,1,0:T(8,128)(2,1)}, bf16[16,64,512]{2,1,0:T(8,128)(2,1)S(1)}, u32[]{:S(2)}) copy-start(bf16[16,64,512]{2,1,0:T(8,128)(2,1)S(1)} %all-to-all-done.1.refs_0_) | copy-start | bytes 3145732
  202.7 29.8 %all-to-all-start.2 = ((bf16[16,64,512]{2,1,0:T(8,128)(2,1)}), bf16[16,64,512]{2,1,0:T(8,128)(2,1)S(1)}, u32[]{:S(2)}, u32[]{:S(2)}) async-start(bf16[16,64,512]{2,1,0:T(8,128)(2,1)} %add_convert_fusion), calls=%async_computation.2 | async-start | bytes 2097152 | tf_op jit(solution)/shard_map/all_to_all | solution.py:211
  207.8 30.3 %collective-permute-start.8 = (bf16[8,1024]{1,0:T(8,128)(2,1)S(1)}, bf16[8,1024]{1,0:T(8,128)(2,1)S(1)}, u32[]{:S(2)}, u32[]{:S(2)}) collective-permute-start(bf16[8,1024]{1,0:T(8,128)(2,1)S(1)} %reshape_squeeze.7), channel_id=1, source_target_pairs={{2,0},{4,2},{6,4},{8,6},{10,8},{12,10},{14,12},{16,14},{18,16},{20... | collective-permute-start | bytes 49160 | tf_op jit(solution)/shard_map/ppermute | solution.py:268
  232.5 6.2 %copy-start.2 = (bf16[16,64,512]{2,1,0:T(8,128)(2,1)}, bf16[16,64,512]{2,1,0:T(8,128)(2,1)S(1)}, u32[]{:S(2)}) copy-start(bf16[16,64,512]{2,1,0:T(8,128)(2,1)S(1)} %all-to-all-done.2.refs_1_) | copy-start | bytes 3145732
  233.0 4.0 collective-permute-start.9
  233.4 4.6 %collective-permute-start.7 = (bf16[8,1024]{1,0:T(8,128)(2,1)S(1)}, bf16[8,1024]{1,0:T(8,128)(2,1)S(1)}, u32[]{:S(2)}, u32[]{:S(2)}) collective-permute-start(bf16[8,1024]{1,0:T(8,128)(2,1)S(1)} %reshape_squeeze.6), channel_id=1, source_target_pairs={{0,2},{2,4},{4,6},{6,8},{8,10},{10,12},{12,14},{14,16},{16,18},{18... | collective-permute-start | bytes 49160 | tf_op jit(solution)/shard_map/ppermute | solution.py:268
  259.0 2.8 copy-start.17
  260.6 7.4 %collective-permute-start.12 = (f32[8,128]{1,0:T(8,128)S(1)}, f32[8,128]{1,0:T(8,128)S(1)}, u32[]{:S(2)}, u32[]{:S(2)}) collective-permute-start(f32[8,128]{1,0:T(8,128)S(1)} %bitcast.166), channel_id=1, source_target_pairs={{0,1},{1,0},{2,3},{3,2},{4,5},{5,4},{6,7},{7,6},{8,9},{9,8},{10,11... | collective-permute-start | bytes 12296 | tf_op jit(solution)/shard_map/ppermute | solution.py:274
  261.8 7.3 %collective-permute-start.10 = (f32[8,1024]{1,0:T(8,128)S(1)}, f32[8,1024]{1,0:T(8,128)S(1)}, u32[]{:S(2)}, u32[]{:S(2)}) collective-permute-start(f32[8,1024]{1,0:T(8,128)S(1)} %get-tuple-element.32), channel_id=1, source_target_pairs={{0,2},{2,4},{4,6},{6,8},{8,10},{10,12},{12,14},{14,16},{16,18},{18... | collective-permute-start | bytes 98312 | tf_op jit(solution)/shard_map/ppermute | solution.py:268
  266.1 5.2 %collective-permute-start.11 = (f32[8,1024]{1,0:T(8,128)S(1)}, f32[8,1024]{1,0:T(8,128)S(1)}, u32[]{:S(2)}, u32[]{:S(2)}) collective-permute-start(f32[8,1024]{1,0:T(8,128)S(1)} %get-tuple-element.33), channel_id=1, source_target_pairs={{2,0},{4,2},{6,4},{8,6},{10,8},{12,10},{14,12},{16,14},{18,16},{20... | collective-permute-start | bytes 98312 | tf_op jit(solution)/shard_map/ppermute | solution.py:268
  276.9 31.1 %all-to-all-start.4 = ((bf16[16,64,512]{2,1,0:T(8,128)(2,1)}), bf16[16,64,512]{2,1,0:T(8,128)(2,1)S(1)}, u32[]{:S(2)}, u32[]{:S(2)}) async-start(bf16[16,64,512]{2,1,0:T(8,128)(2,1)} %rim_lines.3), calls=%async_computation.4 | async-start | bytes 2097152 | tf_op jit(solution)/shard_map/all_to_all | solution.py:211
  307.9 29.8 %all-to-all-start.3 = ((bf16[16,64,512]{2,1,0:T(8,128)(2,1)}), bf16[16,64,512]{2,1,0:T(8,128)(2,1)S(1)}, u32[]{:S(2)}, u32[]{:S(2)}) async-start(bf16[16,64,512]{2,1,0:T(8,128)(2,1)} %rim_lines.2), calls=%async_computation.3 | async-start | bytes 2097152 | tf_op jit(solution)/shard_map/all_to_all | solution.py:211
  312.9 27.9 %collective-permute-start.17 = (bf16[16,64,512]{2,1,0:T(8,128)(2,1)S(1)}, bf16[16,64,512]{2,1,0:T(8,128)(2,1)}, u32[]{:S(2)}, u32[]{:S(2)}) collective-permute-start(bf16[16,64,512]{2,1,0:T(8,128)(2,1)S(1)} %all-to-all-done.4), channel_id=1, source_target_pairs={{0,1},{1,0},{2,3},{3,2},{4,5},{5,4},{6,7},{7,6},{8,9},{9,8},{10,11... | collective-permute-start | bytes 3145736 | tf_op jit(solution)/shard_map/ppermute | solution.py:219
  313.2 50.1 %collective-permute-start.16 = (bf16[16,64,512]{2,1,0:T(8,128)(2,1)S(1)}, bf16[16,64,512]{2,1,0:T(8,128)(2,1)}, u32[]{:S(2)}, u32[]{:S(2)}) collective-permute-start(bf16[16,64,512]{2,1,0:T(8,128)(2,1)S(1)} %all-to-all-done.4), channel_id=1, source_target_pairs={{0,2},{2,0},{4,6},{6,4},{8,10},{10,8},{12,14},{14,12},{16,18},{18,... | collective-permute-start | bytes 3145736 | tf_op jit(solution)/shard_map/ppermute | solution.py:220
  337.7 25.0 %collective-permute-start.14 = (bf16[16,64,512]{2,1,0:T(8,128)(2,1)S(1)}, bf16[16,64,512]{2,1,0:T(8,128)(2,1)S(1)}, u32[]{:S(2)}, u32[]{:S(2)}) collective-permute-start(bf16[16,64,512]{2,1,0:T(8,128)(2,1)S(1)} %all-to-all-done.3), channel_id=1, source_target_pairs={{0,1},{1,0},{2,3},{3,2},{4,5},{5,4},{6,7},{7,6},{8,9},{9,8},{10,11... | collective-permute-start | bytes 3145736 | tf_op jit(solution)/shard_map/ppermute | solution.py:219
  338.1 33.0 %collective-permute-start.13 = (bf16[16,64,512]{2,1,0:T(8,128)(2,1)S(1)}, bf16[16,64,512]{2,1,0:T(8,128)(2,1)S(1)}, u32[]{:S(2)}, u32[]{:S(2)}) collective-permute-start(bf16[16,64,512]{2,1,0:T(8,128)(2,1)S(1)} %all-to-all-done.3), channel_id=1, source_target_pairs={{0,2},{2,0},{4,6},{6,4},{8,10},{10,8},{12,14},{14,12},{16,18},{18,... | collective-permute-start | bytes 3145736 | tf_op jit(solution)/shard_map/ppermute | solution.py:220
  339.0 24.3 %copy-start.3 = (bf16[512,512]{1,0:T(8,128)(2,1)S(1)}, bf16[512,512]{1,0:T(8,128)(2,1)}, u32[]{:S(2)}) copy-start(bf16[512,512]{1,0:T(8,128)(2,1)} %get-tuple-element.21) | copy-start | bytes 1572868
  340.8 31.2 %collective-permute-start.18 = (bf16[16,64,512]{2,1,0:T(8,128)(2,1)}, bf16[16,64,512]{2,1,0:T(8,128)(2,1)S(1)}, u32[]{:S(2)}, u32[]{:S(2)}) collective-permute-start(bf16[16,64,512]{2,1,0:T(8,128)(2,1)} %collective-permute-done.17), channel_id=1, source_target_pairs={{0,2},{2,0},{4,6},{6,4},{8,10},{10,8},{12,14},{14,12},{16,18},{18,... | collective-permute-start | bytes 3145736 | tf_op jit(solution)/shard_map/ppermute | solution.py:221
  362.7 8.8 %copy-start.6 = (bf16[16,64,512]{2,1,0:T(8,128)(2,1)}, bf16[16,64,512]{2,1,0:T(8,128)(2,1)S(1)}, u32[]{:S(2)}) copy-start(bf16[16,64,512]{2,1,0:T(8,128)(2,1)S(1)} %collective-permute-done.14) | copy-start | bytes 3145732
  362.7 12.7 %collective-permute-start.15 = (bf16[16,64,512]{2,1,0:T(8,128)(2,1)S(1)}, bf16[16,64,512]{2,1,0:T(8,128)(2,1)S(1)}, u32[]{:S(2)}, u32[]{:S(2)}) collective-permute-start(bf16[16,64,512]{2,1,0:T(8,128)(2,1)S(1)} %collective-permute-done.14), channel_id=1, source_target_pairs={{0,2},{2,0},{4,6},{6,4},{8,10},{10,8},{12,14},{14,12},{16,18},{18,... | collective-permute-start | bytes 3145736 | tf_op jit(solution)/shard_map/ppermute | solution.py:221
  365.0 1.7 copy-start.5
  371.0 1.0 copy-start.8
  371.5 2.6 copy-start.20
  372.0 3.3 copy-start.11
  374.1 2.3 copy-start.18
  375.4 1.0 copy-start.13
  378.6 7.6 %copy-start.4 = (bf16[512,512]{1,0:T(8,128)(2,1)S(1)}, bf16[512,512]{1,0:T(8,128)(2,1)}, u32[]{:S(2)}) copy-start(bf16[512,512]{1,0:T(8,128)(2,1)} %get-tuple-element.21) | copy-start | bytes 1572868
  378.6 7.6 %copy-start.9 = (bf16[16,64,512]{2,1,0:T(8,128)(2,1)S(1)}, bf16[16,64,512]{2,1,0:T(8,128)(2,1)}, u32[]{:S(2)}) copy-start(bf16[16,64,512]{2,1,0:T(8,128)(2,1)} %copy-done.8) | copy-start | bytes 3145732
  381.1 30.1 %all-to-all-start.5 = ((bf16[16,128,256]{2,1,0:T(8,128)(2,1)}), bf16[16,128,256]{2,1,0:T(8,128)(2,1)}, u32[]{:S(2)}, u32[]{:S(2)}) async-start(bf16[16,128,256]{2,1,0:T(8,128)(2,1)} %bitcast.152), calls=%async_computation.5 | async-start | bytes 2097152 | tf_op jit(solution)/shard_map/all_to_all | solution.py:211
  386.2 1.8 copy-start.7
  388.0 1.2 copy-start.10
  388.0 1.5 copy-start.12
  389.6 1.2 copy-start.14
  389.6 2.5 copy-start.21
  392.1 2.2 copy-start.19
Sparse Core Ops, SparseCore 0:
  10.2 73.0 all-gather.2
  94.3 50.3 all-gather.4

commit v3 on v2

v3 whole, which is shorter than its diff:
```python
import functools

import jax
import jax.numpy as jnp
from jax import lax
from jax.experimental import pallas as pl
from jax.experimental.pallas import tpu as pltpu
from jax.sharding import PartitionSpec as P

BF16 = jnp.bfloat16
F32 = jnp.float32
STEP = 16
CHUNKS = 2
PARAMS = pltpu.CompilerParams(vmem_limit_bytes=56 * 1024 * 1024)


def cost(flops, *arrays):
    return pl.CostEstimate(
        flops=flops,
        bytes_accessed=sum(a.size * a.dtype.itemsize for a in arrays),
        transcendentals=0,
    )


def store_lines(turned, out, parts, chunk):
    levels, width = turned.shape[1:]
    part, piece = width // parts, out.shape[2]
    for l in range(levels):
        for s in range(parts):
            at = s * part + chunk * piece
            out[l * parts + s] = turned[:, l, at : at + piece].astype(BF16)


def lines_body(parts, chunk, block, out, turned):
    turned[...] = block[...].astype(F32)
    store_lines(turned, out, parts, chunk)


def as_lines(block, parts, chunk):
    rows, levels, width = block.shape
    shape = (levels * parts, rows, width // parts // CHUNKS)
    return pl.pallas_call(
        functools.partial(lines_body, parts, chunk),
        grid=(rows // STEP,),
        in_specs=[pl.BlockSpec((STEP, levels, width), lambda i: (i, 0, 0))],
        out_specs=pl.BlockSpec((shape[0], STEP, shape[2]), lambda i: (0, i, 0)),
        out_shape=jax.ShapeDtypeStruct(shape, BF16),
        scratch_shapes=[pltpu.VMEM((STEP, levels, width), F32)],
        compiler_params=PARAMS,
        cost_estimate=cost(0, block, block),
        name="as_lines",
    )(block)


def gradient_body(parts, lines, control, *rest):
    out, turned = rest[-2:]
    levels, width = control.shape[1:]
    part = width // parts
    for l in range(levels):
        for s in range(parts):
            turned[:, l, s * part : (s + 1) * part] = lines[l * parts + s].astype(F32)
    out[...] = control[...].astype(F32) + turned[...]


def add_lines(control, lines, parts, chunk, target):
    rows, levels, width = control.shape
    whole = (STEP, levels, width)
    cut = rows // CHUNKS
    offset = chunk * cut // STEP
    operands = [lines, control] + ([] if target is None else [target])
    return pl.pallas_call(
        functools.partial(gradient_body, parts),
        grid=(cut // STEP,),
        in_specs=[
            pl.BlockSpec((lines.shape[0], STEP, lines.shape[2]), lambda i: (0, i, 0)),
            pl.BlockSpec(whole, lambda i: (i + offset, 0, 0)),
        ]
        + [pl.BlockSpec(memory_space=pl.ANY)] * (len(operands) - 2),
        out_specs=pl.BlockSpec(whole, lambda i: (i + offset, 0, 0)),
        out_shape=jax.ShapeDtypeStruct(control.shape, F32),
        input_output_aliases={} if target is None else {2: 0},
        scratch_shapes=[pltpu.VMEM(whole, F32)],
        compiler_params=PARAMS,
        cost_estimate=cost(control.size // 2, control, control),
        name="add_lines",
    )(*operands)


def forward_body(*refs):
    starts = refs[:CHUNKS]
    rows_in, sides, innovation, weight, wind_x, wind_y = refs[CHUNKS : CHUNKS + 6]
    end, flat, row_flux, side_flux, state, carry = refs[CHUNKS + 6 :]
    step = pl.program_id(0)
    rows, levels, width = flat.shape
    cut = rows // CHUNKS

    @pl.when(step == 0)
    def _():
        state[pl.ds(0, 1)] = rows_in[pl.ds(0, 1)]
        state[pl.ds(rows + 1, 1)] = rows_in[pl.ds(1, 1)]
        for h in range(CHUNKS):
            state[pl.ds(1 + h * cut, cut)] = starts[h][...].astype(F32)
        carry[...] = jnp.zeros(carry.shape, F32)

    first = step * STEP
    place = lax.broadcasted_iota(jnp.int32, (levels, width), 1)
    left_edge, right_edge = place == 0, place == width - 1
    q_old, q_last, pending = carry[0], carry[1], carry[2]
    up, here = state[first], state[first + 1]
    for j in range(STEP):
        down = state[first + j + 2]
        cx, cy = wind_x[j], wind_y[j]
        left = jnp.where(left_edge, sides[j, :, 0:1], pltpu.roll(here, 1, 1))
        right = jnp.where(right_edge, sides[j, :, 1:2], pltpu.roll(here, width - 1, 1))
        after = here - cx * (down - up) * 0.5 - cy * (right - left) * 0.5
        end[j] = after
        misfit = weight[j] * (after - innovation[j])
        p, q = cy * misfit, cx * misfit
        side_flux[j, :, 0:1] = p[:, 0:1]
        side_flux[j, :, 1:2] = p[:, width - 1 : width]
        at = first + j - 1 if j > 0 else jnp.maximum(first - 1, 0)
        flat[at] = pending + 0.5 * (q - q_old)
        left = jnp.where(left_edge, 0.0, pltpu.roll(p, 1, 1))
        right = jnp.where(right_edge, 0.0, pltpu.roll(p, width - 1, 1))
        pending = misfit + 0.5 * (right - left)
        q_old, q_last = q_last, q
        up, here = here, down
        if j == 0:

            @pl.when(step == 0)
            def _(q=q):
                row_flux[0] = q

    carry[0], carry[1], carry[2] = q_old, q_last, pending

    @pl.when(step == rows // STEP - 1)
    def _():
        flat[rows - 1] = pending - 0.5 * q_old
        row_flux[1] = q_last


def forward(starts, rows_in, sides, innovation, weight, wind_x, wind_y):
    rows, levels, width = innovation.shape
    blocked = pl.BlockSpec((STEP, levels, width), lambda i: (i, 0, 0))
    side = pl.BlockSpec((STEP, levels, 2), lambda i: (i, 0, 0))
    pair = pl.BlockSpec((2, levels, width), lambda i: (0, 0, 0))
    start = pl.BlockSpec(starts[0].shape, lambda i: (0, 0, 0))
    whole = pl.BlockSpec((rows, levels, width), lambda i: (0, 0, 0))
    return pl.pallas_call(
        forward_body,
        grid=(rows // STEP,),
        in_specs=[start] * CHUNKS + [pair, side, blocked, blocked, blocked, blocked],
        out_specs=[blocked, whole, pair, side],
        out_shape=[
            jax.ShapeDtypeStruct((rows, levels, width), F32),
            jax.ShapeDtypeStruct((rows, levels, width), F32),
            jax.ShapeDtypeStruct((2, levels, width), F32),
            jax.ShapeDtypeStruct((rows, levels, 2), F32),
        ],
        scratch_shapes=[
            pltpu.VMEM((rows + 2, levels, width), F32),
            pltpu.VMEM((3, levels, width), F32),
        ],
        compiler_params=PARAMS,
        cost_estimate=cost(30 * innovation.size, *[innovation] * 7),
        name="forward",
    )(*starts, rows_in, sides, innovation, weight, wind_x, wind_y)


def rim_body(parts, chunk, last, flat, rows_in, sides, out, turned):
    step = pl.program_id(0)
    width = flat.shape[2]
    place = lax.broadcasted_iota(jnp.int32, flat.shape, 2)
    value = flat[...]
    value = value - jnp.where(place == 0, 0.5 * sides[:, :, 0:1], 0.0)
    value = value + jnp.where(place == width - 1, 0.5 * sides[:, :, 1:2], 0.0)
    turned[...] = value

    @pl.when(step == 0)
    def _():
        turned[pl.ds(0, 1)] += -0.5 * rows_in[pl.ds(0, 1)]

    @pl.when(step == last)
    def _():
        turned[pl.ds(STEP - 1, 1)] += 0.5 * rows_in[pl.ds(1, 1)]

    store_lines(turned, out, parts, chunk)


def rim_lines(flat, rows_in, sides, parts, chunk):
    rows, levels, width = flat.shape
    shape = (levels * parts, rows, width // parts // CHUNKS)
    return pl.pallas_call(
        functools.partial(rim_body, parts, chunk, rows // STEP - 1),
        grid=(rows // STEP,),
        in_specs=[
            pl.BlockSpec((STEP, levels, width), lambda i: (i, 0, 0)),
            pl.BlockSpec((2, levels, width), lambda i: (0, 0, 0)),
            pl.BlockSpec((STEP, levels, 2), lambda i: (i, 0, 0)),
        ],
        out_specs=pl.BlockSpec((shape[0], STEP, shape[2]), lambda i: (0, i, 0)),
        out_shape=jax.ShapeDtypeStruct(shape, BF16),
        scratch_shapes=[pltpu.VMEM((STEP, levels, width), F32)],
        compiler_params=PARAMS,
        cost_estimate=cost(4 * flat.size, flat, flat),
        name="rim_lines",
    )(flat, rows_in, sides)


def swap_all(lines):
    return lax.all_to_all(lines, "gx", 0, 0, tiled=True)


def plane_pieces(lines, parts):
    n_x, n_y = lax.axis_size("gx"), lax.axis_size("gy")
    groups = [list(range(i, i + parts)) for i in range(0, n_x, parts)]
    if n_y == 2 and parts == 2:
        pairs = [(a, b) for g in groups for a, b in (g, g[::-1])]
        far = lax.ppermute(lines, "gy", [(0, 1), (1, 0)])
        near = lax.ppermute(lines, "gx", pairs)
        cross = lax.ppermute(far, "gx", pairs)
        return [lines, near, far, cross]
    plane = lax.all_gather(lines, "gy", axis=0, tiled=False)
    plane = lax.all_gather(plane, "gx", axis=0, tiled=False, axis_index_groups=groups)
    return [plane[s, g] for s in range(parts) for g in range(n_y)]


def piece_order(parts):
    n_y = lax.axis_size("gy")
    sub, me = lax.rem(lax.axis_index("gx"), parts), lax.axis_index("gy")
    if n_y == 2 and parts == 2:
        return [(sub, me), (1 - sub, me), (sub, 1 - me), (1 - sub, 1 - me)]
    return [(s, g) for s in range(parts) for g in range(n_y)]


def filter_rows(filter_y, parts):
    width = filter_y.shape[0]
    part = width // parts
    sub = lax.rem(lax.axis_index("gx"), parts)
    return [
        lax.dynamic_slice(filter_y, (sub * part, g * width + s * part), (part, part))
        for s, g in piece_order(parts)
    ]


def filter_columns(filter_y, parts):
    width, n_y = filter_y.shape[0], lax.axis_size("gy")
    part = width // parts
    sub, me = lax.rem(lax.axis_index("gx"), parts), lax.axis_index("gy")
    order = piece_order(parts)
    if n_y == 2 and parts == 2:
        mine = lax.dynamic_slice(filter_y, (0, me * width + sub * part), (width, part))
        sent = lax.dynamic_slice(
            filter_y, (0, (1 - me) * width + sub * part), (width, part)
        )
        got = lax.ppermute(sent, "gy", [(0, 1), (1, 0)])
        return [
            lax.dynamic_slice_in_dim(source, s * part, part, axis=0)
            for source, (s, _) in zip((mine, mine, got, got), order)
        ]
    split = filter_y.reshape(width, n_y, parts, part)
    split = lax.dynamic_index_in_dim(split, sub, axis=2, keepdims=False)
    split = lax.all_to_all(split, "gy", 1, 0, tiled=True)
    split = split.reshape(n_y, parts, part, part)
    return [split[g, s] for s, g in order]


def row_halo(first, last):
    n_x = lax.axis_size("gx")
    up = [(i, i + 1) for i in range(n_x - 1)]
    down = [(i + 1, i) for i in range(n_x - 1)]
    return jnp.stack([lax.ppermute(last, "gx", up), lax.ppermute(first, "gx", down)])


def side_halo(first, last):
    n_y, me = lax.axis_size("gy"), lax.axis_index("gy")
    if n_y == 2:
        got = lax.ppermute(jnp.where(me == 0, last, first), "gy", [(0, 1), (1, 0)])
        none = jnp.zeros_like(got)
        return jnp.where(me == 0, none, got), jnp.where(me == 0, got, none)
    up = [(i, i + 1) for i in range(n_y - 1)]
    down = [(i + 1, i) for i in range(n_y - 1)]
    return lax.ppermute(last, "gy", up), lax.ppermute(first, "gy", down)


def per_device(control, innovation, obs_weight, courant_x, courant_y, filter_x, filter_y):
    rows, levels, width = control.shape
    n_x = lax.axis_size("gx")
    parts = n_x // levels
    part = width // parts
    cut, piece = rows // CHUNKS, part // CHUNKS
    spans = [slice(w * piece, (w + 1) * piece) for w in range(CHUNKS)]

    rows_y = filter_rows(filter_y, parts)
    matrix_x = [lax.all_gather(filter_x[:cut], "gx", axis=0, tiled=True)]
    lines = [swap_all(as_lines(control, parts, w)) for w in range(CHUNKS)]
    lines = [l.reshape(n_x * rows, piece) for l in lines]
    lines[-1], filter_x = lax.optimization_barrier((lines[-1], filter_x))
    for h in range(1, CHUNKS):
        share = filter_x[h * cut : (h + 1) * cut]
        matrix_x.append(lax.all_gather(share, "gx", axis=0, tiled=True))
    starts = []
    for h in range(CHUNKS):
        start = 0.0
        for w, span in enumerate(spans):
            smoothed = jnp.dot(matrix_x[h], lines[w], preferred_element_type=F32)
            smoothed = smoothed.astype(BF16).reshape(n_x, cut, piece)
            for plane, matrix in zip(plane_pieces(smoothed, parts), rows_y):
                start = start + jnp.einsum(
                    "brc,kc->brk", plane, matrix[:, span], preferred_element_type=F32
                )
        came = swap_all(start.astype(BF16)).reshape(levels, parts, cut, part)
        came = came.transpose(2, 0, 1, 3).reshape(cut, levels, width)
        if h == 0:
            came, filter_y = lax.optimization_barrier((came, filter_y))
            columns_y = filter_columns(filter_y, parts)
        starts.append(came)

    rows_in = row_halo(starts[0][0], starts[-1][-1]).astype(F32)
    before, after = side_halo(
        jnp.concatenate([s[:, :, 0] for s in starts]),
        jnp.concatenate([s[:, :, -1] for s in starts]),
    )
    sides = jnp.stack([before, after], axis=2).astype(F32)
    end_state, flat, row_flux, side_flux = forward(
        starts, rows_in, sides, innovation, obs_weight, courant_x, courant_y
    )
    rows_in = row_halo(row_flux[0], row_flux[1])
    before, after = side_halo(side_flux[:, :, 0], side_flux[:, :, 1])
    sides = jnp.stack([before, after], axis=2)
    flat, columns_y = lax.optimization_barrier((flat, columns_y))

    pulled = []
    for w in range(CHUNKS):
        adjoint = swap_all(rim_lines(flat, rows_in, sides, parts, w))
        adjoint = adjoint.reshape(n_x, CHUNKS, cut, piece)
        total = 0.0
        for h in range(CHUNKS):
            total = total + jnp.einsum(
                "ij,ic->jc",
                matrix_x[h],
                adjoint[:, h].reshape(n_x * cut, piece),
                preferred_element_type=F32,
            )
        pulled.append(total.astype(BF16).reshape(n_x, CHUNKS, cut, piece))
    gradient = None
    for h in range(CHUNKS):
        carried = 0.0
        for w, span in enumerate(spans):
            for plane, matrix in zip(plane_pieces(pulled[w][:, h], parts), columns_y):
                carried = carried + jnp.einsum(
                    "brk,kc->brc", plane, matrix[span], preferred_element_type=F32
                )
        carried = swap_all(carried.astype(BF16))
        gradient = add_lines(control, carried, parts, h, gradient)
    return (end_state, gradient)


def solution(mesh):
    placed = (
        P("gx", None, "gy"),
        P("gx", None, "gy"),
        P("gx", None, "gy"),
        P("gx", None, "gy"),
        P("gx", None, "gy"),
        P("gx", None),
        P("gy", None),
    )
    return jax.shard_map(
        per_device,
        mesh=mesh,
        in_specs=placed,
        out_specs=(P("gx", None, "gy"), P("gx", None, "gy")),
        check_vma=False,
    )
```

time: 458 us -> 438 us (0.956)
  blocking collectives: 107 us -> 48.4 us
  starting transfers between devices: 50.5 us -> 73.1 us
  Pallas kernels: 45.9 us -> 55.4 us
    all_to_all x2 -> x1, blocking collectives: 107 us -> 48.4 us  [swap_all(): return lax.all_to_all(lines, 'gx', 0, 0, tiled=True)]
    all_to_all x5 -> x7, starting transfers between devices: 26 us -> 39.9 us  [swap_all(): return lax.all_to_all(lines, 'gx', 0, 0, tiled=True)]
    all_to_all x5 -> x7, waiting for transfers between devices: 82.1 us -> 92.7 us  [swap_all(): return lax.all_to_all(lines, 'gx', 0, 0, tiled=True)]
    pallas_call x5 -> x7, Pallas kernels: 45.9 us -> 55.4 us  [the longest x1 19.4 us: forward(): pl.pallas_call(forward_body, grid=(rows // STEP,), in_specs=[start] * CHU...]
    reshape x0 -> x3, local copies, waits for them, and re-layouts: none -> 5.64 us  [the longest x2 3.86 us: per_device(): came = swap_all(start.astype(BF16)).reshape(levels, parts, cut, part)]
    ppermute x4 -> x8, waiting for transfers between devices: 53.9 us -> 50.1 us  [plane_pieces(): far = lax.ppermute(lines, 'gy', [(0, 1), (1, 0)])]
    dot_general x30 -> x40, matrix products: 52.6 us -> 52.5 us  [the longest x16 16.5 us: per_device(): jnp.einsum('brk,kc->brc', plane, matrix[span], preferred_element_type=F32)]
  transfers between devices with their start and end apart: 26 -> 40, of which waited for: 10 -> 14; matrix products, arithmetic and copies ran while one was open for 14% -> 17% of each run, Pallas kernels for 3% -> 6%
where the time goes in v3:
time: 438 us; the launch traced here: 436 us
  waiting for transfers between devices  162 us (37%)
  starting transfers between devices  73.1 us (17%)
  Pallas kernels  55.4 us (13%)
  matrix products  52.5 us (12%)
  blocking collectives  48.4 us (11%)
  local copies, waits for them, and re-layouts  26.4 us (6%)
  between operations  14.7 us (3%)
    all_to_all x7, waiting for transfers between devices, swap_all(): return lax.all_to_all(lines, 'gx', 0, 0, tiled=True)  92.7 us
    ppermute x8, waiting for transfers between devices, plane_pieces(): far = lax.ppermute(lines, 'gy', [(0, 1), (1, 0)])  50.1 us
    all_to_all x1, blocking collectives, swap_all(): return lax.all_to_all(lines, 'gx', 0, 0, tiled=True)  48.4 us
    all_to_all x7, starting transfers between devices, swap_all(): return lax.all_to_all(lines, 'gx', 0, 0, tiled=True)  39.9 us
    pallas_call x1, Pallas kernels, forward(): pl.pallas_call(forward_body, grid=(rows // STEP,), in_specs=[start] * CHU...  19.4 us
    ppermute x1, waiting for transfers between devices, filter_columns(): got = lax.ppermute(sent, 'gy', [(0, 1), (1, 0)])  18.6 us
    dot_general x16, matrix products, per_device(): jnp.einsum('brk,kc->brc', plane, matrix[span], preferred_element_type=F32)  16.5 us
    pallas_call x2, Pallas kernels, rim_lines(): pl.pallas_call(functools.partial(rim_body, parts, chunk, rows // STEP - 1...  14.9 us
  transfers between devices with their start and end apart: 40, of which 14 were waited for; matrix products, arithmetic and copies ran while one was open for 17% of the time, Pallas kernels for 6%

profile of v3, /device:TPU:9, one launch (start us, length us, event | category | flops | bytes accessed | tf_op | source)
XLA Modules:
  0.0 435.5 jit_solution(14862539556729851507)
XLA Ops:
  9.0 6.5 %as_lines.3 = bf16[16,128,256]{2,1,0:T(8,128)(2,1)} custom-call(bf16[128,8,1024]{2,1,0:T(8,128)(2,1)} %control.3), custom_call_target="tpu_custom_call" | custom-call | bytes 4194304 | tf_op jit(solution)/shard_map/as_lines/pallas_call | solution.py:42
  15.4 48.4 %all_to_all.40 = bf16[16,128,256]{2,1,0:T(8,128)(2,1)S(1)} all-to-all(bf16[16,128,256]{2,1,0:T(8,128)(2,1)} %as_lines.3), channel_id=1, replica_groups=mesh['gx'=16,'gy'=2] {'gx'}, dimensions={0} | all-to-all | bytes 2097152 | tf_op jit(solution)/shard_map/all_to_all | solution.py:211
  64.6 6.5 %as_lines.2 = bf16[16,128,256]{2,1,0:T(8,128)(2,1)} custom-call(bf16[128,8,1024]{2,1,0:T(8,128)(2,1)} %control.3), custom_call_target="tpu_custom_call" | custom-call | bytes 4194304 | tf_op jit(solution)/shard_map/as_lines/pallas_call | solution.py:42
  71.0 6.2 %all-to-all-start = ((bf16[16,128,256]{2,1,0:T(8,128)(2,1)}), bf16[16,128,256]{2,1,0:T(8,128)(2,1)S(1)}, u32[]{:S(2)}, u32[]{:S(2)}) async-start(bf16[16,128,256]{2,1,0:T(8,128)(2,1)} %as_lines.2), calls=%async_computation | async-start | bytes 2097152 | tf_op jit(solution)/shard_map/all_to_all | solution.py:211
  77.3 3.5 fusion.4
  82.8 27.8 %all-to-all-done = bf16[16,128,256]{2,1,0:T(8,128)(2,1)S(1)} async-done(((bf16[16,128,256]{2,1,0:T(8,128)(2,1)}), bf16[16,128,256]{2,1,0:T(8,128)(2,1)S(1)}, u32[]{:S(2)}, u32[]{:S(2)}) %all-to-all-start) | async-done | bytes 1048608 | tf_op jit(solution)/shard_map/all_to_all | solution.py:211
  110.6 4.3 convolution_convert_fusion.3
  117.2 11.5 %collective-permute-done.1 = bf16[16,64,256]{2,1,0:T(8,128)(2,1)S(1)} collective-permute-done((bf16[16,64,256]{2,1,0:T(8,128)(2,1)S(1)}, bf16[16,64,256]{2,1,0:T(8,128)(2,1)S(1)}, u32[]{:S(2)}, u32[]{:S(2)}) %collective-permute-start.1) | collective-permute-done | bytes 524320 | tf_op jit(solution)/shard_map/ppermute | solution.py:219
  132.9 1.9 add_convert_fusion.3
  134.8 5.0 %all-to-all-start.2 = ((bf16[16,64,512]{2,1,0:T(8,128)(2,1)}), bf16[16,64,512]{2,1,0:T(8,128)(2,1)S(1)}, u32[]{:S(2)}, u32[]{:S(2)}) async-start(bf16[16,64,512]{2,1,0:T(8,128)(2,1)} %add_convert_fusion.3), calls=%async_computation.2 | async-start | bytes 2097152 | tf_op jit(solution)/shard_map/all_to_all | solution.py:211
  139.8 3.6 convolution_convert_fusion
  148.1 8.5 %collective-permute-done.10 = bf16[16,64,256]{2,1,0:T(8,128)(2,1)S(1)} collective-permute-done((bf16[16,64,256]{2,1,0:T(8,128)(2,1)S(1)}, bf16[16,64,256]{2,1,0:T(8,128)(2,1)S(1)}, u32[]{:S(2)}, u32[]{:S(2)}) %collective-permute-start.10) | collective-permute-done | bytes 524320 | tf_op jit(solution)/shard_map/ppermute | solution.py:219
  157.1 2.0 collective-permute-start.11
  159.1 8.7 %collective-permute-done.7 = bf16[16,64,256]{2,1,0:T(8,128)(2,1)S(1)} collective-permute-done((bf16[16,64,256]{2,1,0:T(8,128)(2,1)S(1)}, bf16[16,64,256]{2,1,0:T(8,128)(2,1)S(1)}, u32[]{:S(2)}, u32[]{:S(2)}) %collective-permute-start.7) | collective-permute-done | bytes 524320 | tf_op jit(solution)/shard_map/ppermute | solution.py:219
  171.0 1.9 add_convert_fusion.2
  172.9 6.0 %all-to-all-start.3 = ((bf16[16,64,512]{2,1,0:T(8,128)(2,1)}), bf16[16,64,512]{2,1,0:T(8,128)(2,1)}, u32[]{:S(2)}, u32[]{:S(2)}) async-start(bf16[16,64,512]{2,1,0:T(8,128)(2,1)} %add_convert_fusion.2), calls=%async_computation.3 | async-start | bytes 2097152 | tf_op jit(solution)/shard_map/all_to_all | solution.py:211
  182.3 2.5 collective-permute-start.13
  185.3 1.9 fusion.65
  187.2 18.6 %collective-permute-done.15 = bf16[1024,512]{1,0:T(8,128)(2,1)} collective-permute-done((bf16[1024,512]{1,0:T(8,128)(2,1)S(1)}, bf16[1024,512]{1,0:T(8,128)(2,1)}, u32[]{:S(2)}, u32[]{:S(2)}) %collective-permute-start.15) | collective-permute-done | bytes 1048608 | tf_op jit(solution)/shard_map/ppermute | solution.py:256
  205.7 2.1 constant_dynamic-slice_fusion
  207.9 3.3 copy.288
  211.1 1.8 reshape.59.refs_1_
  215.2 4.4 %collective-permute-start.12 = (bf16[8,1024]{1,0:T(8,128)(2,1)S(1)}, bf16[8,1024]{1,0:T(8,128)(2,1)S(1)}, u32[]{:S(2)}, u32[]{:S(2)}) collective-permute-start(bf16[8,1024]{1,0:T(8,128)(2,1)S(1)} %bitcast.234), channel_id=1, source_target_pairs={{0,2},{2,4},{4,6},{6,8},{8,10},{10,12},{12,14},{14,16},{16,18},{18... | collective-permute-start | bytes 49160 | tf_op jit(solution)/shard_map/ppermute | solution.py:272
  221.4 19.4 %forward.1 = (f32[128,8,1024]{2,1,0:T(8,128)}, f32[128,8,1024]{2,1,0:T(8,128)}, f32[2,8,1024]{2,1,0:T(8,128)}, f32[128,8,2]{2,1,0:T(8,128)}) custom-call(bf16[64,8,1024]{2,1,0:T(8,128)(2,1)} %bitcast.207, bf16[64,8,1024]{2,1,0:T(8,128)(2,1)} %copy-done.5, f32[2,8,1024]{2,1,0:T(8,128)} %maximum_convert_fusion.refs_2_, f32[128,8,2]{2,1,0:T(8,128)} %copy.268.refs_3_, ...), custom_call_target="tpu_custom_call" | custom-call | flops 31457280 | bytes 29360128 | tf_op jit(solution)/shard_map/forward/pallas_call | solution.py:149
  242.9 4.1 collective-permute-start.17
  247.0 2.1 collective-permute-start.16
  250.8 7.4 %rim_lines.3 = bf16[16,128,256]{2,1,0:T(8,128)(2,1)} custom-call(f32[128,8,1024]{2,1,0:T(8,128)} %get-tuple-element.21.flat, f32[2,8,1024]{2,1,0:T(8,128)} %pad_maximum_fusion.rows_in, f32[128,8,2]{2,1,0:T(8,128)} %copy.270.sides), custom_call_target="tpu_custom_call" | custom-call | flops 4194304 | bytes 8388608 | tf_op jit(solution)/shard_map/rim_lines/pallas_call | solution.py:193
  258.2 7.7 %all-to-all-start.5 = ((bf16[16,128,256]{2,1,0:T(8,128)(2,1)}), bf16[16,128,256]{2,1,0:T(8,128)(2,1)S(1)}, u32[]{:S(2)}, u32[]{:S(2)}) async-start(bf16[16,128,256]{2,1,0:T(8,128)(2,1)} %rim_lines.3), calls=%async_computation.5 | async-start | bytes 2097152 | tf_op jit(solution)/shard_map/all_to_all | solution.py:211
  265.9 7.4 %rim_lines.2 = bf16[16,128,256]{2,1,0:T(8,128)(2,1)} custom-call(f32[128,8,1024]{2,1,0:T(8,128)} %get-tuple-element.21.flat, f32[2,8,1024]{2,1,0:T(8,128)} %pad_maximum_fusion.rows_in, f32[128,8,2]{2,1,0:T(8,128)} %copy.270.sides), custom_call_target="tpu_custom_call" | custom-call | flops 4194304 | bytes 8388608 | tf_op jit(solution)/shard_map/rim_lines/pallas_call | solution.py:193
  273.4 17.4 %all-to-all-done.5 = bf16[16,128,256]{2,1,0:T(8,128)(2,1)S(1)} async-done(((bf16[16,128,256]{2,1,0:T(8,128)(2,1)}), bf16[16,128,256]{2,1,0:T(8,128)(2,1)S(1)}, u32[]{:S(2)}, u32[]{:S(2)}) %all-to-all-start.5) | async-done | bytes 1048608 | tf_op jit(solution)/shard_map/all_to_all | solution.py:211
  290.8 5.0 %all-to-all-start.4 = ((bf16[16,128,256]{2,1,0:T(8,128)(2,1)}), bf16[16,128,256]{2,1,0:T(8,128)(2,1)}, u32[]{:S(2)}, u32[]{:S(2)}) async-start(bf16[16,128,256]{2,1,0:T(8,128)(2,1)} %rim_lines.2), calls=%async_computation.4 | async-start | bytes 2097152 | tf_op jit(solution)/shard_map/all_to_all | solution.py:211
  295.9 3.6 fusion.71
  299.5 2.3 fusion.2
  306.0 1.7 fusion.17
  307.7 13.0 %all-to-all-done.4 = bf16[16,128,256]{2,1,0:T(8,128)(2,1)} async-done(((bf16[16,128,256]{2,1,0:T(8,128)(2,1)}), bf16[16,128,256]{2,1,0:T(8,128)(2,1)}, u32[]{:S(2)}, u32[]{:S(2)}) %all-to-all-start.4) | async-done | bytes 1048608 | tf_op jit(solution)/shard_map/all_to_all | solution.py:211
  322.0 3.6 fusion.70
  325.6 2.3 fusion.3
  330.5 1.7 fusion.33
  334.6 11.4 %collective-permute-done.29 = bf16[16,64,256]{2,1,0:T(8,128)(2,1)S(1)} collective-permute-done((bf16[16,64,256]{2,1,0:T(8,128)(2,1)S(1)}, bf16[16,64,256]{2,1,0:T(8,128)(2,1)S(1)}, u32[]{:S(2)}, u32[]{:S(2)}) %collective-permute-start.29) | collective-permute-done | bytes 524320 | tf_op jit(solution)/shard_map/ppermute | solution.py:219
  347.2 10.0 %collective-permute-done.26 = bf16[16,64,256]{2,1,0:T(8,128)(2,1)S(1)} collective-permute-done((bf16[16,64,256]{2,1,0:T(8,128)(2,1)S(1)}, bf16[16,64,256]{2,1,0:T(8,128)(2,1)S(1)}, u32[]{:S(2)}, u32[]{:S(2)}) %collective-permute-start.26) | collective-permute-done | bytes 524320 | tf_op jit(solution)/shard_map/ppermute | solution.py:219
  362.1 1.8 add_convert_fusion
  363.9 5.0 %all-to-all-start.7 = ((bf16[16,64,512]{2,1,0:T(8,128)(2,1)}), bf16[16,64,512]{2,1,0:T(8,128)(2,1)S(1)}, u32[]{:S(2)}, u32[]{:S(2)}) async-start(bf16[16,64,512]{2,1,0:T(8,128)(2,1)} %add_convert_fusion), calls=%async_computation.7 | async-start | bytes 2097152 | tf_op jit(solution)/shard_map/all_to_all | solution.py:211
  378.1 1.8 add_convert_fusion.1
  379.9 13.8 %all-to-all-done.7.lines = bf16[16,64,512]{2,1,0:T(8,128)(2,1)S(1)} async-done(((bf16[16,64,512]{2,1,0:T(8,128)(2,1)}), bf16[16,64,512]{2,1,0:T(8,128)(2,1)S(1)}, u32[]{:S(2)}, u32[]{:S(2)}) %all-to-all-start.7) | async-done | bytes 1048608 | tf_op jit(solution)/shard_map/all_to_all | solution.py:211
  393.7 5.0 %all-to-all-start.6 = ((bf16[16,64,512]{2,1,0:T(8,128)(2,1)}), bf16[16,64,512]{2,1,0:T(8,128)(2,1)S(1)}, u32[]{:S(2)}, u32[]{:S(2)}) async-start(bf16[16,64,512]{2,1,0:T(8,128)(2,1)} %add_convert_fusion.1), calls=%async_computation.6 | async-start | bytes 2097152 | tf_op jit(solution)/shard_map/all_to_all | solution.py:211
  398.7 4.1 add_lines.2.rest_0_
  402.8 20.7 %all-to-all-done.6.lines = bf16[16,64,512]{2,1,0:T(8,128)(2,1)S(1)} async-done(((bf16[16,64,512]{2,1,0:T(8,128)(2,1)}), bf16[16,64,512]{2,1,0:T(8,128)(2,1)S(1)}, u32[]{:S(2)}, u32[]{:S(2)}) %all-to-all-start.6) | async-done | bytes 1048608 | tf_op jit(solution)/shard_map/all_to_all | solution.py:211
  424.6 4.1 add_lines.3
  (156 shorter events, 57.6 us)
Async XLA Ops:
  7.2 70.1 %all-gather.3.cloned.1.call-start = ((), (), s32[]{:S(2)}) async-start(), calls=%async_computation.8 | async-start | bytes 4456448 | tf_op jit(solution)/shard_map/all_gather | solution.py:295
  8.9 54.9 %copy-start.13 = (bf16[128,2048]{1,0:T(8,128)(2,1)S(1)}, bf16[128,2048]{1,0:T(8,128)(2,1)}, u32[]{:S(2)}) copy-start(bf16[128,2048]{1,0:T(8,128)(2,1)} %param.12) | copy-start | bytes 1572868
  8.9 130.8 %all-gather.5.cloned.1.call-start = ((), (), s32[]{:S(2)}) async-start(), calls=%async_computation.9 | async-start | bytes 4456448 | tf_op jit(solution)/shard_map/all_gather | solution.py:301
  71.0 39.5 %all-to-all-start = ((bf16[16,128,256]{2,1,0:T(8,128)(2,1)}), bf16[16,128,256]{2,1,0:T(8,128)(2,1)S(1)}, u32[]{:S(2)}, u32[]{:S(2)}) async-start(bf16[16,128,256]{2,1,0:T(8,128)(2,1)} %as_lines.2), calls=%async_computation | async-start | bytes 2097152 | tf_op jit(solution)/shard_map/all_to_all | solution.py:211
  81.0 48.4 %collective-permute-start.4 = (bf16[16,64,256]{2,1,0:T(8,128)(2,1)S(1)}, bf16[16,64,256]{2,1,0:T(8,128)(2,1)S(1)}, u32[]{:S(2)}, u32[]{:S(2)}) collective-permute-start(bf16[16,64,256]{2,1,0:T(8,128)(2,1)S(1)} %bitcast.212), channel_id=1, source_target_pairs={{0,1},{1,0},{2,3},{3,2},{4,5},{5,4},{6,7},{7,6},{8,9},{9,8},{10,11... | collective-permute-start | bytes 1572872 | tf_op jit(solution)/shard_map/ppermute | solution.py:219
  82.2 48.6 %collective-permute-start.3 = (bf16[16,64,256]{2,1,0:T(8,128)(2,1)S(1)}, bf16[16,64,256]{2,1,0:T(8,128)(2,1)}, u32[]{:S(2)}, u32[]{:S(2)}) collective-permute-start(bf16[16,64,256]{2,1,0:T(8,128)(2,1)S(1)} %bitcast.213), channel_id=1, source_target_pairs={{0,2},{2,0},{4,6},{6,4},{8,10},{10,8},{12,14},{14,12},{16,18},{18,... | collective-permute-start | bytes 1572872 | tf_op jit(solution)/shard_map/ppermute | solution.py:220
  110.6 5.6 %copy-start = (bf16[1024,2048]{1,0:T(8,128)(2,1)S(1)}, bf16[1024,2048]{1,0:T(8,128)(2,1)}, u32[]{:S(2)}) copy-start(bf16[1024,2048]{1,0:T(8,128)(2,1)} %param.13) | copy-start | bytes 12582916
  114.9 13.8 %collective-permute-start.1 = (bf16[16,64,256]{2,1,0:T(8,128)(2,1)S(1)}, bf16[16,64,256]{2,1,0:T(8,128)(2,1)S(1)}, u32[]{:S(2)}, u32[]{:S(2)}) collective-permute-start(bf16[16,64,256]{2,1,0:T(8,128)(2,1)S(1)} %bitcast.225), channel_id=1, source_target_pairs={{0,1},{1,0},{2,3},{3,2},{4,5},{5,4},{6,7},{7,6},{8,9},{9,8},{10,11... | collective-permute-start | bytes 1572872 | tf_op jit(solution)/shard_map/ppermute | solution.py:219
  116.2 14.2 %collective-permute-start = (bf16[16,64,256]{2,1,0:T(8,128)(2,1)S(1)}, bf16[16,64,256]{2,1,0:T(8,128)(2,1)S(1)}, u32[]{:S(2)}, u32[]{:S(2)}) collective-permute-start(bf16[16,64,256]{2,1,0:T(8,128)(2,1)S(1)} %bitcast.226), channel_id=1, source_target_pairs={{0,2},{2,0},{4,6},{6,4},{8,10},{10,8},{12,14},{14,12},{16,18},{18,... | collective-permute-start | bytes 1572872 | tf_op jit(solution)/shard_map/ppermute | solution.py:220
  128.7 3.7 collective-permute-start.2
  129.4 3.5 collective-permute-start.5
  134.8 38.1 %all-to-all-start.2 = ((bf16[16,64,512]{2,1,0:T(8,128)(2,1)}), bf16[16,64,512]{2,1,0:T(8,128)(2,1)S(1)}, u32[]{:S(2)}, u32[]{:S(2)}) async-start(bf16[16,64,512]{2,1,0:T(8,128)(2,1)} %add_convert_fusion.3), calls=%async_computation.2 | async-start | bytes 2097152 | tf_op jit(solution)/shard_map/all_to_all | solution.py:211
  139.7 5.4 %copy-start.12 = (bf16[16,128,256]{2,1,0:T(8,128)(2,1)S(1)}, bf16[16,128,256]{2,1,0:T(8,128)(2,1)}, u32[]{:S(2)}) copy-start(bf16[16,128,256]{2,1,0:T(8,128)(2,1)} %copy-done.11) | copy-start | bytes 3145732
  139.7 5.4 %copy-start.18 = (bf16[1024,2048]{1,0:T(8,128)(2,1)S(1)}, bf16[1024,2048]{1,0:T(8,128)(2,1)}, u32[]{:S(2)}) copy-start(bf16[1024,2048]{1,0:T(8,128)(2,1)} %all-gather.5.cloned.1.call-done) | copy-start | bytes 12582916
  143.4 13.2 %collective-permute-start.10 = (bf16[16,64,256]{2,1,0:T(8,128)(2,1)S(1)}, bf16[16,64,256]{2,1,0:T(8,128)(2,1)S(1)}, u32[]{:S(2)}, u32[]{:S(2)}) collective-permute-start(bf16[16,64,256]{2,1,0:T(8,128)(2,1)S(1)} %bitcast.219), channel_id=1, source_target_pairs={{0,1},{1,0},{2,3},{3,2},{4,5},{5,4},{6,7},{7,6},{8,9},{9,8},{10,11... | collective-permute-start | bytes 1572872 | tf_op jit(solution)/shard_map/ppermute | solution.py:219
  144.5 25.0 %collective-permute-start.9 = (bf16[16,64,256]{2,1,0:T(8,128)(2,1)S(1)}, bf16[16,64,256]{2,1,0:T(8,128)(2,1)S(1)}, u32[]{:S(2)}, u32[]{:S(2)}) collective-permute-start(bf16[16,64,256]{2,1,0:T(8,128)(2,1)S(1)} %bitcast.220), channel_id=1, source_target_pairs={{0,2},{2,0},{4,6},{6,4},{8,10},{10,8},{12,14},{14,12},{16,18},{18,... | collective-permute-start | bytes 1572872 | tf_op jit(solution)/shard_map/ppermute | solution.py:220
  146.4 21.4 %collective-permute-start.7 = (bf16[16,64,256]{2,1,0:T(8,128)(2,1)S(1)}, bf16[16,64,256]{2,1,0:T(8,128)(2,1)S(1)}, u32[]{:S(2)}, u32[]{:S(2)}) collective-permute-start(bf16[16,64,256]{2,1,0:T(8,128)(2,1)S(1)} %bitcast.222), channel_id=1, source_target_pairs={{0,1},{1,0},{2,3},{3,2},{4,5},{5,4},{6,7},{7,6},{8,9},{9,8},{10,11... | collective-permute-start | bytes 1572872 | tf_op jit(solution)/shard_map/ppermute | solution.py:219
  146.9 23.1 %collective-permute-start.6 = (bf16[16,64,256]{2,1,0:T(8,128)(2,1)S(1)}, bf16[16,64,256]{2,1,0:T(8,128)(2,1)S(1)}, u32[]{:S(2)}, u32[]{:S(2)}) collective-permute-start(bf16[16,64,256]{2,1,0:T(8,128)(2,1)S(1)} %bitcast.223), channel_id=1, source_target_pairs={{0,2},{2,0},{4,6},{6,4},{8,10},{10,8},{12,14},{14,12},{16,18},{18,... | collective-permute-start | bytes 1572872 | tf_op jit(solution)/shard_map/ppermute | solution.py:220
  157.1 14.0 %collective-permute-start.11 = (bf16[16,64,256]{2,1,0:T(8,128)(2,1)S(1)}, bf16[16,64,256]{2,1,0:T(8,128)(2,1)S(1)}, u32[]{:S(2)}, u32[]{:S(2)}) collective-permute-start(bf16[16,64,256]{2,1,0:T(8,128)(2,1)S(1)} %collective-permute-done.10), channel_id=1, source_target_pairs={{0,2},{2,0},{4,6},{6,4},{8,10},{10,8},{12,14},{14,12},{16,18},{18,... | collective-permute-start | bytes 1572872 | tf_op jit(solution)/shard_map/ppermute | solution.py:221
  167.8 2.7 collective-permute-start.8
  172.9 35.0 %all-to-all-start.3 = ((bf16[16,64,512]{2,1,0:T(8,128)(2,1)}), bf16[16,64,512]{2,1,0:T(8,128)(2,1)}, u32[]{:S(2)}, u32[]{:S(2)}) async-start(bf16[16,64,512]{2,1,0:T(8,128)(2,1)} %add_convert_fusion.2), calls=%async_computation.3 | async-start | bytes 2097152 | tf_op jit(solution)/shard_map/all_to_all | solution.py:211
  179.5 7.7 %copy-start.4 = (bf16[8,2,64,512]{3,0,1,2:T(8,128)(2,1)}, bf16[8,2,64,512]{3,0,1,2:T(8,128)(2,1)S(1)}, u32[]{:S(2)}) copy-start(bf16[8,2,64,512]{3,0,1,2:T(8,128)(2,1)S(1)} %copy.262) | copy-start | bytes 3145732
  181.2 24.6 %collective-permute-start.15 = (bf16[1024,512]{1,0:T(8,128)(2,1)S(1)}, bf16[1024,512]{1,0:T(8,128)(2,1)}, u32[]{:S(2)}, u32[]{:S(2)}) collective-permute-start(bf16[1024,512]{1,0:T(8,128)(2,1)S(1)} %constant_dynamic-slice_fusion.2), channel_id=1, source_target_pairs={{0,1},{1,0},{2,3},{3,2},{4,5},{5,4},{6,7},{7,6},{8,9},{9,8},{10,11... | collective-permute-start | bytes 3145736 | tf_op jit(solution)/shard_map/ppermute | solution.py:256
  182.3 38.5 %collective-permute-start.13 = (bf16[8,1024]{1,0:T(8,128)(2,1)S(1)}, bf16[8,1024]{1,0:T(8,128)(2,1)S(1)}, u32[]{:S(2)}, u32[]{:S(2)}) collective-permute-start(bf16[8,1024]{1,0:T(8,128)(2,1)S(1)} %slice_bitcast_fusion.7), channel_id=1, source_target_pairs={{2,0},{4,2},{6,4},{8,6},{10,8},{12,10},{14,12},{16,14},{18,16},{20... | collective-permute-start | bytes 49160 | tf_op jit(solution)/shard_map/ppermute | solution.py:272
  187.2 118.8 %copy-start.7 = (bf16[512,512]{1,0:T(8,128)(2,1)}, bf16[512,512]{1,0:T(8,128)(2,1)S(1)}, u32[]{:S(2)}) copy-start(bf16[512,512]{1,0:T(8,128)(2,1)S(1)} %get-tuple-element.24) | copy-start | bytes 1572868
  212.9 8.5 %copy-start.5 = (bf16[64,8,1024]{2,1,0:T(8,128)(2,1)}, bf16[64,8,1024]{2,1,0:T(8,128)(2,1)S(1)}, u32[]{:S(2)}) copy-start(bf16[64,8,1024]{2,1,0:T(8,128)(2,1)S(1)} %reshape.59.refs_1_) | copy-start | bytes 3145732
  213.4 6.3 %collective-permute-start.14 = (bf16[128,8]{0,1:T(8,128)(2,1)S(1)}, bf16[128,8]{0,1:T(8,128)(2,1)S(1)}, u32[]{:S(2)}, u32[]{:S(2)}) collective-permute-start(bf16[128,8]{0,1:T(8,128)(2,1)S(1)} %maximum_select_fusion), channel_id=1, source_target_pairs={{0,1},{1,0},{2,3},{3,2},{4,5},{5,4},{6,7},{7,6},{8,9},{9,8},{10,11... | collective-permute-start | bytes 6152 | tf_op jit(solution)/shard_map/ppermute | solution.py:278
  215.2 5.5 %collective-permute-start.12 = (bf16[8,1024]{1,0:T(8,128)(2,1)S(1)}, bf16[8,1024]{1,0:T(8,128)(2,1)S(1)}, u32[]{:S(2)}, u32[]{:S(2)}) collective-permute-start(bf16[8,1024]{1,0:T(8,128)(2,1)S(1)} %bitcast.234), channel_id=1, source_target_pairs={{0,2},{2,4},{4,6},{6,8},{8,10},{10,12},{12,14},{14,16},{16,18},{18... | collective-permute-start | bytes 49160 | tf_op jit(solution)/shard_map/ppermute | solution.py:272
  242.4 6.7 %collective-permute-start.18 = (f32[128,8]{0,1:T(8,128)S(1)}, f32[128,8]{0,1:T(8,128)S(1)}, u32[]{:S(2)}, u32[]{:S(2)}) collective-permute-start(f32[128,8]{0,1:T(8,128)S(1)} %bitcast.241), channel_id=1, source_target_pairs={{0,1},{1,0},{2,3},{3,2},{4,5},{5,4},{6,7},{7,6},{8,9},{9,8},{10,11... | collective-permute-start | bytes 12296 | tf_op jit(solution)/shard_map/ppermute | solution.py:278
  242.9 7.3 %collective-permute-start.17 = (f32[8,1024]{1,0:T(8,128)S(1)}, f32[8,1024]{1,0:T(8,128)S(1)}, u32[]{:S(2)}, u32[]{:S(2)}) collective-permute-start(f32[8,1024]{1,0:T(8,128)S(1)} %get-tuple-element.45), channel_id=1, source_target_pairs={{2,0},{4,2},{6,4},{8,6},{10,8},{12,10},{14,12},{16,14},{18,16},{20... | collective-permute-start | bytes 98312 | tf_op jit(solution)/shard_map/ppermute | solution.py:272
  247.0 3.2 collective-permute-start.16
  258.2 32.6 %all-to-all-start.5 = ((bf16[16,128,256]{2,1,0:T(8,128)(2,1)}), bf16[16,128,256]{2,1,0:T(8,128)(2,1)S(1)}, u32[]{:S(2)}, u32[]{:S(2)}) async-start(bf16[16,128,256]{2,1,0:T(8,128)(2,1)} %rim_lines.3), calls=%async_computation.5 | async-start | bytes 2097152 | tf_op jit(solution)/shard_map/all_to_all | solution.py:211
  290.8 29.9 %all-to-all-start.4 = ((bf16[16,128,256]{2,1,0:T(8,128)(2,1)}), bf16[16,128,256]{2,1,0:T(8,128)(2,1)}, u32[]{:S(2)}, u32[]{:S(2)}) async-start(bf16[16,128,256]{2,1,0:T(8,128)(2,1)} %rim_lines.2), calls=%async_computation.4 | async-start | bytes 2097152 | tf_op jit(solution)/shard_map/all_to_all | solution.py:211
  304.3 64.6 %collective-permute-start.23 = (bf16[16,64,256]{2,1,0:T(8,128)(2,1)}, bf16[16,64,256]{2,1,0:T(8,128)(2,1)}, u32[]{:S(2)}, u32[]{:S(2)}) collective-permute-start(bf16[16,64,256]{2,1,0:T(8,128)(2,1)} %get-tuple-element.33), channel_id=1, source_target_pairs={{0,1},{1,0},{2,3},{3,2},{4,5},{5,4},{6,7},{7,6},{8,9},{9,8},{10,11... | collective-permute-start | bytes 1572872 | tf_op jit(solution)/shard_map/ppermute | solution.py:219
  305.3 68.0 %collective-permute-start.22 = (bf16[16,64,256]{2,1,0:T(8,128)(2,1)}, bf16[16,64,256]{2,1,0:T(8,128)(2,1)}, u32[]{:S(2)}, u32[]{:S(2)}) collective-permute-start(bf16[16,64,256]{2,1,0:T(8,128)(2,1)} %get-tuple-element.33), channel_id=1, source_target_pairs={{0,2},{2,0},{4,6},{6,4},{8,10},{10,8},{12,14},{14,12},{16,18},{18,... | collective-permute-start | bytes 1572872 | tf_op jit(solution)/shard_map/ppermute | solution.py:220
  332.3 13.7 %collective-permute-start.29 = (bf16[16,64,256]{2,1,0:T(8,128)(2,1)S(1)}, bf16[16,64,256]{2,1,0:T(8,128)(2,1)S(1)}, u32[]{:S(2)}, u32[]{:S(2)}) collective-permute-start(bf16[16,64,256]{2,1,0:T(8,128)(2,1)S(1)} %copy-done.14), channel_id=1, source_target_pairs={{0,1},{1,0},{2,3},{3,2},{4,5},{5,4},{6,7},{7,6},{8,9},{9,8},{10,11... | collective-permute-start | bytes 1572872 | tf_op jit(solution)/shard_map/ppermute | solution.py:219
  333.3 25.4 %collective-permute-start.28 = (bf16[16,64,256]{2,1,0:T(8,128)(2,1)S(1)}, bf16[16,64,256]{2,1,0:T(8,128)(2,1)S(1)}, u32[]{:S(2)}, u32[]{:S(2)}) collective-permute-start(bf16[16,64,256]{2,1,0:T(8,128)(2,1)S(1)} %copy-done.14), channel_id=1, source_target_pairs={{0,2},{2,0},{4,6},{6,4},{8,10},{10,8},{12,14},{14,12},{16,18},{18,... | collective-permute-start | bytes 1572872 | tf_op jit(solution)/shard_map/ppermute | solution.py:220
  333.3 23.9 %collective-permute-start.26 = (bf16[16,64,256]{2,1,0:T(8,128)(2,1)S(1)}, bf16[16,64,256]{2,1,0:T(8,128)(2,1)S(1)}, u32[]{:S(2)}, u32[]{:S(2)}) collective-permute-start(bf16[16,64,256]{2,1,0:T(8,128)(2,1)S(1)} %get-tuple-element.30), channel_id=1, source_target_pairs={{0,1},{1,0},{2,3},{3,2},{4,5},{5,4},{6,7},{7,6},{8,9},{9,8},{10,11... | collective-permute-start | bytes 1572872 | tf_op jit(solution)/shard_map/ppermute | solution.py:219
  334.2 12.6 %copy-start.6 = (bf16[512,512]{1,0:T(8,128)(2,1)S(1)}, bf16[512,512]{1,0:T(8,128)(2,1)}, u32[]{:S(2)}) copy-start(bf16[512,512]{1,0:T(8,128)(2,1)} %get-tuple-element.26) | copy-start | bytes 1572868
  346.0 14.1 %collective-permute-start.25 = (bf16[16,64,256]{2,1,0:T(8,128)(2,1)S(1)}, bf16[16,64,256]{2,1,0:T(8,128)(2,1)S(1)}, u32[]{:S(2)}, u32[]{:S(2)}) collective-permute-start(bf16[16,64,256]{2,1,0:T(8,128)(2,1)S(1)} %get-tuple-element.30), channel_id=1, source_target_pairs={{0,2},{2,0},{4,6},{6,4},{8,10},{10,8},{12,14},{14,12},{16,18},{18,... | collective-permute-start | bytes 1572872 | tf_op jit(solution)/shard_map/ppermute | solution.py:220
  357.2 13.6 %collective-permute-start.20 = (bf16[16,64,256]{2,1,0:T(8,128)(2,1)}, bf16[16,64,256]{2,1,0:T(8,128)(2,1)}, u32[]{:S(2)}, u32[]{:S(2)}) collective-permute-start(bf16[16,64,256]{2,1,0:T(8,128)(2,1)} %get-tuple-element.31), channel_id=1, source_target_pairs={{0,1},{1,0},{2,3},{3,2},{4,5},{5,4},{6,7},{7,6},{8,9},{9,8},{10,11... | collective-permute-start | bytes 1572872 | tf_op jit(solution)/shard_map/ppermute | solution.py:219
  358.7 2.5 collective-permute-start.27
  360.1 2.0 collective-permute-start.30
  361.2 13.7 %collective-permute-start.19 = (bf16[16,64,256]{2,1,0:T(8,128)(2,1)}, bf16[16,64,256]{2,1,0:T(8,128)(2,1)}, u32[]{:S(2)}, u32[]{:S(2)}) collective-permute-start(bf16[16,64,256]{2,1,0:T(8,128)(2,1)} %get-tuple-element.31), channel_id=1, source_target_pairs={{0,2},{2,0},{4,6},{6,4},{8,10},{10,8},{12,14},{14,12},{16,18},{18,... | collective-permute-start | bytes 1572872 | tf_op jit(solution)/shard_map/ppermute | solution.py:220
  363.9 29.9 %all-to-all-start.7 = ((bf16[16,64,512]{2,1,0:T(8,128)(2,1)}), bf16[16,64,512]{2,1,0:T(8,128)(2,1)S(1)}, u32[]{:S(2)}, u32[]{:S(2)}) async-start(bf16[16,64,512]{2,1,0:T(8,128)(2,1)} %add_convert_fusion), calls=%async_computation.7 | async-start | bytes 2097152 | tf_op jit(solution)/shard_map/all_to_all | solution.py:211
  370.4 6.6 %collective-permute-start.24 = (bf16[16,64,256]{2,1,0:T(8,128)(2,1)}, bf16[16,64,256]{2,1,0:T(8,128)(2,1)S(1)}, u32[]{:S(2)}, u32[]{:S(2)}) collective-permute-start(bf16[16,64,256]{2,1,0:T(8,128)(2,1)} %collective-permute-done.23), channel_id=1, source_target_pairs={{0,2},{2,0},{4,6},{6,4},{8,10},{10,8},{12,14},{14,12},{16,18},{18,... | collective-permute-start | bytes 1572872 | tf_op jit(solution)/shard_map/ppermute | solution.py:221
  370.8 5.7 %collective-permute-start.21 = (bf16[16,64,256]{2,1,0:T(8,128)(2,1)}, bf16[16,64,256]{2,1,0:T(8,128)(2,1)S(1)}, u32[]{:S(2)}, u32[]{:S(2)}) collective-permute-start(bf16[16,64,256]{2,1,0:T(8,128)(2,1)} %collective-permute-done.20), channel_id=1, source_target_pairs={{0,2},{2,0},{4,6},{6,4},{8,10},{10,8},{12,14},{14,12},{16,18},{18,... | collective-permute-start | bytes 1572872 | tf_op jit(solution)/shard_map/ppermute | solution.py:221
  393.7 29.8 %all-to-all-start.6 = ((bf16[16,64,512]{2,1,0:T(8,128)(2,1)}), bf16[16,64,512]{2,1,0:T(8,128)(2,1)S(1)}, u32[]{:S(2)}, u32[]{:S(2)}) async-start(bf16[16,64,512]{2,1,0:T(8,128)(2,1)} %add_convert_fusion.1), calls=%async_computation.6 | async-start | bytes 2097152 | tf_op jit(solution)/shard_map/all_to_all | solution.py:211
  (11 other events, 31.2 us)
Sparse Core Ops, SparseCore 0:
  10.7 61.2 all-gather.2
  74.1 61.2 all-gather.4

commit v4 on v3

--- a/solution.py
+++ b/solution.py
@@ -9,7 +9,8 @@
 
 BF16 = jnp.bfloat16
 F32 = jnp.float32
-STEP = 16
+STEP = 32
+GROUP = 4
 CHUNKS = 2
 PARAMS = pltpu.CompilerParams(vmem_limit_bytes=56 * 1024 * 1024)
 
@@ -22,18 +23,28 @@
     )
 
 
-def store_lines(turned, out, parts, chunk):
-    levels, width = turned.shape[1:]
-    part, piece = width // parts, out.shape[2]
-    for l in range(levels):
+def chunk_spans(width, parts, chunk):
+    part = width // parts
+    piece = part // CHUNKS
+    return [
+        slice(s * part + chunk * piece, s * part + (chunk + 1) * piece)
+        for s in range(parts)
+    ]
+
+
+def store_lines(turned, out, parts):
+    piece = out.shape[2]
+    for l in range(turned.shape[1]):
         for s in range(parts):
-            at = s * part + chunk * piece
-            out[l * parts + s] = turned[:, l, at : at + piece].astype(BF16)
+            got = turned[:, l, s * piece : (s + 1) * piece]
+            out[l * parts + s] = got.astype(BF16)
 
 
 def lines_body(parts, chunk, block, out, turned):
-    turned[...] = block[...].astype(F32)
-    store_lines(turned, out, parts, chunk)
+    piece = out.shape[2]
+    for s, span in enumerate(chunk_spans(block.shape[2], parts, chunk)):
+        turned[:, :, s * piece : (s + 1) * piece] = block[:, :, span].astype(F32)
+    store_lines(turned, out, parts)
 
 
 def as_lines(block, parts, chunk):
@@ -45,7 +56,7 @@
         in_specs=[pl.BlockSpec((STEP, levels, width), lambda i: (i, 0, 0))],
         out_specs=pl.BlockSpec((shape[0], STEP, shape[2]), lambda i: (0, i, 0)),
         out_shape=jax.ShapeDtypeStruct(shape, BF16),
-        scratch_shapes=[pltpu.VMEM((STEP, levels, width), F32)],
+        scratch_shapes=[pltpu.VMEM((STEP, levels, width // CHUNKS), F32)],
         compiler_params=PARAMS,
         cost_estimate=cost(0, block, block),
         name="as_lines",
@@ -103,40 +114,41 @@
         carry[...] = jnp.zeros(carry.shape, F32)
 
     first = step * STEP
-    place = lax.broadcasted_iota(jnp.int32, (levels, width), 1)
+    place = lax.broadcasted_iota(jnp.int32, (GROUP, levels, width), 2)
     left_edge, right_edge = place == 0, place == width - 1
-    q_old, q_last, pending = carry[0], carry[1], carry[2]
-    up, here = state[first], state[first + 1]
-    for j in range(STEP):
-        down = state[first + j + 2]
-        cx, cy = wind_x[j], wind_y[j]
-        left = jnp.where(left_edge, sides[j, :, 0:1], pltpu.roll(here, 1, 1))
-        right = jnp.where(right_edge, sides[j, :, 1:2], pltpu.roll(here, width - 1, 1))
-        after = here - cx * (down - up) * 0.5 - cy * (right - left) * 0.5
-        end[j] = after
-        misfit = weight[j] * (after - innovation[j])
+    for j in range(0, STEP, GROUP):
+        rows_j, at = pl.ds(j, GROUP), first + j
+        here = state[pl.ds(at + 1, GROUP)]
+        cx, cy = wind_x[rows_j], wind_y[rows_j]
+        left = jnp.where(left_edge, sides[rows_j, :, 0:1], pltpu.roll(here, 1, 2))
+        right = jnp.where(
+            right_edge, sides[rows_j, :, 1:2], pltpu.roll(here, width - 1, 2)
+        )
+        dx = state[pl.ds(at + 2, GROUP)] - state[pl.ds(at, GROUP)]
+        after = here - cx * dx * 0.5 - cy * (right - left) * 0.5
+        end[rows_j] = after
+        misfit = weight[rows_j] * (after - innovation[rows_j])
         p, q = cy * misfit, cx * misfit
-        side_flux[j, :, 0:1] = p[:, 0:1]
-        side_flux[j, :, 1:2] = p[:, width - 1 : width]
-        at = first + j - 1 if j > 0 else jnp.maximum(first - 1, 0)
-        flat[at] = pending + 0.5 * (q - q_old)
-        left = jnp.where(left_edge, 0.0, pltpu.roll(p, 1, 1))
-        right = jnp.where(right_edge, 0.0, pltpu.roll(p, width - 1, 1))
-        pending = misfit + 0.5 * (right - left)
-        q_old, q_last = q_last, q
-        up, here = here, down
+        side_flux[rows_j, :, 0:1] = p[:, :, 0:1]
+        side_flux[rows_j, :, 1:2] = p[:, :, width - 1 : width]
+        left = jnp.where(left_edge, 0.0, pltpu.roll(p, 1, 2))
+        right = jnp.where(right_edge, 0.0, pltpu.roll(p, width - 1, 2))
+        flat_j = misfit + 0.5 * (right - left)
+        flat[jnp.maximum(at - 1, 0)] = carry[2] + 0.5 * (q[0] - carry[0])
+        flat[at] = flat_j[0] + 0.5 * (q[1] - carry[1])
+        flat[pl.ds(at + 1, GROUP - 2)] = flat_j[1:-1] + 0.5 * (q[2:] - q[:-2])
         if j == 0:
-
-            @pl.when(step == 0)
-            def _(q=q):
-                row_flux[0] = q
-
-    carry[0], carry[1], carry[2] = q_old, q_last, pending
+            carry[3] = q[0]
+        carry[0], carry[1], carry[2] = q[GROUP - 2], q[GROUP - 1], flat_j[GROUP - 1]
+
+    @pl.when(step == 0)
+    def _():
+        row_flux[0] = carry[3]
 
     @pl.when(step == rows // STEP - 1)
     def _():
-        flat[rows - 1] = pending - 0.5 * q_old
-        row_flux[1] = q_last
+        flat[rows - 1] = carry[2] - 0.5 * carry[0]
+        row_flux[1] = carry[1]
 
 
 def forward(starts, rows_in, sides, innovation, weight, wind_x, wind_y):
@@ -159,7 +171,7 @@
         ],
         scratch_shapes=[
             pltpu.VMEM((rows + 2, levels, width), F32),
-            pltpu.VMEM((3, levels, width), F32),
+            pltpu.VMEM((4, levels, width), F32),
         ],
         compiler_params=PARAMS,
         cost_estimate=cost(30 * innovation.size, *[innovation] * 7),
@@ -169,22 +181,31 @@
 
 def rim_body(parts, chunk, last, flat, rows_in, sides, out, turned):
     step = pl.program_id(0)
-    width = flat.shape[2]
-    place = lax.broadcasted_iota(jnp.int32, flat.shape, 2)
-    value = flat[...]
-    value = value - jnp.where(place == 0, 0.5 * sides[:, :, 0:1], 0.0)
-    value = value + jnp.where(place == width - 1, 0.5 * sides[:, :, 1:2], 0.0)
-    turned[...] = value
+    levels, width = flat.shape[1:]
+    piece = out.shape[2]
+    place = lax.broadcasted_iota(jnp.int32, (STEP, levels, piece), 2)
+    spans = chunk_spans(width, parts, chunk)
+    for s, span in enumerate(spans):
+        value = flat[:, :, span]
+        if span.start == 0:
+            value = value - jnp.where(place == 0, 0.5 * sides[:, :, 0:1], 0.0)
+        if span.stop == width:
+            value = value + jnp.where(place == piece - 1, 0.5 * sides[:, :, 1:2], 0.0)
+        turned[:, :, s * piece : (s + 1) * piece] = value
 
     @pl.when(step == 0)
     def _():
-        turned[pl.ds(0, 1)] += -0.5 * rows_in[pl.ds(0, 1)]
+        for s, span in enumerate(spans):
+            at = slice(s * piece, (s + 1) * piece)
+            turned[0, :, at] += -0.5 * rows_in[0, :, span]
 
     @pl.when(step == last)
     def _():
-        turned[pl.ds(STEP - 1, 1)] += 0.5 * rows_in[pl.ds(1, 1)]
-
-    store_lines(turned, out, parts, chunk)
+        for s, span in enumerate(spans):
+            at = slice(s * piece, (s + 1) * piece)
+            turned[STEP - 1, :, at] += 0.5 * rows_in[1, :, span]
+
+    store_lines(turned, out, parts)
 
 
 def rim_lines(flat, rows_in, sides, parts, chunk):
@@ -200,7 +221,7 @@
         ],
         out_specs=pl.BlockSpec((shape[0], STEP, shape[2]), lambda i: (0, i, 0)),
         out_shape=jax.ShapeDtypeStruct(shape, BF16),
-        scratch_shapes=[pltpu.VMEM((STEP, levels, width), F32)],
+        scratch_shapes=[pltpu.VMEM((STEP, levels, width // CHUNKS), F32)],
         compiler_params=PARAMS,
         cost_estimate=cost(4 * flat.size, flat, flat),
         name="rim_lines",
@@ -309,11 +330,12 @@
                 start = start + jnp.einsum(
                     "brc,kc->brk", plane, matrix[:, span], preferred_element_type=F32
                 )
-        came = swap_all(start.astype(BF16)).reshape(levels, parts, cut, part)
+        start = start.astype(BF16)
+        if h == CHUNKS - 1:
+            start, filter_y = lax.optimization_barrier((start, filter_y))
+            columns_y = filter_columns(filter_y, parts)
+        came = swap_all(start).reshape(levels, parts, cut, part)
         came = came.transpose(2, 0, 1, 3).reshape(cut, levels, width)
-        if h == 0:
-            came, filter_y = lax.optimization_barrier((came, filter_y))
-            columns_y = filter_columns(filter_y, parts)
         starts.append(came)
 
     rows_in = row_halo(starts[0][0], starts[-1][-1]).astype(F32)

time: 438 us -> 417 us (0.952)
  Pallas kernels: 55.4 us -> 41.8 us
    ppermute x1, waiting for transfers between devices: 18.6 us -> 0.01 us  [filter_columns(): got = lax.ppermute(sent, 'gy', [(0, 1), (1, 0)])]
    all_to_all x7, waiting for transfers between devices: 92.7 us -> 108 us  [swap_all(): return lax.all_to_all(lines, 'gx', 0, 0, tiled=True)]
    pallas_call x1, Pallas kernels: 19.4 us -> 14.7 us  [forward(): pl.pallas_call(forward_body, grid=(rows // STEP,), in_specs=[start] * CHU...]
  transfers between devices with their start and end apart: 40 -> 40, of which waited for: 14 -> 15; matrix products, arithmetic and copies ran while one was open for 17% -> 17% of each run, Pallas kernels for 6% -> 4%
where the time goes in v4:
time: 417 us; the launch traced here: 416 us
  waiting for transfers between devices  163 us (39%)
  starting transfers between devices  73.1 us (18%)
  matrix products  51.7 us (12%)
  blocking collectives  44.1 us (11%)
  Pallas kernels  41.8 us (10%)
  local copies, waits for them, and re-layouts  24.9 us (6%)
  between operations  14.6 us (4%)
    all_to_all x7, waiting for transfers between devices, swap_all(): return lax.all_to_all(lines, 'gx', 0, 0, tiled=True)  108 us
    ppermute x8, waiting for transfers between devices, plane_pieces(): far = lax.ppermute(lines, 'gy', [(0, 1), (1, 0)])  50.2 us
    all_to_all x1, blocking collectives, swap_all(): return lax.all_to_all(lines, 'gx', 0, 0, tiled=True)  44.1 us
    all_to_all x7, starting transfers between devices, swap_all(): return lax.all_to_all(lines, 'gx', 0, 0, tiled=True)  40.4 us
    dot_general x16, matrix products, per_device(): jnp.einsum('brk,kc->brc', plane, matrix[span], preferred_element_type=F32)  15.5 us
    pallas_call x1, Pallas kernels, forward(): pl.pallas_call(forward_body, grid=(rows // STEP,), in_specs=[start] * CHU...  14.7 us
    dot_general x16, matrix products, per_device(): jnp.einsum('brc,kc->brk', plane, matrix[:, span], preferred_element_type=...  12.5 us
    dot_general x4, matrix products, per_device(): smoothed = jnp.dot(matrix_x[h], lines[w], preferred_element_type=F32)  11.9 us
  transfers between devices with their start and end apart: 40, of which 15 were waited for; matrix products, arithmetic and copies ran while one was open for 17% of the time, Pallas kernels for 4%

profile of v4, /device:TPU:9, one launch (start us, length us, event | category | flops | bytes accessed | tf_op | source)
XLA Modules:
  0.0 415.7 jit_solution(11549273836189326634)
XLA Ops:
  9.0 4.8 %as_lines.3 = bf16[16,128,256]{2,1,0:T(8,128)(2,1)} custom-call(bf16[128,8,1024]{2,1,0:T(8,128)(2,1)} %control.3), custom_call_target="tpu_custom_call" | custom-call | bytes 4194304 | tf_op jit(solution)/shard_map/as_lines/pallas_call | solution.py:53
  13.8 44.1 %all_to_all.40 = bf16[16,128,256]{2,1,0:T(8,128)(2,1)S(1)} all-to-all(bf16[16,128,256]{2,1,0:T(8,128)(2,1)} %as_lines.3), channel_id=1, replica_groups=mesh['gx'=16,'gy'=2] {'gx'}, dimensions={0} | all-to-all | bytes 2097152 | tf_op jit(solution)/shard_map/all_to_all | solution.py:232
  58.7 4.8 %as_lines.2 = bf16[16,128,256]{2,1,0:T(8,128)(2,1)} custom-call(bf16[128,8,1024]{2,1,0:T(8,128)(2,1)} %control.3), custom_call_target="tpu_custom_call" | custom-call | bytes 4194304 | tf_op jit(solution)/shard_map/as_lines/pallas_call | solution.py:53
  63.4 7.1 %all-to-all-start = ((bf16[16,128,256]{2,1,0:T(8,128)(2,1)}), bf16[16,128,256]{2,1,0:T(8,128)(2,1)S(1)}, u32[]{:S(2)}, u32[]{:S(2)}) async-start(bf16[16,128,256]{2,1,0:T(8,128)(2,1)} %as_lines.2), calls=%async_computation | async-start | bytes 2097152 | tf_op jit(solution)/shard_map/all_to_all | solution.py:232
  70.6 3.9 all-gather.3.cloned.1.call-done
  74.4 3.5 fusion.4
  79.9 23.9 %all-to-all-done = bf16[16,128,256]{2,1,0:T(8,128)(2,1)S(1)} async-done(((bf16[16,128,256]{2,1,0:T(8,128)(2,1)}), bf16[16,128,256]{2,1,0:T(8,128)(2,1)S(1)}, u32[]{:S(2)}, u32[]{:S(2)}) %all-to-all-start) | async-done | bytes 1048608 | tf_op jit(solution)/shard_map/all_to_all | solution.py:232
  103.8 3.6 convolution_convert_fusion.3
  109.8 11.6 %collective-permute-done.1 = bf16[16,64,256]{2,1,0:T(8,128)(2,1)S(1)} collective-permute-done((bf16[16,64,256]{2,1,0:T(8,128)(2,1)S(1)}, bf16[16,64,256]{2,1,0:T(8,128)(2,1)S(1)}, u32[]{:S(2)}, u32[]{:S(2)}) %collective-permute-start.1) | collective-permute-done | bytes 524320 | tf_op jit(solution)/shard_map/ppermute | solution.py:240
  126.4 1.9 add_convert_fusion.3
  128.3 5.3 %all-to-all-start.2 = ((bf16[16,64,512]{2,1,0:T(8,128)(2,1)}), bf16[16,64,512]{2,1,0:T(8,128)(2,1)S(1)}, u32[]{:S(2)}, u32[]{:S(2)}) async-start(bf16[16,64,512]{2,1,0:T(8,128)(2,1)} %add_convert_fusion.3), calls=%async_computation.2 | async-start | bytes 2097152 | tf_op jit(solution)/shard_map/all_to_all | solution.py:232
  133.6 3.6 convolution_convert_fusion
  142.0 8.5 %collective-permute-done.10 = bf16[16,64,256]{2,1,0:T(8,128)(2,1)S(1)} collective-permute-done((bf16[16,64,256]{2,1,0:T(8,128)(2,1)S(1)}, bf16[16,64,256]{2,1,0:T(8,128)(2,1)S(1)}, u32[]{:S(2)}, u32[]{:S(2)}) %collective-permute-start.10) | collective-permute-done | bytes 524320 | tf_op jit(solution)/shard_map/ppermute | solution.py:240
  150.9 2.0 collective-permute-start.11
  153.0 8.7 %collective-permute-done.7 = bf16[16,64,256]{2,1,0:T(8,128)(2,1)S(1)} collective-permute-done((bf16[16,64,256]{2,1,0:T(8,128)(2,1)S(1)}, bf16[16,64,256]{2,1,0:T(8,128)(2,1)S(1)}, u32[]{:S(2)}, u32[]{:S(2)}) %collective-permute-start.7) | collective-permute-done | bytes 524320 | tf_op jit(solution)/shard_map/ppermute | solution.py:240
  164.9 1.9 add_convert_fusion.2
  166.8 6.0 %all-to-all-start.3 = ((bf16[16,64,512]{2,1,0:T(8,128)(2,1)}), bf16[16,64,512]{2,1,0:T(8,128)(2,1)S(1)}, u32[]{:S(2)}, u32[]{:S(2)}) async-start(bf16[16,64,512]{2,1,0:T(8,128)(2,1)} %add_convert_fusion.2), calls=%async_computation.3 | async-start | bytes 2097152 | tf_op jit(solution)/shard_map/all_to_all | solution.py:232
  172.8 2.3 constant_dynamic-slice_fusion.2
  177.0 2.5 collective-permute-start.13
  180.0 2.7 fusion.65
  182.7 15.0 %all-to-all-done.3 = bf16[16,64,512]{2,1,0:T(8,128)(2,1)S(1)} async-done(((bf16[16,64,512]{2,1,0:T(8,128)(2,1)}), bf16[16,64,512]{2,1,0:T(8,128)(2,1)S(1)}, u32[]{:S(2)}, u32[]{:S(2)}) %all-to-all-start.3) | async-done | bytes 1048608 | tf_op jit(solution)/shard_map/all_to_all | solution.py:232
  198.6 1.8 copy.291
  202.2 2.1 constant_dynamic-slice_fusion
  204.3 3.5 collective-permute-start.12
  209.6 14.7 %forward.1 = (f32[128,8,1024]{2,1,0:T(8,128)}, f32[128,8,1024]{2,1,0:T(8,128)}, f32[2,8,1024]{2,1,0:T(8,128)}, f32[128,8,2]{2,1,0:T(8,128)}) custom-call(bf16[64,8,1024]{2,1,0:T(8,128)(2,1)} %bitcast.207, bf16[64,8,1024]{2,1,0:T(8,128)(2,1)} %bitcast.210, f32[2,8,1024]{2,1,0:T(8,128)} %maximum_convert_fusion.refs_2_, f32[128,8,2]{2,1,0:T(8,128)} %copy.269.refs_3_, ...), custom_call_target="tpu_custom_call" | custom-call | flops 31457280 | bytes 29360128 | tf_op jit(solution)/shard_map/forward/pallas_call | solution.py:161
  226.1 3.6 collective-permute-start.17
  229.7 2.8 collective-permute-start.16
  234.2 5.7 %rim_lines.3 = bf16[16,128,256]{2,1,0:T(8,128)(2,1)} custom-call(f32[128,8,1024]{2,1,0:T(8,128)} %get-tuple-element.21.flat, f32[2,8,1024]{2,1,0:T(8,128)} %pad_maximum_fusion.rows_in, f32[128,8,2]{2,1,0:T(8,128)} %copy.271.sides), custom_call_target="tpu_custom_call" | custom-call | flops 4194304 | bytes 8388608 | tf_op jit(solution)/shard_map/rim_lines/pallas_call | solution.py:214
  239.9 7.0 %all-to-all-start.5 = ((bf16[16,128,256]{2,1,0:T(8,128)(2,1)}), bf16[16,128,256]{2,1,0:T(8,128)(2,1)S(1)}, u32[]{:S(2)}, u32[]{:S(2)}) async-start(bf16[16,128,256]{2,1,0:T(8,128)(2,1)} %rim_lines.3), calls=%async_computation.5 | async-start | bytes 2097152 | tf_op jit(solution)/shard_map/all_to_all | solution.py:232
  247.0 5.7 %rim_lines.2 = bf16[16,128,256]{2,1,0:T(8,128)(2,1)} custom-call(f32[128,8,1024]{2,1,0:T(8,128)} %get-tuple-element.21.flat, f32[2,8,1024]{2,1,0:T(8,128)} %pad_maximum_fusion.rows_in, f32[128,8,2]{2,1,0:T(8,128)} %copy.271.sides), custom_call_target="tpu_custom_call" | custom-call | flops 4194304 | bytes 8388608 | tf_op jit(solution)/shard_map/rim_lines/pallas_call | solution.py:214
  252.7 19.1 %all-to-all-done.5 = bf16[16,128,256]{2,1,0:T(8,128)(2,1)S(1)} async-done(((bf16[16,128,256]{2,1,0:T(8,128)(2,1)}), bf16[16,128,256]{2,1,0:T(8,128)(2,1)S(1)}, u32[]{:S(2)}, u32[]{:S(2)}) %all-to-all-start.5) | async-done | bytes 1048608 | tf_op jit(solution)/shard_map/all_to_all | solution.py:232
  271.8 5.0 %all-to-all-start.4 = ((bf16[16,128,256]{2,1,0:T(8,128)(2,1)}), bf16[16,128,256]{2,1,0:T(8,128)(2,1)}, u32[]{:S(2)}, u32[]{:S(2)}) async-start(bf16[16,128,256]{2,1,0:T(8,128)(2,1)} %rim_lines.2), calls=%async_computation.4 | async-start | bytes 2097152 | tf_op jit(solution)/shard_map/all_to_all | solution.py:232
  276.9 3.6 fusion.71
  280.5 2.2 fusion.2
  287.3 1.8 fusion.17
  289.0 12.7 %all-to-all-done.4 = bf16[16,128,256]{2,1,0:T(8,128)(2,1)} async-done(((bf16[16,128,256]{2,1,0:T(8,128)(2,1)}), bf16[16,128,256]{2,1,0:T(8,128)(2,1)}, u32[]{:S(2)}, u32[]{:S(2)}) %all-to-all-start.4) | async-done | bytes 1048608 | tf_op jit(solution)/shard_map/all_to_all | solution.py:232
  303.0 3.6 fusion.70
  306.7 2.3 fusion.3
  315.6 11.4 %collective-permute-done.29 = bf16[16,64,256]{2,1,0:T(8,128)(2,1)S(1)} collective-permute-done((bf16[16,64,256]{2,1,0:T(8,128)(2,1)S(1)}, bf16[16,64,256]{2,1,0:T(8,128)(2,1)S(1)}, u32[]{:S(2)}, u32[]{:S(2)}) %collective-permute-start.29) | collective-permute-done | bytes 524320 | tf_op jit(solution)/shard_map/ppermute | solution.py:240
  328.2 10.0 %collective-permute-done.26 = bf16[16,64,256]{2,1,0:T(8,128)(2,1)S(1)} collective-permute-done((bf16[16,64,256]{2,1,0:T(8,128)(2,1)S(1)}, bf16[16,64,256]{2,1,0:T(8,128)(2,1)S(1)}, u32[]{:S(2)}, u32[]{:S(2)}) %collective-permute-start.26) | collective-permute-done | bytes 524320 | tf_op jit(solution)/shard_map/ppermute | solution.py:240
  343.3 1.8 add_convert_fusion
  345.1 5.0 %all-to-all-start.7 = ((bf16[16,64,512]{2,1,0:T(8,128)(2,1)}), bf16[16,64,512]{2,1,0:T(8,128)(2,1)S(1)}, u32[]{:S(2)}, u32[]{:S(2)}) async-start(bf16[16,64,512]{2,1,0:T(8,128)(2,1)} %add_convert_fusion), calls=%async_computation.7 | async-start | bytes 2097152 | tf_op jit(solution)/shard_map/all_to_all | solution.py:232
  358.0 1.8 add_convert_fusion.1
  359.8 15.2 %all-to-all-done.7.lines = bf16[16,64,512]{2,1,0:T(8,128)(2,1)S(1)} async-done(((bf16[16,64,512]{2,1,0:T(8,128)(2,1)}), bf16[16,64,512]{2,1,0:T(8,128)(2,1)S(1)}, u32[]{:S(2)}, u32[]{:S(2)}) %all-to-all-start.7) | async-done | bytes 1048608 | tf_op jit(solution)/shard_map/all_to_all | solution.py:232
  375.0 5.0 %all-to-all-start.6 = ((bf16[16,64,512]{2,1,0:T(8,128)(2,1)}), bf16[16,64,512]{2,1,0:T(8,128)(2,1)S(1)}, u32[]{:S(2)}, u32[]{:S(2)}) async-start(bf16[16,64,512]{2,1,0:T(8,128)(2,1)} %add_convert_fusion.1), calls=%async_computation.6 | async-start | bytes 2097152 | tf_op jit(solution)/shard_map/all_to_all | solution.py:232
  380.0 3.1 add_lines.2.rest_0_
  383.0 21.8 %all-to-all-done.6.lines = bf16[16,64,512]{2,1,0:T(8,128)(2,1)S(1)} async-done(((bf16[16,64,512]{2,1,0:T(8,128)(2,1)}), bf16[16,64,512]{2,1,0:T(8,128)(2,1)S(1)}, u32[]{:S(2)}, u32[]{:S(2)}) %all-to-all-start.6) | async-done | bytes 1048608 | tf_op jit(solution)/shard_map/all_to_all | solution.py:232
  405.8 3.1 add_lines.3
  (152 shorter events, 58.1 us)
Async XLA Ops:
  7.2 67.3 %all-gather.3.cloned.1.call-start = ((), (), s32[]{:S(2)}) async-start(), calls=%async_computation.8 | async-start | bytes 4456448 | tf_op jit(solution)/shard_map/all_gather | solution.py:316
  8.9 49.0 %copy-start.12 = (bf16[128,2048]{1,0:T(8,128)(2,1)S(1)}, bf16[128,2048]{1,0:T(8,128)(2,1)}, u32[]{:S(2)}) copy-start(bf16[128,2048]{1,0:T(8,128)(2,1)} %param.12) | copy-start | bytes 1572868
  8.9 124.7 %all-gather.5.cloned.1.call-start = ((), (), s32[]{:S(2)}) async-start(), calls=%async_computation.9 | async-start | bytes 4456448 | tf_op jit(solution)/shard_map/all_gather | solution.py:322
  63.4 40.4 %all-to-all-start = ((bf16[16,128,256]{2,1,0:T(8,128)(2,1)}), bf16[16,128,256]{2,1,0:T(8,128)(2,1)S(1)}, u32[]{:S(2)}, u32[]{:S(2)}) async-start(bf16[16,128,256]{2,1,0:T(8,128)(2,1)} %as_lines.2), calls=%async_computation | async-start | bytes 2097152 | tf_op jit(solution)/shard_map/all_to_all | solution.py:232
  78.1 43.7 %collective-permute-start.4 = (bf16[16,64,256]{2,1,0:T(8,128)(2,1)S(1)}, bf16[16,64,256]{2,1,0:T(8,128)(2,1)}, u32[]{:S(2)}, u32[]{:S(2)}) collective-permute-start(bf16[16,64,256]{2,1,0:T(8,128)(2,1)S(1)} %bitcast.214), channel_id=1, source_target_pairs={{0,1},{1,0},{2,3},{3,2},{4,5},{5,4},{6,7},{7,6},{8,9},{9,8},{10,11... | collective-permute-start | bytes 1572872 | tf_op jit(solution)/shard_map/ppermute | solution.py:240
  79.4 45.0 %collective-permute-start.3 = (bf16[16,64,256]{2,1,0:T(8,128)(2,1)S(1)}, bf16[16,64,256]{2,1,0:T(8,128)(2,1)}, u32[]{:S(2)}, u32[]{:S(2)}) collective-permute-start(bf16[16,64,256]{2,1,0:T(8,128)(2,1)S(1)} %bitcast.215), channel_id=1, source_target_pairs={{0,2},{2,0},{4,6},{6,4},{8,10},{10,8},{12,14},{14,12},{16,18},{18,... | collective-permute-start | bytes 1572872 | tf_op jit(solution)/shard_map/ppermute | solution.py:241
  103.8 4.9 %copy-start = (bf16[1024,2048]{1,0:T(8,128)(2,1)S(1)}, bf16[1024,2048]{1,0:T(8,128)(2,1)}, u32[]{:S(2)}) copy-start(bf16[1024,2048]{1,0:T(8,128)(2,1)} %param.13) | copy-start | bytes 12582916
  107.4 13.9 %collective-permute-start.1 = (bf16[16,64,256]{2,1,0:T(8,128)(2,1)S(1)}, bf16[16,64,256]{2,1,0:T(8,128)(2,1)S(1)}, u32[]{:S(2)}, u32[]{:S(2)}) collective-permute-start(bf16[16,64,256]{2,1,0:T(8,128)(2,1)S(1)} %bitcast.227), channel_id=1, source_target_pairs={{0,1},{1,0},{2,3},{3,2},{4,5},{5,4},{6,7},{7,6},{8,9},{9,8},{10,11... | collective-permute-start | bytes 1572872 | tf_op jit(solution)/shard_map/ppermute | solution.py:240
  108.8 15.1 %collective-permute-start = (bf16[16,64,256]{2,1,0:T(8,128)(2,1)S(1)}, bf16[16,64,256]{2,1,0:T(8,128)(2,1)S(1)}, u32[]{:S(2)}, u32[]{:S(2)}) collective-permute-start(bf16[16,64,256]{2,1,0:T(8,128)(2,1)S(1)} %bitcast.228), channel_id=1, source_target_pairs={{0,2},{2,0},{4,6},{6,4},{8,10},{10,8},{12,14},{14,12},{16,18},{18,... | collective-permute-start | bytes 1572872 | tf_op jit(solution)/shard_map/ppermute | solution.py:241
  121.3 4.6 %collective-permute-start.2 = (bf16[16,64,256]{2,1,0:T(8,128)(2,1)S(1)}, bf16[16,64,256]{2,1,0:T(8,128)(2,1)S(1)}, u32[]{:S(2)}, u32[]{:S(2)}) collective-permute-start(bf16[16,64,256]{2,1,0:T(8,128)(2,1)S(1)} %collective-permute-done.1), channel_id=1, source_target_pairs={{0,2},{2,0},{4,6},{6,4},{8,10},{10,8},{12,14},{14,12},{16,18},{18,... | collective-permute-start | bytes 1572872 | tf_op jit(solution)/shard_map/ppermute | solution.py:242
  121.8 4.6 %collective-permute-start.5 = (bf16[16,64,256]{2,1,0:T(8,128)(2,1)}, bf16[16,64,256]{2,1,0:T(8,128)(2,1)S(1)}, u32[]{:S(2)}, u32[]{:S(2)}) collective-permute-start(bf16[16,64,256]{2,1,0:T(8,128)(2,1)} %collective-permute-done.4), channel_id=1, source_target_pairs={{0,2},{2,0},{4,6},{6,4},{8,10},{10,8},{12,14},{14,12},{16,18},{18,... | collective-permute-start | bytes 1572872 | tf_op jit(solution)/shard_map/ppermute | solution.py:242
  128.3 38.5 %all-to-all-start.2 = ((bf16[16,64,512]{2,1,0:T(8,128)(2,1)}), bf16[16,64,512]{2,1,0:T(8,128)(2,1)S(1)}, u32[]{:S(2)}, u32[]{:S(2)}) async-start(bf16[16,64,512]{2,1,0:T(8,128)(2,1)} %add_convert_fusion.3), calls=%async_computation.2 | async-start | bytes 2097152 | tf_op jit(solution)/shard_map/all_to_all | solution.py:232
  133.6 5.6 %copy-start.17 = (bf16[1024,2048]{1,0:T(8,128)(2,1)S(1)}, bf16[1024,2048]{1,0:T(8,128)(2,1)}, u32[]{:S(2)}) copy-start(bf16[1024,2048]{1,0:T(8,128)(2,1)} %all-gather.5.cloned.1.call-done) | copy-start | bytes 12582916
  137.2 13.2 %collective-permute-start.10 = (bf16[16,64,256]{2,1,0:T(8,128)(2,1)S(1)}, bf16[16,64,256]{2,1,0:T(8,128)(2,1)S(1)}, u32[]{:S(2)}, u32[]{:S(2)}) collective-permute-start(bf16[16,64,256]{2,1,0:T(8,128)(2,1)S(1)} %bitcast.221), channel_id=1, source_target_pairs={{0,1},{1,0},{2,3},{3,2},{4,5},{5,4},{6,7},{7,6},{8,9},{9,8},{10,11... | collective-permute-start | bytes 1572872 | tf_op jit(solution)/shard_map/ppermute | solution.py:240
  138.6 24.8 %collective-permute-start.9 = (bf16[16,64,256]{2,1,0:T(8,128)(2,1)S(1)}, bf16[16,64,256]{2,1,0:T(8,128)(2,1)S(1)}, u32[]{:S(2)}, u32[]{:S(2)}) collective-permute-start(bf16[16,64,256]{2,1,0:T(8,128)(2,1)S(1)} %bitcast.222), channel_id=1, source_target_pairs={{0,2},{2,0},{4,6},{6,4},{8,10},{10,8},{12,14},{14,12},{16,18},{18,... | collective-permute-start | bytes 1572872 | tf_op jit(solution)/shard_map/ppermute | solution.py:241
  140.5 21.2 %collective-permute-start.7 = (bf16[16,64,256]{2,1,0:T(8,128)(2,1)S(1)}, bf16[16,64,256]{2,1,0:T(8,128)(2,1)S(1)}, u32[]{:S(2)}, u32[]{:S(2)}) collective-permute-start(bf16[16,64,256]{2,1,0:T(8,128)(2,1)S(1)} %bitcast.224), channel_id=1, source_target_pairs={{0,1},{1,0},{2,3},{3,2},{4,5},{5,4},{6,7},{7,6},{8,9},{9,8},{10,11... | collective-permute-start | bytes 1572872 | tf_op jit(solution)/shard_map/ppermute | solution.py:240
  140.7 23.1 %collective-permute-start.6 = (bf16[16,64,256]{2,1,0:T(8,128)(2,1)S(1)}, bf16[16,64,256]{2,1,0:T(8,128)(2,1)S(1)}, u32[]{:S(2)}, u32[]{:S(2)}) collective-permute-start(bf16[16,64,256]{2,1,0:T(8,128)(2,1)S(1)} %bitcast.225), channel_id=1, source_target_pairs={{0,2},{2,0},{4,6},{6,4},{8,10},{10,8},{12,14},{14,12},{16,18},{18,... | collective-permute-start | bytes 1572872 | tf_op jit(solution)/shard_map/ppermute | solution.py:241
  150.9 14.0 %collective-permute-start.11 = (bf16[16,64,256]{2,1,0:T(8,128)(2,1)S(1)}, bf16[16,64,256]{2,1,0:T(8,128)(2,1)S(1)}, u32[]{:S(2)}, u32[]{:S(2)}) collective-permute-start(bf16[16,64,256]{2,1,0:T(8,128)(2,1)S(1)} %collective-permute-done.10), channel_id=1, source_target_pairs={{0,2},{2,0},{4,6},{6,4},{8,10},{10,8},{12,14},{14,12},{16,18},{18,... | collective-permute-start | bytes 1572872 | tf_op jit(solution)/shard_map/ppermute | solution.py:242
  161.7 2.7 collective-permute-start.8
  166.8 30.9 %all-to-all-start.3 = ((bf16[16,64,512]{2,1,0:T(8,128)(2,1)}), bf16[16,64,512]{2,1,0:T(8,128)(2,1)S(1)}, u32[]{:S(2)}, u32[]{:S(2)}) async-start(bf16[16,64,512]{2,1,0:T(8,128)(2,1)} %add_convert_fusion.2), calls=%async_computation.3 | async-start | bytes 2097152 | tf_op jit(solution)/shard_map/all_to_all | solution.py:232
  175.1 27.1 %collective-permute-start.15 = (bf16[1024,512]{1,0:T(8,128)(2,1)}, bf16[1024,512]{1,0:T(8,128)(2,1)}, u32[]{:S(2)}, u32[]{:S(2)}) collective-permute-start(bf16[1024,512]{1,0:T(8,128)(2,1)} %constant_dynamic-slice_fusion.2), channel_id=1, source_target_pairs={{0,1},{1,0},{2,3},{3,2},{4,5},{5,4},{6,7},{7,6},{8,9},{9,8},{10,11... | collective-permute-start | bytes 3145736 | tf_op jit(solution)/shard_map/ppermute | solution.py:277
  177.0 23.4 %copy-start.4 = (bf16[8,2,64,512]{3,0,1,2:T(8,128)(2,1)}, bf16[8,2,64,512]{3,0,1,2:T(8,128)(2,1)S(1)}, u32[]{:S(2)}) copy-start(bf16[8,2,64,512]{3,0,1,2:T(8,128)(2,1)S(1)} %copy.292) | copy-start | bytes 3145732
  177.0 31.9 %collective-permute-start.13 = (bf16[8,1024]{1,0:T(8,128)(2,1)S(1)}, bf16[8,1024]{1,0:T(8,128)(2,1)S(1)}, u32[]{:S(2)}, u32[]{:S(2)}) collective-permute-start(bf16[8,1024]{1,0:T(8,128)(2,1)S(1)} %bitcast.236), channel_id=1, source_target_pairs={{2,0},{4,2},{6,4},{8,6},{10,8},{12,10},{14,12},{16,14},{18,16},{20... | collective-permute-start | bytes 49160 | tf_op jit(solution)/shard_map/ppermute | solution.py:293
  200.4 9.1 %copy-start.5 = (bf16[8,2,64,512]{3,0,1,2:T(8,128)(2,1)}, bf16[8,2,64,512]{3,0,1,2:T(8,128)(2,1)S(1)}, u32[]{:S(2)}) copy-start(bf16[8,2,64,512]{3,0,1,2:T(8,128)(2,1)S(1)} %copy.291) | copy-start | bytes 3145732
  200.9 6.9 %collective-permute-start.14 = (bf16[128,8]{0,1:T(8,128)(2,1)S(1)}, bf16[128,8]{0,1:T(8,128)(2,1)S(1)}, u32[]{:S(2)}, u32[]{:S(2)}) collective-permute-start(bf16[128,8]{0,1:T(8,128)(2,1)S(1)} %maximum_select_fusion), channel_id=1, source_target_pairs={{0,1},{1,0},{2,3},{3,2},{4,5},{5,4},{6,7},{7,6},{8,9},{9,8},{10,11... | collective-permute-start | bytes 6152 | tf_op jit(solution)/shard_map/ppermute | solution.py:299
  204.3 4.6 %collective-permute-start.12 = (bf16[8,1024]{1,0:T(8,128)(2,1)S(1)}, bf16[8,1024]{1,0:T(8,128)(2,1)S(1)}, u32[]{:S(2)}, u32[]{:S(2)}) collective-permute-start(bf16[8,1024]{1,0:T(8,128)(2,1)S(1)} %bitcast.237), channel_id=1, source_target_pairs={{0,2},{2,4},{4,6},{6,8},{8,10},{10,12},{12,14},{14,16},{16,18},{18... | collective-permute-start | bytes 49160 | tf_op jit(solution)/shard_map/ppermute | solution.py:293
  225.9 6.6 %collective-permute-start.18 = (f32[128,8]{0,1:T(8,128)S(1)}, f32[128,8]{0,1:T(8,128)S(1)}, u32[]{:S(2)}, u32[]{:S(2)}) collective-permute-start(f32[128,8]{0,1:T(8,128)S(1)} %bitcast.244), channel_id=1, source_target_pairs={{0,1},{1,0},{2,3},{3,2},{4,5},{5,4},{6,7},{7,6},{8,9},{9,8},{10,11... | collective-permute-start | bytes 12296 | tf_op jit(solution)/shard_map/ppermute | solution.py:299
  226.1 7.5 %collective-permute-start.17 = (f32[8,1024]{1,0:T(8,128)S(1)}, f32[8,1024]{1,0:T(8,128)S(1)}, u32[]{:S(2)}, u32[]{:S(2)}) collective-permute-start(f32[8,1024]{1,0:T(8,128)S(1)} %get-tuple-element.49), channel_id=1, source_target_pairs={{2,0},{4,2},{6,4},{8,6},{10,8},{12,10},{14,12},{16,14},{18,16},{20... | collective-permute-start | bytes 98312 | tf_op jit(solution)/shard_map/ppermute | solution.py:293
  229.7 3.9 collective-permute-start.16
  239.9 31.9 %all-to-all-start.5 = ((bf16[16,128,256]{2,1,0:T(8,128)(2,1)}), bf16[16,128,256]{2,1,0:T(8,128)(2,1)S(1)}, u32[]{:S(2)}, u32[]{:S(2)}) async-start(bf16[16,128,256]{2,1,0:T(8,128)(2,1)} %rim_lines.3), calls=%async_computation.5 | async-start | bytes 2097152 | tf_op jit(solution)/shard_map/all_to_all | solution.py:232
  271.8 29.9 %all-to-all-start.4 = ((bf16[16,128,256]{2,1,0:T(8,128)(2,1)}), bf16[16,128,256]{2,1,0:T(8,128)(2,1)}, u32[]{:S(2)}, u32[]{:S(2)}) async-start(bf16[16,128,256]{2,1,0:T(8,128)(2,1)} %rim_lines.2), calls=%async_computation.4 | async-start | bytes 2097152 | tf_op jit(solution)/shard_map/all_to_all | solution.py:232
  282.8 4.5 %copy-start.7 = (bf16[512,512]{1,0:T(8,128)(2,1)S(1)}, bf16[512,512]{1,0:T(8,128)(2,1)}, u32[]{:S(2)}) copy-start(bf16[512,512]{1,0:T(8,128)(2,1)} %get-tuple-element.24) | copy-start | bytes 1572868
  285.4 64.8 %collective-permute-start.23 = (bf16[16,64,256]{2,1,0:T(8,128)(2,1)}, bf16[16,64,256]{2,1,0:T(8,128)(2,1)}, u32[]{:S(2)}, u32[]{:S(2)}) collective-permute-start(bf16[16,64,256]{2,1,0:T(8,128)(2,1)} %get-tuple-element.33), channel_id=1, source_target_pairs={{0,1},{1,0},{2,3},{3,2},{4,5},{5,4},{6,7},{7,6},{8,9},{9,8},{10,11... | collective-permute-start | bytes 1572872 | tf_op jit(solution)/shard_map/ppermute | solution.py:240
  286.6 66.6 %collective-permute-start.22 = (bf16[16,64,256]{2,1,0:T(8,128)(2,1)}, bf16[16,64,256]{2,1,0:T(8,128)(2,1)}, u32[]{:S(2)}, u32[]{:S(2)}) collective-permute-start(bf16[16,64,256]{2,1,0:T(8,128)(2,1)} %get-tuple-element.33), channel_id=1, source_target_pairs={{0,2},{2,0},{4,6},{6,4},{8,10},{10,8},{12,14},{14,12},{16,18},{18,... | collective-permute-start | bytes 1572872 | tf_op jit(solution)/shard_map/ppermute | solution.py:241
  313.3 13.7 %collective-permute-start.29 = (bf16[16,64,256]{2,1,0:T(8,128)(2,1)S(1)}, bf16[16,64,256]{2,1,0:T(8,128)(2,1)S(1)}, u32[]{:S(2)}, u32[]{:S(2)}) collective-permute-start(bf16[16,64,256]{2,1,0:T(8,128)(2,1)S(1)} %copy-done.13), channel_id=1, source_target_pairs={{0,1},{1,0},{2,3},{3,2},{4,5},{5,4},{6,7},{7,6},{8,9},{9,8},{10,11... | collective-permute-start | bytes 1572872 | tf_op jit(solution)/shard_map/ppermute | solution.py:240
  314.5 25.4 %collective-permute-start.28 = (bf16[16,64,256]{2,1,0:T(8,128)(2,1)S(1)}, bf16[16,64,256]{2,1,0:T(8,128)(2,1)S(1)}, u32[]{:S(2)}, u32[]{:S(2)}) collective-permute-start(bf16[16,64,256]{2,1,0:T(8,128)(2,1)S(1)} %copy-done.13), channel_id=1, source_target_pairs={{0,2},{2,0},{4,6},{6,4},{8,10},{10,8},{12,14},{14,12},{16,18},{18,... | collective-permute-start | bytes 1572872 | tf_op jit(solution)/shard_map/ppermute | solution.py:241
  314.6 23.7 %collective-permute-start.26 = (bf16[16,64,256]{2,1,0:T(8,128)(2,1)S(1)}, bf16[16,64,256]{2,1,0:T(8,128)(2,1)S(1)}, u32[]{:S(2)}, u32[]{:S(2)}) collective-permute-start(bf16[16,64,256]{2,1,0:T(8,128)(2,1)S(1)} %get-tuple-element.30), channel_id=1, source_target_pairs={{0,1},{1,0},{2,3},{3,2},{4,5},{5,4},{6,7},{7,6},{8,9},{9,8},{10,11... | collective-permute-start | bytes 1572872 | tf_op jit(solution)/shard_map/ppermute | solution.py:240
  315.2 12.6 %copy-start.6 = (bf16[512,512]{1,0:T(8,128)(2,1)S(1)}, bf16[512,512]{1,0:T(8,128)(2,1)}, u32[]{:S(2)}) copy-start(bf16[512,512]{1,0:T(8,128)(2,1)} %get-tuple-element.26) | copy-start | bytes 1572868
  327.0 14.3 %collective-permute-start.25 = (bf16[16,64,256]{2,1,0:T(8,128)(2,1)S(1)}, bf16[16,64,256]{2,1,0:T(8,128)(2,1)S(1)}, u32[]{:S(2)}, u32[]{:S(2)}) collective-permute-start(bf16[16,64,256]{2,1,0:T(8,128)(2,1)S(1)} %get-tuple-element.30), channel_id=1, source_target_pairs={{0,2},{2,0},{4,6},{6,4},{8,10},{10,8},{12,14},{14,12},{16,18},{18,... | collective-permute-start | bytes 1572872 | tf_op jit(solution)/shard_map/ppermute | solution.py:241
  338.2 13.8 %collective-permute-start.20 = (bf16[16,64,256]{2,1,0:T(8,128)(2,1)}, bf16[16,64,256]{2,1,0:T(8,128)(2,1)S(1)}, u32[]{:S(2)}, u32[]{:S(2)}) collective-permute-start(bf16[16,64,256]{2,1,0:T(8,128)(2,1)} %get-tuple-element.31), channel_id=1, source_target_pairs={{0,1},{1,0},{2,3},{3,2},{4,5},{5,4},{6,7},{7,6},{8,9},{9,8},{10,11... | collective-permute-start | bytes 1572872 | tf_op jit(solution)/shard_map/ppermute | solution.py:240
  340.0 2.5 collective-permute-start.27
  341.3 2.0 collective-permute-start.30
  342.4 12.3 %collective-permute-start.19 = (bf16[16,64,256]{2,1,0:T(8,128)(2,1)}, bf16[16,64,256]{2,1,0:T(8,128)(2,1)}, u32[]{:S(2)}, u32[]{:S(2)}) collective-permute-start(bf16[16,64,256]{2,1,0:T(8,128)(2,1)} %get-tuple-element.31), channel_id=1, source_target_pairs={{0,2},{2,0},{4,6},{6,4},{8,10},{10,8},{12,14},{14,12},{16,18},{18,... | collective-permute-start | bytes 1572872 | tf_op jit(solution)/shard_map/ppermute | solution.py:241
  345.1 29.9 %all-to-all-start.7 = ((bf16[16,64,512]{2,1,0:T(8,128)(2,1)}), bf16[16,64,512]{2,1,0:T(8,128)(2,1)S(1)}, u32[]{:S(2)}, u32[]{:S(2)}) async-start(bf16[16,64,512]{2,1,0:T(8,128)(2,1)} %add_convert_fusion), calls=%async_computation.7 | async-start | bytes 2097152 | tf_op jit(solution)/shard_map/all_to_all | solution.py:232
  351.6 5.2 %collective-permute-start.24 = (bf16[16,64,256]{2,1,0:T(8,128)(2,1)}, bf16[16,64,256]{2,1,0:T(8,128)(2,1)S(1)}, u32[]{:S(2)}, u32[]{:S(2)}) collective-permute-start(bf16[16,64,256]{2,1,0:T(8,128)(2,1)} %collective-permute-done.23), channel_id=1, source_target_pairs={{0,2},{2,0},{4,6},{6,4},{8,10},{10,8},{12,14},{14,12},{16,18},{18,... | collective-permute-start | bytes 1572872 | tf_op jit(solution)/shard_map/ppermute | solution.py:242
  352.0 4.3 %collective-permute-start.21 = (bf16[16,64,256]{2,1,0:T(8,128)(2,1)S(1)}, bf16[16,64,256]{2,1,0:T(8,128)(2,1)S(1)}, u32[]{:S(2)}, u32[]{:S(2)}) collective-permute-start(bf16[16,64,256]{2,1,0:T(8,128)(2,1)S(1)} %collective-permute-done.20), channel_id=1, source_target_pairs={{0,2},{2,0},{4,6},{6,4},{8,10},{10,8},{12,14},{14,12},{16,18},{18,... | collective-permute-start | bytes 1572872 | tf_op jit(solution)/shard_map/ppermute | solution.py:242
  375.0 5.0 %copy-start.9 = (bf16[16,64,512]{2,1,0:T(8,128)(2,1)}, bf16[16,64,512]{2,1,0:T(8,128)(2,1)S(1)}, u32[]{:S(2)}) copy-start(bf16[16,64,512]{2,1,0:T(8,128)(2,1)S(1)} %all-to-all-done.7.lines) | copy-start | bytes 3145732
  375.0 29.8 %all-to-all-start.6 = ((bf16[16,64,512]{2,1,0:T(8,128)(2,1)}), bf16[16,64,512]{2,1,0:T(8,128)(2,1)S(1)}, u32[]{:S(2)}, u32[]{:S(2)}) async-start(bf16[16,64,512]{2,1,0:T(8,128)(2,1)} %add_convert_fusion.1), calls=%async_computation.6 | async-start | bytes 2097152 | tf_op jit(solution)/shard_map/all_to_all | solution.py:232
  (10 other events, 22.6 us)
Sparse Core Ops, SparseCore 0:
  10.7 63.6 all-gather.2
  76.6 56.5 all-gather.4

commit v5 on v4

--- a/solution.py
+++ b/solution.py
@@ -100,7 +100,7 @@
 def forward_body(*refs):
     starts = refs[:CHUNKS]
     rows_in, sides, innovation, weight, wind_x, wind_y = refs[CHUNKS : CHUNKS + 6]
-    end, flat, row_flux, side_flux, state, carry = refs[CHUNKS + 6 :]
+    end, flat, state, carry = refs[CHUNKS + 6 :]
     step = pl.program_id(0)
     rows, levels, width = flat.shape
     cut = rows // CHUNKS
@@ -129,26 +129,17 @@
         end[rows_j] = after
         misfit = weight[rows_j] * (after - innovation[rows_j])
         p, q = cy * misfit, cx * misfit
-        side_flux[rows_j, :, 0:1] = p[:, :, 0:1]
-        side_flux[rows_j, :, 1:2] = p[:, :, width - 1 : width]
         left = jnp.where(left_edge, 0.0, pltpu.roll(p, 1, 2))
         right = jnp.where(right_edge, 0.0, pltpu.roll(p, width - 1, 2))
         flat_j = misfit + 0.5 * (right - left)
         flat[jnp.maximum(at - 1, 0)] = carry[2] + 0.5 * (q[0] - carry[0])
         flat[at] = flat_j[0] + 0.5 * (q[1] - carry[1])
         flat[pl.ds(at + 1, GROUP - 2)] = flat_j[1:-1] + 0.5 * (q[2:] - q[:-2])
-        if j == 0:
-            carry[3] = q[0]
         carry[0], carry[1], carry[2] = q[GROUP - 2], q[GROUP - 1], flat_j[GROUP - 1]
-
-    @pl.when(step == 0)
-    def _():
-        row_flux[0] = carry[3]
 
     @pl.when(step == rows // STEP - 1)
     def _():
         flat[rows - 1] = carry[2] - 0.5 * carry[0]
-        row_flux[1] = carry[1]
 
 
 def forward(starts, rows_in, sides, innovation, weight, wind_x, wind_y):
@@ -162,16 +153,14 @@
         forward_body,
         grid=(rows // STEP,),
         in_specs=[start] * CHUNKS + [pair, side, blocked, blocked, blocked, blocked],
-        out_specs=[blocked, whole, pair, side],
+        out_specs=[blocked, whole],
         out_shape=[
             jax.ShapeDtypeStruct((rows, levels, width), F32),
             jax.ShapeDtypeStruct((rows, levels, width), F32),
-            jax.ShapeDtypeStruct((2, levels, width), F32),
-            jax.ShapeDtypeStruct((rows, levels, 2), F32),
         ],
         scratch_shapes=[
             pltpu.VMEM((rows + 2, levels, width), F32),
-            pltpu.VMEM((4, levels, width), F32),
+            pltpu.VMEM((3, levels, width), F32),
         ],
         compiler_params=PARAMS,
         cost_estimate=cost(30 * innovation.size, *[innovation] * 7),
@@ -232,12 +221,13 @@
     return lax.all_to_all(lines, "gx", 0, 0, tiled=True)
 
 
-def plane_pieces(lines, parts):
+def plane_pieces(lines, parts, after=None):
     n_x, n_y = lax.axis_size("gx"), lax.axis_size("gy")
     groups = [list(range(i, i + parts)) for i in range(0, n_x, parts)]
     if n_y == 2 and parts == 2:
         pairs = [(a, b) for g in groups for a, b in (g, g[::-1])]
-        far = lax.ppermute(lines, "gy", [(0, 1), (1, 0)])
+        sent = lines if after is None else lax.optimization_barrier((lines, after))[0]
+        far = lax.ppermute(sent, "gy", [(0, 1), (1, 0)])
         near = lax.ppermute(lines, "gx", pairs)
         cross = lax.ppermute(far, "gx", pairs)
         return [lines, near, far, cross]
@@ -264,25 +254,32 @@
     ]
 
 
-def filter_columns(filter_y, parts):
+def send_columns(filter_y, parts):
+    width, n_y = filter_y.shape[0], lax.axis_size("gy")
+    part = width // parts
+    sub, me = lax.rem(lax.axis_index("gx"), parts), lax.axis_index("gy")
+    if n_y == 2 and parts == 2:
+        sent = lax.dynamic_slice(
+            filter_y, (0, (1 - me) * width + sub * part), (width, part)
+        )
+        return lax.ppermute(sent, "gy", [(0, 1), (1, 0)])
+    split = filter_y.reshape(width, n_y, parts, part)
+    split = lax.dynamic_index_in_dim(split, sub, axis=2, keepdims=False)
+    return lax.all_to_all(split, "gy", 1, 0, tiled=True)
+
+
+def filter_columns(filter_y, got, parts):
     width, n_y = filter_y.shape[0], lax.axis_size("gy")
     part = width // parts
     sub, me = lax.rem(lax.axis_index("gx"), parts), lax.axis_index("gy")
     order = piece_order(parts)
     if n_y == 2 and parts == 2:
         mine = lax.dynamic_slice(filter_y, (0, me * width + sub * part), (width, part))
-        sent = lax.dynamic_slice(
-            filter_y, (0, (1 - me) * width + sub * part), (width, part)
-        )
-        got = lax.ppermute(sent, "gy", [(0, 1), (1, 0)])
         return [
             lax.dynamic_slice_in_dim(source, s * part, part, axis=0)
             for source, (s, _) in zip((mine, mine, got, got), order)
         ]
-    split = filter_y.reshape(width, n_y, parts, part)
-    split = lax.dynamic_index_in_dim(split, sub, axis=2, keepdims=False)
-    split = lax.all_to_all(split, "gy", 1, 0, tiled=True)
-    split = split.reshape(n_y, parts, part, part)
+    split = got.reshape(n_y, parts, part, part)
     return [split[g, s] for s, g in order]
 
 
@@ -302,6 +299,43 @@
     up = [(i, i + 1) for i in range(n_y - 1)]
     down = [(i + 1, i) for i in range(n_y - 1)]
     return lax.ppermute(last, "gy", up), lax.ppermute(first, "gy", down)
+
+
+def edge_flux(starts, rows_in, before, after, fields):
+    def flux(up, here, down, left, right, fields, wind):
+        innovation, weight, cx, cy = fields
+        end = here - cx * (down - up) * 0.5 - cy * (right - left) * 0.5
+        return fields[wind] * (weight * (end - innovation))
+
+    top = starts[0][:2].astype(F32)
+    bottom = starts[-1][-2:].astype(F32)
+    here = jnp.stack([top[0], bottom[1]])
+    ends = jnp.stack([before[0], before[-1]]), jnp.stack([after[0], after[-1]])
+    row_flux = flux(
+        jnp.stack([rows_in[0], bottom[0]]),
+        here,
+        jnp.stack([top[1], rows_in[1]]),
+        jnp.concatenate([ends[0][:, :, None], here[:, :, :-1]], axis=2),
+        jnp.concatenate([here[:, :, 1:], ends[1][:, :, None]], axis=2),
+        [jnp.stack([f[0], f[-1]]) for f in fields],
+        2,
+    )
+    side = [
+        jnp.concatenate([s[:, :, at] for s in starts]).astype(F32)
+        for at in (0, 1, -2, -1)
+    ]
+    here = jnp.stack([side[0], side[3]])
+    halo = jnp.stack([rows_in[:, :, 0], rows_in[:, :, -1]])
+    side_flux = flux(
+        jnp.concatenate([halo[:, :1], here[:, :-1]], axis=1),
+        here,
+        jnp.concatenate([here[:, 1:], halo[:, 1:]], axis=1),
+        jnp.stack([before, side[2]]),
+        jnp.stack([side[1], after]),
+        [jnp.stack([f[:, :, 0], f[:, :, -1]]) for f in fields],
+        3,
+    )
+    return row_flux, side_flux
 
 
 def per_device(control, innovation, obs_weight, courant_x, courant_y, filter_x, filter_y):
@@ -333,7 +367,7 @@
         start = start.astype(BF16)
         if h == CHUNKS - 1:
             start, filter_y = lax.optimization_barrier((start, filter_y))
-            columns_y = filter_columns(filter_y, parts)
+            columns_y = send_columns(filter_y, parts)
         came = swap_all(start).reshape(levels, parts, cut, part)
         came = came.transpose(2, 0, 1, 3).reshape(cut, levels, width)
         starts.append(came)
@@ -343,14 +377,16 @@
         jnp.concatenate([s[:, :, 0] for s in starts]),
         jnp.concatenate([s[:, :, -1] for s in starts]),
     )
-    sides = jnp.stack([before, after], axis=2).astype(F32)
-    end_state, flat, row_flux, side_flux = forward(
-        starts, rows_in, sides, innovation, obs_weight, courant_x, courant_y
+    before, after = before.astype(F32), after.astype(F32)
+    fields = (innovation, obs_weight, courant_x, courant_y)
+    row_flux, side_flux = edge_flux(starts, rows_in, before, after, fields)
+    end_state, flat = forward(
+        starts, rows_in, jnp.stack([before, after], axis=2), *fields
     )
     rows_in = row_halo(row_flux[0], row_flux[1])
-    before, after = side_halo(side_flux[:, :, 0], side_flux[:, :, 1])
-    sides = jnp.stack([before, after], axis=2)
+    sides = jnp.stack(side_halo(side_flux[0], side_flux[1]), axis=2)
     flat, columns_y = lax.optimization_barrier((flat, columns_y))
+    columns_y = filter_columns(filter_y, columns_y, parts)
 
     pulled = []
     for w in range(CHUNKS):
@@ -365,11 +401,14 @@
                 preferred_element_type=F32,
             )
         pulled.append(total.astype(BF16).reshape(n_x, CHUNKS, cut, piece))
-    gradient = None
+    gradient = far = None
     for h in range(CHUNKS):
         carried = 0.0
         for w, span in enumerate(spans):
-            for plane, matrix in zip(plane_pieces(pulled[w][:, h], parts), columns_y):
+            held = far if h > 0 and w == CHUNKS - 1 else None
+            planes = plane_pieces(pulled[w][:, h], parts, held)
+            far = planes[-2] if w == CHUNKS - 1 else far
+            for plane, matrix in zip(planes, columns_y):
                 carried = carried + jnp.einsum(
                     "brk,kc->brc", plane, matrix[span], preferred_element_type=F32
                 )

time: 417 us -> 421 us (level)
  waiting for transfers between devices: 163 us -> 143 us
  starting transfers between devices: 73.1 us -> 83.5 us
  matrix products: 51.7 us -> 60.9 us
    ppermute x9, waiting for transfers between devices: 50.2 us -> 33.6 us  [the longest x8 33.6 us: plane_pieces(): far = lax.ppermute(sent, 'gy', [(0, 1), (1, 0)])]
    all_to_all x7, starting transfers between devices: 40.4 us -> 51.1 us  [swap_all(): return lax.all_to_all(lines, 'gx', 0, 0, tiled=True)]
    dot_general x16, matrix products: 15.5 us -> 24.8 us  [per_device(): jnp.einsum('brk,kc->brc', plane, matrix[span], preferred_element_type=F32)]
    slice x0 -> x22, local copies, waits for them, and re-layouts: none -> 8.96 us  [the longest x4 5.7 us: edge_flux(): f[:, :, 0]]
    dynamic_slice x3 -> x1, local copies, waits for them, and re-layouts: 7.11 us -> 2.28 us  [send_columns(): lax.dynamic_slice(filter_y, (0, (1 - me) * width + sub * part), (width, p...]
    all_to_all x7, waiting for transfers between devices: 108 us -> 103 us  [swap_all(): return lax.all_to_all(lines, 'gx', 0, 0, tiled=True)]
  transfers between devices with their start and end apart: 40 -> 40, of which waited for: 15 -> 14; matrix products, arithmetic and copies ran while one was open for 17% -> 21% of each run, Pallas kernels for 4% -> 8%
where the time goes in v5:
time: 421 us; the launch traced here: 417 us
  waiting for transfers between devices  143 us (34%)
  starting transfers between devices  83.5 us (20%)
  matrix products  60.9 us (14%)
  blocking collectives  44.1 us (10%)
  Pallas kernels  41.3 us (10%)
  local copies, waits for them, and re-layouts  27.5 us (7%)
  between operations  15.2 us (4%)
    all_to_all x7, waiting for transfers between devices, swap_all(): return lax.all_to_all(lines, 'gx', 0, 0, tiled=True)  103 us
    all_to_all x7, starting transfers between devices, swap_all(): return lax.all_to_all(lines, 'gx', 0, 0, tiled=True)  51.1 us
    all_to_all x1, blocking collectives, swap_all(): return lax.all_to_all(lines, 'gx', 0, 0, tiled=True)  44.1 us
    ppermute x8, waiting for transfers between devices, plane_pieces(): far = lax.ppermute(sent, 'gy', [(0, 1), (1, 0)])  33.6 us
    dot_general x16, matrix products, per_device(): jnp.einsum('brk,kc->brc', plane, matrix[span], preferred_element_type=F32)  24.8 us
    pallas_call x1, Pallas kernels, forward(): pl.pallas_call(forward_body, grid=(rows // STEP,), in_specs=[start] * CHU...  14.2 us
    dot_general x16, matrix products, per_device(): jnp.einsum('brc,kc->brk', plane, matrix[:, span], preferred_element_type=...  12.5 us
    dot_general x4, matrix products, per_device(): smoothed = jnp.dot(matrix_x[h], lines[w], preferred_element_type=F32)  11.9 us
  transfers between devices with their start and end apart: 40, of which 14 were waited for; matrix products, arithmetic and copies ran while one was open for 21% of the time, Pallas kernels for 8%

profile of v5, /device:TPU:9, one launch (start us, length us, event | category | flops | bytes accessed | tf_op | source)
XLA Modules:
  0.0 417.1 jit_solution(2503799989560280639)
XLA Ops:
  9.0 4.8 %as_lines.3 = bf16[16,128,256]{2,1,0:T(8,128)(2,1)} custom-call(bf16[128,8,1024]{2,1,0:T(8,128)(2,1)} %control.3), custom_call_target="tpu_custom_call" | custom-call | bytes 4194304 | tf_op jit(solution)/shard_map/as_lines/pallas_call | solution.py:53
  13.8 44.1 %all_to_all.40 = bf16[16,128,256]{2,1,0:T(8,128)(2,1)S(1)} all-to-all(bf16[16,128,256]{2,1,0:T(8,128)(2,1)} %as_lines.3), channel_id=1, replica_groups=mesh['gx'=16,'gy'=2] {'gx'}, dimensions={0} | all-to-all | bytes 2097152 | tf_op jit(solution)/shard_map/all_to_all | solution.py:221
  58.6 4.8 %as_lines.2 = bf16[16,128,256]{2,1,0:T(8,128)(2,1)} custom-call(bf16[128,8,1024]{2,1,0:T(8,128)(2,1)} %control.3), custom_call_target="tpu_custom_call" | custom-call | bytes 4194304 | tf_op jit(solution)/shard_map/as_lines/pallas_call | solution.py:53
  63.4 7.1 %all-to-all-start = ((bf16[16,128,256]{2,1,0:T(8,128)(2,1)}), bf16[16,128,256]{2,1,0:T(8,128)(2,1)S(1)}, u32[]{:S(2)}, u32[]{:S(2)}) async-start(bf16[16,128,256]{2,1,0:T(8,128)(2,1)} %as_lines.2), calls=%async_computation | async-start | bytes 2097152 | tf_op jit(solution)/shard_map/all_to_all | solution.py:221
  72.4 2.1 all-gather.3.cloned.1.call-done
  74.4 3.5 fusion.4
  79.9 23.9 %all-to-all-done = bf16[16,128,256]{2,1,0:T(8,128)(2,1)S(1)} async-done(((bf16[16,128,256]{2,1,0:T(8,128)(2,1)}), bf16[16,128,256]{2,1,0:T(8,128)(2,1)S(1)}, u32[]{:S(2)}, u32[]{:S(2)}) %all-to-all-start) | async-done | bytes 1048608 | tf_op jit(solution)/shard_map/all_to_all | solution.py:221
  103.8 3.6 convolution_convert_fusion.3
  109.7 11.6 %collective-permute-done.1 = bf16[16,64,256]{2,1,0:T(8,128)(2,1)S(1)} collective-permute-done((bf16[16,64,256]{2,1,0:T(8,128)(2,1)S(1)}, bf16[16,64,256]{2,1,0:T(8,128)(2,1)S(1)}, u32[]{:S(2)}, u32[]{:S(2)}) %collective-permute-start.1) | collective-permute-done | bytes 524320 | tf_op jit(solution)/shard_map/ppermute | solution.py:230
  126.4 1.9 add_convert_fusion.3
  128.2 15.9 %all-to-all-start.2 = ((bf16[16,64,512]{2,1,0:T(8,128)(2,1)}), bf16[16,64,512]{2,1,0:T(8,128)(2,1)S(1)}, u32[]{:S(2)}, u32[]{:S(2)}) async-start(bf16[16,64,512]{2,1,0:T(8,128)(2,1)} %add_convert_fusion.3), calls=%async_computation.2 | async-start | bytes 2097152 | tf_op jit(solution)/shard_map/all_to_all | solution.py:221
  144.2 3.6 convolution_convert_fusion
  152.5 8.5 %collective-permute-done.10 = bf16[16,64,256]{2,1,0:T(8,128)(2,1)S(1)} collective-permute-done((bf16[16,64,256]{2,1,0:T(8,128)(2,1)S(1)}, bf16[16,64,256]{2,1,0:T(8,128)(2,1)S(1)}, u32[]{:S(2)}, u32[]{:S(2)}) %collective-permute-start.10) | collective-permute-done | bytes 524320 | tf_op jit(solution)/shard_map/ppermute | solution.py:230
  161.4 2.0 collective-permute-start.11
  163.5 8.7 %collective-permute-done.7 = bf16[16,64,256]{2,1,0:T(8,128)(2,1)S(1)} collective-permute-done((bf16[16,64,256]{2,1,0:T(8,128)(2,1)S(1)}, bf16[16,64,256]{2,1,0:T(8,128)(2,1)S(1)}, u32[]{:S(2)}, u32[]{:S(2)}) %collective-permute-start.7) | collective-permute-done | bytes 524320 | tf_op jit(solution)/shard_map/ppermute | solution.py:230
  175.4 1.9 add_convert_fusion.2
  177.3 6.0 %all-to-all-start.3 = ((bf16[16,64,512]{2,1,0:T(8,128)(2,1)}), bf16[16,64,512]{2,1,0:T(8,128)(2,1)}, u32[]{:S(2)}, u32[]{:S(2)}) async-start(bf16[16,64,512]{2,1,0:T(8,128)(2,1)} %add_convert_fusion.2), calls=%async_computation.3 | async-start | bytes 2097152 | tf_op jit(solution)/shard_map/all_to_all | solution.py:221
  191.2 2.3 collective-permute-start.13
  194.0 2.3 constant_dynamic-slice_fusion
  197.8 10.4 %all-to-all-done.3 = bf16[16,64,512]{2,1,0:T(8,128)(2,1)} async-done(((bf16[16,64,512]{2,1,0:T(8,128)(2,1)}), bf16[16,64,512]{2,1,0:T(8,128)(2,1)}, u32[]{:S(2)}, u32[]{:S(2)}) %all-to-all-start.3) | async-done | bytes 1048608 | tf_op jit(solution)/shard_map/all_to_all | solution.py:221
  208.3 1.8 copy.565
  210.1 3.2 collective-permute-start.12
  215.8 4.1 collective-permute-done.14
  223.6 14.2 %forward.1 = (f32[128,8,1024]{2,1,0:T(8,128)}, f32[128,8,1024]{2,1,0:T(8,128)}) custom-call(bf16[64,8,1024]{2,1,0:T(8,128)(2,1)} %bitcast.231, bf16[64,8,1024]{2,1,0:T(8,128)(2,1)} %bitcast.235, f32[2,8,1024]{2,1,0:T(8,128)} %copy-done.8, f32[128,8,2]{2,1,0:T(8,128)} %copy.510.refs_3_, f32[128,8,1024]{2,1,0:T(8,128)} %refs_4_.1, f32[128,8,1024]{2,1,0:T(8,128)} %refs_5_.1, ...), custom_call_target="tpu_custom_call" | custom-call | flops 31457280 | bytes 29360128 | tf_op jit(solution)/shard_map/forward/pallas_call | solution.py:152
  237.7 4.3 %collective-permute-start.17 = (f32[8,1024]{1,0:T(8,128)S(1)}, f32[8,1024]{1,0:T(8,128)S(1)}, u32[]{:S(2)}, u32[]{:S(2)}) collective-permute-start(f32[8,1024]{1,0:T(8,128)S(1)} %get-tuple-element.59), channel_id=1, source_target_pairs={{2,0},{4,2},{6,4},{8,6},{10,8},{12,10},{14,12},{16,14},{18,16},{20... | collective-permute-start | bytes 98312 | tf_op jit(solution)/shard_map/ppermute | solution.py:290
  242.1 3.0 collective-permute-start.16
  246.8 5.7 %rim_lines.2 = bf16[16,128,256]{2,1,0:T(8,128)(2,1)} custom-call(f32[128,8,1024]{2,1,0:T(8,128)} %get-tuple-element.17.flat, f32[2,8,1024]{2,1,0:T(8,128)} %pad_maximum_fusion.2.rows_in, f32[128,8,2]{2,1,0:T(8,128)} %copy.535.sides), custom_call_target="tpu_custom_call" | custom-call | flops 4194304 | bytes 8388608 | tf_op jit(solution)/shard_map/rim_lines/pallas_call | solution.py:203
  252.5 7.0 %all-to-all-start.4 = ((bf16[16,128,256]{2,1,0:T(8,128)(2,1)}), bf16[16,128,256]{2,1,0:T(8,128)(2,1)S(1)}, u32[]{:S(2)}, u32[]{:S(2)}) async-start(bf16[16,128,256]{2,1,0:T(8,128)(2,1)} %rim_lines.2), calls=%async_computation.4 | async-start | bytes 2097152 | tf_op jit(solution)/shard_map/all_to_all | solution.py:221
  259.5 5.7 %rim_lines.3 = bf16[16,128,256]{2,1,0:T(8,128)(2,1)} custom-call(f32[128,8,1024]{2,1,0:T(8,128)} %get-tuple-element.17.flat, f32[2,8,1024]{2,1,0:T(8,128)} %pad_maximum_fusion.2.rows_in, f32[128,8,2]{2,1,0:T(8,128)} %copy.535.sides), custom_call_target="tpu_custom_call" | custom-call | flops 4194304 | bytes 8388608 | tf_op jit(solution)/shard_map/rim_lines/pallas_call | solution.py:203
  265.1 19.2 %all-to-all-done.4 = bf16[16,128,256]{2,1,0:T(8,128)(2,1)S(1)} async-done(((bf16[16,128,256]{2,1,0:T(8,128)(2,1)}), bf16[16,128,256]{2,1,0:T(8,128)(2,1)S(1)}, u32[]{:S(2)}, u32[]{:S(2)}) %all-to-all-start.4) | async-done | bytes 1048608 | tf_op jit(solution)/shard_map/all_to_all | solution.py:221
  284.3 5.0 %all-to-all-start.5 = ((bf16[16,128,256]{2,1,0:T(8,128)(2,1)}), bf16[16,128,256]{2,1,0:T(8,128)(2,1)S(1)}, u32[]{:S(2)}, u32[]{:S(2)}) async-start(bf16[16,128,256]{2,1,0:T(8,128)(2,1)} %rim_lines.3), calls=%async_computation.5 | async-start | bytes 2097152 | tf_op jit(solution)/shard_map/all_to_all | solution.py:221
  289.4 3.6 fusion.80
  293.1 2.2 fusion.3
  300.2 13.9 %all-to-all-done.5 = bf16[16,128,256]{2,1,0:T(8,128)(2,1)S(1)} async-done(((bf16[16,128,256]{2,1,0:T(8,128)(2,1)}), bf16[16,128,256]{2,1,0:T(8,128)(2,1)S(1)}, u32[]{:S(2)}, u32[]{:S(2)}) %all-to-all-start.5) | async-done | bytes 1048608 | tf_op jit(solution)/shard_map/all_to_all | solution.py:221
  314.2 3.6 fusion.81
  317.9 2.2 fusion.2
  322.7 2.8 fusion.26
  325.5 2.9 fusion.30
  331.5 4.8 %collective-permute-done.23 = bf16[16,64,256]{2,1,0:T(8,128)(2,1)S(1)} collective-permute-done((bf16[16,64,256]{2,1,0:T(8,128)(2,1)S(1)}, bf16[16,64,256]{2,1,0:T(8,128)(2,1)S(1)}, u32[]{:S(2)}, u32[]{:S(2)}) %collective-permute-start.23) | collective-permute-done | bytes 524320 | tf_op jit(solution)/shard_map/ppermute | solution.py:230
  344.2 1.8 add_convert_fusion
  346.0 5.2 %all-to-all-start.7 = ((bf16[16,64,512]{2,1,0:T(8,128)(2,1)}), bf16[16,64,512]{2,1,0:T(8,128)(2,1)S(1)}, u32[]{:S(2)}, u32[]{:S(2)}) async-start(bf16[16,64,512]{2,1,0:T(8,128)(2,1)} %add_convert_fusion), calls=%async_computation.7 | async-start | bytes 2097152 | tf_op jit(solution)/shard_map/all_to_all | solution.py:221
  354.3 1.7 fusion.28
  359.9 1.8 add_convert_fusion.1
  361.6 14.3 %all-to-all-done.7.lines = bf16[16,64,512]{2,1,0:T(8,128)(2,1)S(1)} async-done(((bf16[16,64,512]{2,1,0:T(8,128)(2,1)}), bf16[16,64,512]{2,1,0:T(8,128)(2,1)S(1)}, u32[]{:S(2)}, u32[]{:S(2)}) %all-to-all-start.7) | async-done | bytes 1048608 | tf_op jit(solution)/shard_map/all_to_all | solution.py:221
  376.0 5.0 %all-to-all-start.6 = ((bf16[16,64,512]{2,1,0:T(8,128)(2,1)}), bf16[16,64,512]{2,1,0:T(8,128)(2,1)S(1)}, u32[]{:S(2)}, u32[]{:S(2)}) async-start(bf16[16,64,512]{2,1,0:T(8,128)(2,1)} %add_convert_fusion.1), calls=%async_computation.6 | async-start | bytes 2097152 | tf_op jit(solution)/shard_map/all_to_all | solution.py:221
  380.9 3.1 add_lines.2.rest_0_
  384.0 21.8 %all-to-all-done.6.lines = bf16[16,64,512]{2,1,0:T(8,128)(2,1)S(1)} async-done(((bf16[16,64,512]{2,1,0:T(8,128)(2,1)}), bf16[16,64,512]{2,1,0:T(8,128)(2,1)S(1)}, u32[]{:S(2)}, u32[]{:S(2)}) %all-to-all-start.6) | async-done | bytes 1048608 | tf_op jit(solution)/shard_map/all_to_all | solution.py:221
  406.8 3.1 add_lines.3
  (181 shorter events, 66.2 us)
Async XLA Ops:
  7.2 67.3 %all-gather.3.cloned.1.call-start = ((), (), s32[]{:S(2)}) async-start(), calls=%async_computation.8 | async-start | bytes 4456448 | tf_op jit(solution)/shard_map/all_gather | solution.py:350
  8.9 49.0 %copy-start.9 = (bf16[128,2048]{1,0:T(8,128)(2,1)S(1)}, bf16[128,2048]{1,0:T(8,128)(2,1)}, u32[]{:S(2)}) copy-start(bf16[128,2048]{1,0:T(8,128)(2,1)} %param.12) | copy-start | bytes 1572868
  8.9 135.2 %all-gather.5.cloned.1.call-start = ((), (), s32[]{:S(2)}) async-start(), calls=%async_computation.9 | async-start | bytes 4456448 | tf_op jit(solution)/shard_map/all_gather | solution.py:356
  63.4 40.4 %all-to-all-start = ((bf16[16,128,256]{2,1,0:T(8,128)(2,1)}), bf16[16,128,256]{2,1,0:T(8,128)(2,1)S(1)}, u32[]{:S(2)}, u32[]{:S(2)}) async-start(bf16[16,128,256]{2,1,0:T(8,128)(2,1)} %as_lines.2), calls=%async_computation | async-start | bytes 2097152 | tf_op jit(solution)/shard_map/all_to_all | solution.py:221
  78.1 43.7 %collective-permute-start.4 = (bf16[16,64,256]{2,1,0:T(8,128)(2,1)S(1)}, bf16[16,64,256]{2,1,0:T(8,128)(2,1)}, u32[]{:S(2)}, u32[]{:S(2)}) collective-permute-start(bf16[16,64,256]{2,1,0:T(8,128)(2,1)S(1)} %bitcast.239), channel_id=1, source_target_pairs={{0,1},{1,0},{2,3},{3,2},{4,5},{5,4},{6,7},{7,6},{8,9},{9,8},{10,11... | collective-permute-start | bytes 1572872 | tf_op jit(solution)/shard_map/ppermute | solution.py:230
  79.4 44.9 %collective-permute-start.3 = (bf16[16,64,256]{2,1,0:T(8,128)(2,1)S(1)}, bf16[16,64,256]{2,1,0:T(8,128)(2,1)}, u32[]{:S(2)}, u32[]{:S(2)}) collective-permute-start(bf16[16,64,256]{2,1,0:T(8,128)(2,1)S(1)} %bitcast.240), channel_id=1, source_target_pairs={{0,2},{2,0},{4,6},{6,4},{8,10},{10,8},{12,14},{14,12},{16,18},{18,... | collective-permute-start | bytes 1572872 | tf_op jit(solution)/shard_map/ppermute | solution.py:231
  103.8 5.0 %copy-start = (bf16[1024,2048]{1,0:T(8,128)(2,1)S(1)}, bf16[1024,2048]{1,0:T(8,128)(2,1)}, u32[]{:S(2)}) copy-start(bf16[1024,2048]{1,0:T(8,128)(2,1)} %param.13) | copy-start | bytes 12582916
  107.4 13.9 %collective-permute-start.1 = (bf16[16,64,256]{2,1,0:T(8,128)(2,1)S(1)}, bf16[16,64,256]{2,1,0:T(8,128)(2,1)S(1)}, u32[]{:S(2)}, u32[]{:S(2)}) collective-permute-start(bf16[16,64,256]{2,1,0:T(8,128)(2,1)S(1)} %bitcast.252), channel_id=1, source_target_pairs={{0,1},{1,0},{2,3},{3,2},{4,5},{5,4},{6,7},{7,6},{8,9},{9,8},{10,11... | collective-permute-start | bytes 1572872 | tf_op jit(solution)/shard_map/ppermute | solution.py:230
  108.7 15.1 %collective-permute-start = (bf16[16,64,256]{2,1,0:T(8,128)(2,1)S(1)}, bf16[16,64,256]{2,1,0:T(8,128)(2,1)S(1)}, u32[]{:S(2)}, u32[]{:S(2)}) collective-permute-start(bf16[16,64,256]{2,1,0:T(8,128)(2,1)S(1)} %bitcast.253), channel_id=1, source_target_pairs={{0,2},{2,0},{4,6},{6,4},{8,10},{10,8},{12,14},{14,12},{16,18},{18,... | collective-permute-start | bytes 1572872 | tf_op jit(solution)/shard_map/ppermute | solution.py:231
  121.3 4.5 %collective-permute-start.2 = (bf16[16,64,256]{2,1,0:T(8,128)(2,1)S(1)}, bf16[16,64,256]{2,1,0:T(8,128)(2,1)S(1)}, u32[]{:S(2)}, u32[]{:S(2)}) collective-permute-start(bf16[16,64,256]{2,1,0:T(8,128)(2,1)S(1)} %collective-permute-done.1), channel_id=1, source_target_pairs={{0,2},{2,0},{4,6},{6,4},{8,10},{10,8},{12,14},{14,12},{16,18},{18,... | collective-permute-start | bytes 1572872 | tf_op jit(solution)/shard_map/ppermute | solution.py:232
  121.8 4.6 %collective-permute-start.5 = (bf16[16,64,256]{2,1,0:T(8,128)(2,1)}, bf16[16,64,256]{2,1,0:T(8,128)(2,1)S(1)}, u32[]{:S(2)}, u32[]{:S(2)}) collective-permute-start(bf16[16,64,256]{2,1,0:T(8,128)(2,1)} %collective-permute-done.4), channel_id=1, source_target_pairs={{0,2},{2,0},{4,6},{6,4},{8,10},{10,8},{12,14},{14,12},{16,18},{18,... | collective-permute-start | bytes 1572872 | tf_op jit(solution)/shard_map/ppermute | solution.py:232
  128.2 49.0 %all-to-all-start.2 = ((bf16[16,64,512]{2,1,0:T(8,128)(2,1)}), bf16[16,64,512]{2,1,0:T(8,128)(2,1)S(1)}, u32[]{:S(2)}, u32[]{:S(2)}) async-start(bf16[16,64,512]{2,1,0:T(8,128)(2,1)} %add_convert_fusion.3), calls=%async_computation.2 | async-start | bytes 2097152 | tf_op jit(solution)/shard_map/all_to_all | solution.py:221
  144.1 5.6 %copy-start.12 = (bf16[1024,2048]{1,0:T(8,128)(2,1)S(1)}, bf16[1024,2048]{1,0:T(8,128)(2,1)}, u32[]{:S(2)}) copy-start(bf16[1024,2048]{1,0:T(8,128)(2,1)} %all-gather.5.cloned.1.call-done) | copy-start | bytes 12582916
  147.7 3.8 copy-start.1
  147.8 13.2 %collective-permute-start.10 = (bf16[16,64,256]{2,1,0:T(8,128)(2,1)S(1)}, bf16[16,64,256]{2,1,0:T(8,128)(2,1)S(1)}, u32[]{:S(2)}, u32[]{:S(2)}) collective-permute-start(bf16[16,64,256]{2,1,0:T(8,128)(2,1)S(1)} %bitcast.246), channel_id=1, source_target_pairs={{0,1},{1,0},{2,3},{3,2},{4,5},{5,4},{6,7},{7,6},{8,9},{9,8},{10,11... | collective-permute-start | bytes 1572872 | tf_op jit(solution)/shard_map/ppermute | solution.py:230
  149.1 24.8 %collective-permute-start.9 = (bf16[16,64,256]{2,1,0:T(8,128)(2,1)S(1)}, bf16[16,64,256]{2,1,0:T(8,128)(2,1)S(1)}, u32[]{:S(2)}, u32[]{:S(2)}) collective-permute-start(bf16[16,64,256]{2,1,0:T(8,128)(2,1)S(1)} %bitcast.247), channel_id=1, source_target_pairs={{0,2},{2,0},{4,6},{6,4},{8,10},{10,8},{12,14},{14,12},{16,18},{18,... | collective-permute-start | bytes 1572872 | tf_op jit(solution)/shard_map/ppermute | solution.py:231
  151.0 21.2 %collective-permute-start.7 = (bf16[16,64,256]{2,1,0:T(8,128)(2,1)S(1)}, bf16[16,64,256]{2,1,0:T(8,128)(2,1)S(1)}, u32[]{:S(2)}, u32[]{:S(2)}) collective-permute-start(bf16[16,64,256]{2,1,0:T(8,128)(2,1)S(1)} %bitcast.249), channel_id=1, source_target_pairs={{0,1},{1,0},{2,3},{3,2},{4,5},{5,4},{6,7},{7,6},{8,9},{9,8},{10,11... | collective-permute-start | bytes 1572872 | tf_op jit(solution)/shard_map/ppermute | solution.py:230
  151.3 23.1 %collective-permute-start.6 = (bf16[16,64,256]{2,1,0:T(8,128)(2,1)S(1)}, bf16[16,64,256]{2,1,0:T(8,128)(2,1)S(1)}, u32[]{:S(2)}, u32[]{:S(2)}) collective-permute-start(bf16[16,64,256]{2,1,0:T(8,128)(2,1)S(1)} %bitcast.250), channel_id=1, source_target_pairs={{0,2},{2,0},{4,6},{6,4},{8,10},{10,8},{12,14},{14,12},{16,18},{18,... | collective-permute-start | bytes 1572872 | tf_op jit(solution)/shard_map/ppermute | solution.py:231
  161.4 14.0 %collective-permute-start.11 = (bf16[16,64,256]{2,1,0:T(8,128)(2,1)S(1)}, bf16[16,64,256]{2,1,0:T(8,128)(2,1)S(1)}, u32[]{:S(2)}, u32[]{:S(2)}) collective-permute-start(bf16[16,64,256]{2,1,0:T(8,128)(2,1)S(1)} %collective-permute-done.10), channel_id=1, source_target_pairs={{0,2},{2,0},{4,6},{6,4},{8,10},{10,8},{12,14},{14,12},{16,18},{18,... | collective-permute-start | bytes 1572872 | tf_op jit(solution)/shard_map/ppermute | solution.py:232
  172.2 2.7 collective-permute-start.8
  177.3 31.0 %all-to-all-start.3 = ((bf16[16,64,512]{2,1,0:T(8,128)(2,1)}), bf16[16,64,512]{2,1,0:T(8,128)(2,1)}, u32[]{:S(2)}, u32[]{:S(2)}) async-start(bf16[16,64,512]{2,1,0:T(8,128)(2,1)} %add_convert_fusion.2), calls=%async_computation.3 | async-start | bytes 2097152 | tf_op jit(solution)/shard_map/all_to_all | solution.py:221
  191.2 18.9 %copy-start.4 = (bf16[8,2,64,512]{3,0,1,2:T(8,128)(2,1)}, bf16[8,2,64,512]{3,0,1,2:T(8,128)(2,1)S(1)}, u32[]{:S(2)}) copy-start(bf16[8,2,64,512]{3,0,1,2:T(8,128)(2,1)S(1)} %copy.566) | copy-start | bytes 3145732
  191.2 30.4 %collective-permute-start.13 = (bf16[8,1024]{1,0:T(8,128)(2,1)S(1)}, bf16[8,1024]{1,0:T(8,128)(2,1)S(1)}, u32[]{:S(2)}, u32[]{:S(2)}) collective-permute-start(bf16[8,1024]{1,0:T(8,128)(2,1)S(1)} %bitcast.287), channel_id=1, source_target_pairs={{2,0},{4,2},{6,4},{8,6},{10,8},{12,10},{14,12},{16,14},{18,16},{20... | collective-permute-start | bytes 49160 | tf_op jit(solution)/shard_map/ppermute | solution.py:290
  196.2 41.5 %collective-permute-start.15 = (bf16[1024,512]{1,0:T(8,128)(2,1)}, bf16[1024,512]{1,0:T(8,128)(2,1)S(1)}, u32[]{:S(2)}, u32[]{:S(2)}) collective-permute-start(bf16[1024,512]{1,0:T(8,128)(2,1)} %constant_dynamic-slice_fusion), channel_id=1, source_target_pairs={{0,1},{1,0},{2,3},{3,2},{4,5},{5,4},{6,7},{7,6},{8,9},{9,8},{10,11... | collective-permute-start | bytes 3145736 | tf_op jit(solution)/shard_map/ppermute | solution.py:265
  210.1 13.5 %copy-start.5 = (bf16[8,2,64,512]{3,0,1,2:T(8,128)(2,1)}, bf16[8,2,64,512]{3,0,1,2:T(8,128)(2,1)S(1)}, u32[]{:S(2)}) copy-start(bf16[8,2,64,512]{3,0,1,2:T(8,128)(2,1)S(1)} %copy.565) | copy-start | bytes 3145732
  210.1 11.5 %collective-permute-start.12 = (bf16[8,1024]{1,0:T(8,128)(2,1)S(1)}, bf16[8,1024]{1,0:T(8,128)(2,1)S(1)}, u32[]{:S(2)}, u32[]{:S(2)}) collective-permute-start(bf16[8,1024]{1,0:T(8,128)(2,1)S(1)} %bitcast.288), channel_id=1, source_target_pairs={{0,2},{2,4},{4,6},{6,8},{8,10},{10,12},{12,14},{14,16},{16,18},{18... | collective-permute-start | bytes 49160 | tf_op jit(solution)/shard_map/ppermute | solution.py:290
  213.9 6.0 %collective-permute-start.14 = (bf16[128,8]{0,1:T(8,128)(2,1)S(1)}, bf16[128,8]{0,1:T(8,128)(2,1)S(1)}, u32[]{:S(2)}, u32[]{:S(2)}) collective-permute-start(bf16[128,8]{0,1:T(8,128)(2,1)S(1)} %maximum_select_fusion), channel_id=1, source_target_pairs={{0,1},{1,0},{2,3},{3,2},{4,5},{5,4},{6,7},{7,6},{8,9},{9,8},{10,11... | collective-permute-start | bytes 6152 | tf_op jit(solution)/shard_map/ppermute | solution.py:296
  222.1 23.0 %collective-permute-start.18 = (f32[128,8]{0,1:T(8,128)S(1)}, f32[128,8]{0,1:T(8,128)S(1)}, u32[]{:S(2)}, u32[]{:S(2)}) collective-permute-start(f32[128,8]{0,1:T(8,128)S(1)} %fusion.50), channel_id=1, source_target_pairs={{0,1},{1,0},{2,3},{3,2},{4,5},{5,4},{6,7},{7,6},{8,9},{9,8},{10,11... | collective-permute-start | bytes 12296 | tf_op jit(solution)/shard_map/ppermute | solution.py:296
  237.7 8.4 %collective-permute-start.17 = (f32[8,1024]{1,0:T(8,128)S(1)}, f32[8,1024]{1,0:T(8,128)S(1)}, u32[]{:S(2)}, u32[]{:S(2)}) collective-permute-start(f32[8,1024]{1,0:T(8,128)S(1)} %get-tuple-element.59), channel_id=1, source_target_pairs={{2,0},{4,2},{6,4},{8,6},{10,8},{12,10},{14,12},{16,14},{18,16},{20... | collective-permute-start | bytes 98312 | tf_op jit(solution)/shard_map/ppermute | solution.py:290
  242.1 4.1 collective-permute-start.16
  252.5 31.8 %all-to-all-start.4 = ((bf16[16,128,256]{2,1,0:T(8,128)(2,1)}), bf16[16,128,256]{2,1,0:T(8,128)(2,1)S(1)}, u32[]{:S(2)}, u32[]{:S(2)}) async-start(bf16[16,128,256]{2,1,0:T(8,128)(2,1)} %rim_lines.2), calls=%async_computation.4 | async-start | bytes 2097152 | tf_op jit(solution)/shard_map/all_to_all | solution.py:221
  284.3 29.8 %all-to-all-start.5 = ((bf16[16,128,256]{2,1,0:T(8,128)(2,1)}), bf16[16,128,256]{2,1,0:T(8,128)(2,1)S(1)}, u32[]{:S(2)}, u32[]{:S(2)}) async-start(bf16[16,128,256]{2,1,0:T(8,128)(2,1)} %rim_lines.3), calls=%async_computation.5 | async-start | bytes 2097152 | tf_op jit(solution)/shard_map/all_to_all | solution.py:221
  289.4 3.7 copy-start.10
  297.8 44.9 %collective-permute-start.20 = (bf16[16,64,256]{2,1,0:T(8,128)(2,1)}, bf16[16,64,256]{2,1,0:T(8,128)(2,1)}, u32[]{:S(2)}, u32[]{:S(2)}) collective-permute-start(bf16[16,64,256]{2,1,0:T(8,128)(2,1)} %get-tuple-element.39), channel_id=1, source_target_pairs={{0,1},{1,0},{2,3},{3,2},{4,5},{5,4},{6,7},{7,6},{8,9},{9,8},{10,11... | collective-permute-start | bytes 1572872 | tf_op jit(solution)/shard_map/ppermute | solution.py:230
  298.0 56.2 %collective-permute-start.19 = (bf16[16,64,256]{2,1,0:T(8,128)(2,1)}, bf16[16,64,256]{2,1,0:T(8,128)(2,1)}, u32[]{:S(2)}, u32[]{:S(2)}) collective-permute-start(bf16[16,64,256]{2,1,0:T(8,128)(2,1)} %get-tuple-element.39), channel_id=1, source_target_pairs={{0,2},{2,0},{4,6},{6,4},{8,10},{10,8},{12,14},{14,12},{16,18},{18,... | collective-permute-start | bytes 1572872 | tf_op jit(solution)/shard_map/ppermute | solution.py:231
  298.7 38.6 %collective-permute-start.27 = (bf16[16,64,256]{2,1,0:T(8,128)(2,1)}, bf16[16,64,256]{2,1,0:T(8,128)(2,1)}, u32[]{:S(2)}, u32[]{:S(2)}) collective-permute-start(bf16[16,64,256]{2,1,0:T(8,128)(2,1)} %get-tuple-element.38), channel_id=1, source_target_pairs={{0,1},{1,0},{2,3},{3,2},{4,5},{5,4},{6,7},{7,6},{8,9},{9,8},{10,11... | collective-permute-start | bytes 1572872 | tf_op jit(solution)/shard_map/ppermute | solution.py:230
  299.9 38.9 %collective-permute-start.26 = (bf16[16,64,256]{2,1,0:T(8,128)(2,1)}, bf16[16,64,256]{2,1,0:T(8,128)(2,1)}, u32[]{:S(2)}, u32[]{:S(2)}) collective-permute-start(bf16[16,64,256]{2,1,0:T(8,128)(2,1)} %get-tuple-element.38), channel_id=1, source_target_pairs={{0,2},{2,0},{4,6},{6,4},{8,10},{10,8},{12,14},{14,12},{16,18},{18,... | collective-permute-start | bytes 1572872 | tf_op jit(solution)/shard_map/ppermute | solution.py:231
  322.5 13.7 %collective-permute-start.23 = (bf16[16,64,256]{2,1,0:T(8,128)(2,1)S(1)}, bf16[16,64,256]{2,1,0:T(8,128)(2,1)S(1)}, u32[]{:S(2)}, u32[]{:S(2)}) collective-permute-start(bf16[16,64,256]{2,1,0:T(8,128)(2,1)S(1)} %get-tuple-element.42), channel_id=1, source_target_pairs={{0,1},{1,0},{2,3},{3,2},{4,5},{5,4},{6,7},{7,6},{8,9},{9,8},{10,11... | collective-permute-start | bytes 1572872 | tf_op jit(solution)/shard_map/ppermute | solution.py:230
  336.2 16.5 %collective-permute-start.22 = (bf16[16,64,256]{2,1,0:T(8,128)(2,1)}, bf16[16,64,256]{2,1,0:T(8,128)(2,1)S(1)}, u32[]{:S(2)}, u32[]{:S(2)}) collective-permute-start(bf16[16,64,256]{2,1,0:T(8,128)(2,1)} %get-tuple-element.19), channel_id=1, source_target_pairs={{0,2},{2,0},{4,6},{6,4},{8,10},{10,8},{12,14},{14,12},{16,18},{18,... | collective-permute-start | bytes 1572872 | tf_op jit(solution)/shard_map/ppermute | solution.py:231
  337.3 3.8 collective-permute-start.29
  338.8 4.1 collective-permute-start.28
  341.1 3.1 collective-permute-start.30
  342.8 13.3 %collective-permute-start.24 = (bf16[16,64,256]{2,1,0:T(8,128)(2,1)}, bf16[16,64,256]{2,1,0:T(8,128)(2,1)S(1)}, u32[]{:S(2)}, u32[]{:S(2)}) collective-permute-start(bf16[16,64,256]{2,1,0:T(8,128)(2,1)} %get-tuple-element.19), channel_id=1, source_target_pairs={{0,1},{1,0},{2,3},{3,2},{4,5},{5,4},{6,7},{7,6},{8,9},{9,8},{10,11... | collective-permute-start | bytes 1572872 | tf_op jit(solution)/shard_map/ppermute | solution.py:230
  343.0 14.8 %collective-permute-start.21 = (bf16[16,64,256]{2,1,0:T(8,128)(2,1)}, bf16[16,64,256]{2,1,0:T(8,128)(2,1)}, u32[]{:S(2)}, u32[]{:S(2)}) collective-permute-start(bf16[16,64,256]{2,1,0:T(8,128)(2,1)} %collective-permute-done.20), channel_id=1, source_target_pairs={{0,2},{2,0},{4,6},{6,4},{8,10},{10,8},{12,14},{14,12},{16,18},{18,... | collective-permute-start | bytes 1572872 | tf_op jit(solution)/shard_map/ppermute | solution.py:232
  346.0 30.0 %all-to-all-start.7 = ((bf16[16,64,512]{2,1,0:T(8,128)(2,1)}), bf16[16,64,512]{2,1,0:T(8,128)(2,1)S(1)}, u32[]{:S(2)}, u32[]{:S(2)}) async-start(bf16[16,64,512]{2,1,0:T(8,128)(2,1)} %add_convert_fusion), calls=%async_computation.7 | async-start | bytes 2097152 | tf_op jit(solution)/shard_map/all_to_all | solution.py:221
  356.0 3.5 collective-permute-start.25
  376.0 5.0 %copy-start.6 = (bf16[16,64,512]{2,1,0:T(8,128)(2,1)}, bf16[16,64,512]{2,1,0:T(8,128)(2,1)S(1)}, u32[]{:S(2)}) copy-start(bf16[16,64,512]{2,1,0:T(8,128)(2,1)S(1)} %all-to-all-done.7.lines) | copy-start | bytes 3145732
  376.0 29.8 %all-to-all-start.6 = ((bf16[16,64,512]{2,1,0:T(8,128)(2,1)}), bf16[16,64,512]{2,1,0:T(8,128)(2,1)S(1)}, u32[]{:S(2)}, u32[]{:S(2)}) async-start(bf16[16,64,512]{2,1,0:T(8,128)(2,1)} %add_convert_fusion.1), calls=%async_computation.6 | async-start | bytes 2097152 | tf_op jit(solution)/shard_map/all_to_all | solution.py:221
  (5 other events, 10.8 us)
Sparse Core Ops, SparseCore 0:
  10.7 63.6 all-gather.2
  76.6 56.5 all-gather.4
